TPU v7x, 32 devices: a whole 2x2x4 slice. The times are simulated.
32 devices in a mesh: comp: 2 (over x), py: 4 (over y, core), px: 4 (over z).
Axes of the slice: x: 2, y: 2, z: 4, core: 2. Of those that a mesh axis runs over, the one named last changes fastest.
Arguments:
- current_speeds: float32 [2, 64, 128, 256], P(None, 'py', 'px'), may hold values from -1.2 to 1.2
- thermal_anomaly: float32 [64, 128, 256], P('py', 'px'), may hold values from -6 to 6
- solute_amounts: float32 [16, 16, 512, 256], P(None, ('py', 'px')), may hold values from -6 to 6
- delayed_link_source: float32 [2, 2, 16, 512, 256], P('comp', None, ('py', 'px')), may hold values from -6 to 6
- marine_indicator: int32 [64, 128], replicated, may hold values 0 or 1
- floor_layer_index: int32 [64, 128], replicated, may hold values from 1 to 256
- holder_rank: int32 [16, 16], replicated, may hold values from 0 to 15, each once within a row
- biota_exchange_matrix: float32 [16, 16], replicated, may hold values from -1.5 to 1.5
- photic_absorb_share: float32 [16], replicated, may hold values from -4 to 4
- chroma_loading: float32 [16], replicated, may hold values from -3 to 3
Outputs:
- coupling_out: float32 [2, 2, 16, 512, 256], P('comp', None, ('py', 'px'))
Inputs may be any that keep to these rules, and one draw needn't show every extreme that they name: `holder_rank`: each row of owner names every tracer owner once.
All inputs are finite; a program needn't handle non-finite values.
Results may differ from a plain program's by a relative error of at most 0.0001.
Values sent between devices are 32-bit elements; how exact they have to be, the bound alone decides.
No kernel may reach another device: no remote copies, remote signals or barrier semaphores. Data moves between devices by JAX's collectives and lax.ppermute only.
A program may use at most 128 MiB of HBM per device.

v0:
```python
import functools

import jax
import jax.numpy as jnp
from jax import lax
from jax.experimental import pallas as pl
from jax.experimental.pallas import tpu as pltpu
from jax.sharding import PartitionSpec as P

advance_marine = 0.1
spreading = 0.1
viscosity = 0.1
damping = 0.05
heat_gain = 0.2
weight_pull_factor = 0.05
coriolis_scale = 1.0
step_tracer = 0.1
heating_speed = 0.06
uptake_rate = 0.01
water_absorb = (0.02, 0.003)
pigment_absorb = (0.03, 0.004)
surface_light = (40.0, 60.0)
CY = 16
CX = 32
KEPT = (0, 1, 2, 4, 5)
VMEM = pl.BlockSpec(memory_space=pltpu.VMEM)
SMEM = pl.BlockSpec(memory_space=pltpu.SMEM)
PARAMS = pltpu.CompilerParams(vmem_limit_bytes=40 * 1024 * 1024)


def shape_of(*dims):
    return jax.ShapeDtypeStruct(dims, jnp.float32)


def level_matrix(levels, pattern):
    row = lax.broadcasted_iota(jnp.int32, (levels, levels), 0)
    col = lax.broadcasted_iota(jnp.int32, (levels, levels), 1)
    if pattern == "above":
        m = jnp.where(row < col, 1.0, jnp.where(row == col, 0.5, 0.0))
    elif pattern == "below":
        m = jnp.where(row >= col, 1.0, 0.0)
    else:
        m = jnp.where(row < col, 1.0, 0.0)
    return m.astype(jnp.bfloat16)


def level_sums(x, matrix):
    hi = x.astype(jnp.bfloat16)
    rest = x - hi.astype(jnp.float32)
    mid = rest.astype(jnp.bfloat16)
    low = (rest - mid.astype(jnp.float32)).astype(jnp.bfloat16)
    dot = functools.partial(jnp.dot, preferred_element_type=jnp.float32)
    return dot(hi, matrix) + dot(mid, matrix) + dot(low, matrix)


def softplus(x):
    return jnp.maximum(x, 0.0) + jnp.log1p(jnp.exp(-jnp.abs(x)))


def light(chl, sums, level):
    absorbed, irradiance = [], None
    for water, pigment, surface in zip(water_absorb, pigment_absorb, surface_light):
        fade = jnp.exp(-0.5 * (water + pigment * chl))
        intensity = surface * jnp.exp(-(water * level + pigment * sums))
        absorbed.append(intensity * (1.0 - fade * fade))
        part = intensity * fade
        irradiance = part if irradiance is None else irradiance + part
    return absorbed, irradiance


def saturation(n):
    return n * n / (1.0 + n * n)


def transport(rise_half, y):
    top = rise_half * (y + pltpu.roll(y, 1, 1))
    return pltpu.roll(top, top.shape[1] - 1, 1) - top


def wet_of(depth, shape):
    level = lax.broadcasted_iota(jnp.int32, shape, len(shape) - 1)
    return jnp.where(level < depth, 1.0, 0.0)


def level_of(shape):
    return lax.broadcasted_iota(jnp.int32, shape, len(shape) - 1).astype(jnp.float32)


def half_rise(rise):
    k = lax.broadcasted_iota(jnp.int32, rise.shape, 1)
    return jnp.where(k > 0, 0.5 * rise, 0.0)


def project_kernel(sc, x_ref, w_ref, depth_ref, y_ref, g_ref, chl_ref):
    fields, patches, cols, levels = x_ref.shape

    def one(q, carry):
        values = [x_ref[j, q] for j in range(fields)]
        for k in range(y_ref.shape[0]):
            total = w_ref[k, 0] * values[0]
            for j in range(1, fields):
                total = total + w_ref[k, j] * values[j]
            y_ref[k, q] = total
            if k == 0:
                chl_ref[q] = softplus(total)
        return carry

    lax.fori_loop(0, patches, one, 0)
    flat = (patches * cols, levels)
    chl = chl_ref[...].reshape(flat)
    sums = level_sums(chl, level_matrix(levels, "prefix"))
    _, irradiance = light(chl, sums, level_of(flat))
    n = x_ref[0].reshape(flat)
    g_ref[...] = (uptake_rate * irradiance * saturation(n)).reshape(patches, cols, levels)


def project(comp, tracers, weights, depth):
    fields, patches, strip, levels = tracers.shape
    half = strip // 2
    block = 4
    kinds = weights.shape[0]
    return pl.pallas_call(
        project_kernel,
        grid_spec=pltpu.PrefetchScalarGridSpec(
            num_scalar_prefetch=1,
            grid=(patches // block,),
            in_specs=[
                pl.BlockSpec((fields, block, half, levels), lambda i, c: (0, i, c[0], 0)),
                SMEM,
                pl.BlockSpec((block, half, 1), lambda i, c: (i, 0, 0)),
            ],
            out_specs=[
                pl.BlockSpec((kinds, block, half, levels), lambda i, c: (0, i, 0, 0)),
                pl.BlockSpec((block, half, levels), lambda i, c: (i, 0, 0)),
            ],
            scratch_shapes=[pltpu.VMEM((block, half, levels), jnp.float32)],
        ),
        out_shape=(shape_of(kinds, patches, half, levels), shape_of(patches, half, levels)),
        compiler_params=PARAMS,
        name="project",
    )(comp, tracers, weights, depth)


def first_tracer_kernel(sc, y_ref, g_ref, got_ref, own_ref, depth_ref, share_ref, out_ref):
    patches, cols, levels = g_ref.shape
    first = sc[0] == 0

    def one(q, carry):
        rise = jnp.where(first, got_ref[0, q], own_ref[0, q])
        heat = jnp.where(first, got_ref[1, q], own_ref[1, q])
        warm = jnp.exp(heating_speed * heat)
        wet = wet_of(depth_ref[q], (cols, levels))
        up = half_rise(rise)
        g = g_ref[q]
        for place, k in enumerate(KEPT):
            y = y_ref[k, q]
            change = warm * y_ref[k + 1, q] + share_ref[k] * g + transport(up, y)
            out_ref[q, place] = wet * (y + step_tracer * change)
        return carry

    lax.fori_loop(0, patches, one, 0)


def half_spec(lead, cols, levels):
    zeros = (0,) * len(lead)
    return pl.BlockSpec(lead + (cols, levels), lambda i, c: zeros + (c[0], 0))


def first_tracer(comp, projected, g, got, linked, depth, shares):
    _, patches, half, levels = projected.shape
    return pl.pallas_call(
        first_tracer_kernel,
        grid_spec=pltpu.PrefetchScalarGridSpec(
            num_scalar_prefetch=1,
            grid=(1,),
            in_specs=[VMEM, VMEM, VMEM, half_spec((2, patches), half, levels), VMEM, SMEM],
            out_specs=VMEM,
        ),
        out_shape=shape_of(patches, len(KEPT), half, levels),
        compiler_params=PARAMS,
        name="first_tracer",
    )(comp, projected, g, got, linked, depth, shares)


def ocean_kernel(
    advance, sc, coriolis_ref, u_ref, v_ref, t_ref, north_ref, south_ref, east_ref, west_ref, depth_ref,
    *rest,
):
    rest = list(rest)
    if advance == 1:
        linked_ref, got_ref = rest[:2]
        rest = rest[2:]
    if advance < 3:
        un_ref, vn_ref, tn_ref, rise_ref, row0_ref, row1_ref, col0_ref, col1_ref = rest[:8]
        p_ref, pn_ref, ps_ref, pe_ref, pw_ref, div_ref = rest[8:]
    else:
        face_ref, rise_ref, div_ref = rest
    rows, cols, levels = u_ref.shape
    if advance < 3:
        above = level_matrix(levels, "above")
        p_ref[...] = (
            weight_pull_factor * level_sums(t_ref[...].reshape(rows * cols, levels), above)
        ).reshape(rows, cols, levels)
        for target, source in ((pn_ref, north_ref), (ps_ref, south_ref), (pe_ref, east_ref), (pw_ref, west_ref)):
            target[...] = weight_pull_factor * level_sums(source[2], above)
    place = lax.broadcasted_iota(jnp.int32, (cols, levels), 0)

    def row(y, at):
        shape = (cols, levels)
        north_in = at < rows - 1
        south_in = at > 0

        def around(ref, f):
            x = ref[y]
            e = east_ref[f, pl.ds(y, 1)]
            w = west_ref[f, pl.ds(y, 1)]
            return (
                x,
                jnp.where(place == cols - 1, e, pltpu.roll(x, cols - 1, 0)),
                jnp.where(place == 0, w, pltpu.roll(x, 1, 0)),
                ref[y + 1] if north_in else north_ref[f],
                ref[y - 1] if south_in else south_ref[f],
            )

        wet = [wet_of(depth_ref[i, y], shape) for i in range(5)]
        u = around(u_ref, 0)
        v = around(v_ref, 1)
        east = 0.5 * (u[0] + u[1]) * wet[0] * wet[1]
        west = 0.5 * (u[2] + u[0]) * wet[2] * wet[0]
        north = 0.5 * (v[0] + v[3]) * wet[0] * wet[3]
        south = 0.5 * (v[4] + v[0]) * wet[4] * wet[0]
        div_ref[y] = east - west + north - south
        if advance == 3:
            for i, face in enumerate((east, west, north, south)):
                face_ref[i, y] = face
            return
        t = around(t_ref, 2)
        pe = pe_ref[pl.ds(y, 1)]
        pw = pw_ref[pl.ds(y, 1)]
        p0 = p_ref[y]
        p = (
            p0,
            jnp.where(place == cols - 1, pe, pltpu.roll(p0, cols - 1, 0)),
            jnp.where(place == 0, pw, pltpu.roll(p0, 1, 0)),
            p_ref[y + 1] if north_in else pn_ref[...],
            p_ref[y - 1] if south_in else ps_ref[...],
        )

        def spread(x):
            return (
                wet[1] * (x[1] - x[0]) + wet[2] * (x[2] - x[0])
                + wet[3] * (x[3] - x[0]) + wet[4] * (x[4] - x[0])
            )

        carry_along = 0.5 * (
            east * (t[0] + t[1]) - west * (t[2] + t[0]) + north * (t[0] + t[3]) - south * (t[4] + t[0])
        )
        change = spreading * spread(t) - carry_along
        if advance == 1:
            absorb = jnp.where(
                sc[0] == 0, linked_ref[0, y] + linked_ref[1, y],
                jnp.concatenate([got_ref[0, y], got_ref[1, y]], axis=0),
            )
            change = change + heat_gain * absorb
        zonal = 0.5 * (wet[1] * (p[1] - p[0]) + wet[2] * (p[0] - p[2]))
        merid = 0.5 * (wet[3] * (p[3] - p[0]) + wet[4] * (p[0] - p[4]))
        turn = coriolis_ref[y]
        results = (
            wet[0] * (u[0] + advance_marine * (turn * v[0] - zonal + viscosity * spread(u) - damping * u[0])),
            wet[0] * (v[0] + advance_marine * (-turn * u[0] - merid + viscosity * spread(v) - damping * v[0])),
            wet[0] * (t[0] + advance_marine * change),
        )
        for f, (ref, value) in enumerate(zip((un_ref, vn_ref, tn_ref), results)):
            ref[y] = value
            col0_ref[f, pl.ds(y, 1)] = value[:1]
            col1_ref[f, pl.ds(y, 1)] = value[cols - 1 :]
            if not south_in:
                row0_ref[f] = value
            if not north_in:
                row1_ref[f] = value

    row(0, 0)

    def inner(y, carry):
        row(y, 1)
        return carry

    lax.fori_loop(1, rows - 1, inner, 0)
    row(rows - 1, rows - 1)
    sums = level_sums(div_ref[...].reshape(rows * cols, levels), level_matrix(levels, "below"))
    rise_ref[...] = -sums.reshape(rows, cols, levels)


def ocean(advance, comp, coriolis, fields, halos, depth, linked=None, got=None):
    rows, cols, levels = fields[0].shape
    grid = shape_of(rows, cols, levels)
    count = len(halos[0])
    if advance < 3:
        outs = (
            grid, grid, grid, grid,
            shape_of(3, cols, levels), shape_of(3, cols, levels), shape_of(3, rows, levels), shape_of(3, rows, levels),
        )
        scratch = [
            (rows, cols, levels), (cols, levels), (cols, levels), (rows, levels), (rows, levels), (rows, cols, levels),
        ]
    else:
        outs = (shape_of(4, rows, cols, levels), grid)
        scratch = [(rows, cols, levels)]
    args = [coriolis, *fields, *halos, depth] + ([linked, got] if advance == 1 else [])
    return pl.pallas_call(
        functools.partial(ocean_kernel, advance),
        grid_spec=pltpu.PrefetchScalarGridSpec(
            num_scalar_prefetch=1,
            grid=(1,),
            in_specs=[SMEM] + [VMEM] * (len(args) - 1),
            out_specs=[VMEM] * len(outs),
            scratch_shapes=[pltpu.VMEM(s, jnp.float32) for s in scratch],
        ),
        out_shape=outs,
        compiler_params=PARAMS,
        name=f"ocean{advance}",
    )(comp, *args)


def absorb_kernel(sc, y_ref, t_ref, t2_ref, irr_ref, row0_ref, row1_ref, col0_ref, col1_ref, depth_ref, chl_ref):
    patches, _, cols, levels = y_ref.shape
    flat = (patches * cols, levels)

    def gather(s, carry):
        chl_ref[s] = softplus(y_ref[sc[1 + s], 0])
        return carry

    lax.fori_loop(0, patches, gather, 0)
    chl = chl_ref[...].reshape(flat)
    sums = level_sums(chl, level_matrix(levels, "prefix"))
    absorbed, irradiance = light(chl, sums, level_of(flat))
    wet = wet_of(depth_ref[0], (patches, cols, levels))
    both = (absorbed[0] + absorbed[1]).reshape(patches, cols, levels)
    t2 = t_ref[...] + advance_marine * heat_gain * (wet * both)
    t2_ref[...] = t2
    irr_ref[...] = irradiance.reshape(patches, cols, levels)
    row0_ref[...] = t2_ref[0]
    row1_ref[...] = t2_ref[patches - 1]
    for s in range(patches):
        col0_ref[pl.ds(s, 1)] = t2_ref[s, :1]
        col1_ref[pl.ds(s, 1)] = t2_ref[s, cols - 1 :]


def two_steps_kernel(
    sc, y_ref, t2_ref, irr_ref, t1_ref, r1_ref, r2_ref, depth_ref, share_ref,
    heat_ref, absorbed_ref, a_ref, b_ref, n_ref, chl_ref,
):
    patches, _, cols, levels = y_ref.shape
    flat = (patches * cols, levels)
    whole = (patches, cols, levels)
    prefix = level_matrix(levels, "prefix")

    def second(s, carry):
        owner = sc[1 + s]
        wet = wet_of(depth_ref[0, s], (cols, levels))
        warm = jnp.exp(heating_speed * t1_ref[s])
        up = half_rise(r1_ref[s])
        y = [y_ref[owner, i] for i in range(len(KEPT))]
        g = uptake_rate * irr_ref[s] * saturation(y[3])
        for ref, i, k in ((a_ref, 0, 0), (b_ref, 1, 1), (n_ref, 3, 4)):
            change = warm * y[i + 1] + share_ref[k] * g + transport(up, y[i])
            ref[s] = wet * (y[i] + step_tracer * change)
        chl_ref[s] = softplus(a_ref[s])
        return carry

    lax.fori_loop(0, patches, second, 0)
    chl = chl_ref[...].reshape(flat)
    absorbed, irradiance = light(chl, level_sums(chl, prefix), level_of(flat))
    wet = wet_of(depth_ref[0], whole)
    heat_ref[...] = advance_marine * heat_gain * (wet * (absorbed[0] + absorbed[1]).reshape(whole))
    n_ref[...] = uptake_rate * irradiance.reshape(whole) * saturation(n_ref[...])

    def third(s, carry):
        wet = wet_of(depth_ref[0, s], (cols, levels))
        warm = jnp.exp(heating_speed * t2_ref[s])
        up = half_rise(r2_ref[s])
        a = a_ref[s]
        change = warm * b_ref[s] + share_ref[0] * n_ref[s] + transport(up, a)
        chl_ref[s] = softplus(wet * (a + step_tracer * change))
        return carry

    lax.fori_loop(0, patches, third, 0)
    chl = chl_ref[...].reshape(flat)
    absorbed, _ = light(chl, level_sums(chl, prefix), level_of(flat))
    for band in range(2):
        absorbed_ref[:, band] = wet * absorbed[band].reshape(whole)


def last_heat_kernel(sc, t_ref, north_ref, south_ref, east_ref, west_ref, face_ref, depth_ref, heat_ref, rise_ref, out_ref):
    rows, cols, levels = t_ref.shape
    place = lax.broadcasted_iota(jnp.int32, (cols, levels), 0)
    for y in range(rows):
        wet = [wet_of(depth_ref[i, y], (cols, levels)) for i in range(5)]
        t = t_ref[y]
        e = jnp.where(place == cols - 1, east_ref[pl.ds(y, 1)], pltpu.roll(t, cols - 1, 0))
        w = jnp.where(place == 0, west_ref[pl.ds(y, 1)], pltpu.roll(t, 1, 0))
        n = t_ref[y + 1] if y < rows - 1 else north_ref[...]
        s = t_ref[y - 1] if y > 0 else south_ref[...]
        spread = wet[1] * (e - t) + wet[2] * (w - t) + wet[3] * (n - t) + wet[4] * (s - t)
        carry_along = 0.5 * (
            face_ref[0, y] * (t + e) - face_ref[1, y] * (w + t) + face_ref[2, y] * (t + n) - face_ref[3, y] * (s + t)
        )
        owner = sc[1 + y]
        out_ref[owner, 0] = rise_ref[y]
        out_ref[owner, 1] = wet[0] * (t + advance_marine * (spreading * spread - carry_along)) + heat_ref[y]


def join_kernel(sc, absorbed_ref, flux_ref, other_ref, out_ref):
    patches, _, half, levels = absorbed_ref.shape
    first = sc[0] == 0
    own = pl.multiple_of(sc[0] * half, half)
    rest = pl.multiple_of((1 - sc[0]) * half, half)
    for s in range(patches):
        for f in range(2):
            mine = jnp.where(first, absorbed_ref[s, f], flux_ref[s, f])
            out_ref[f, s, pl.ds(own, half)] = mine
            out_ref[f, s, pl.ds(rest, half)] = other_ref[s, f]


def call(kernel, comp, args, specs, outs, scratch=(), name=None):
    return pl.pallas_call(
        kernel,
        grid_spec=pltpu.PrefetchScalarGridSpec(
            num_scalar_prefetch=1,
            grid=(1,),
            in_specs=specs,
            out_specs=[VMEM] * len(outs),
            scratch_shapes=[pltpu.VMEM(s, jnp.float32) for s in scratch],
        ),
        out_shape=outs,
        compiler_params=PARAMS,
        name=name,
    )(comp, *args)


def exchange_rows(low, high):
    count = lax.axis_size("py")
    north = lax.ppermute(low, "py", [(i + 1, i) for i in range(count - 1)])
    south = lax.ppermute(high, "py", [(i, i + 1) for i in range(count - 1)])
    return north, south


def exchange_cols(low, high):
    count = lax.axis_size("px")
    east = lax.ppermute(low, "px", [((i + 1) % count, i) for i in range(count)])
    west = lax.ppermute(high, "px", [(i, (i + 1) % count) for i in range(count)])
    return east, west


def exchange_half_cols(low, high):
    count = lax.axis_size("px")
    line = [(h % 2) * count + h // 2 for h in range(2 * count)]
    ahead = [(line[h], line[(h + 1) % len(line)]) for h in range(len(line))]
    east = lax.ppermute(low, ("comp", "px"), [(b, a) for a, b in ahead])
    west = lax.ppermute(high, ("comp", "px"), ahead)
    return east, west


def swap(block):
    return lax.ppermute(block, "comp", [(0, 1), (1, 0)])


def pick(blocks, order, axis):
    return jnp.stack(
        [lax.dynamic_index_in_dim(blocks, order[k], axis, keepdims=False) for k in range(order.shape[0])], axis
    )


def table(levels, pattern):
    return level_matrix(levels, pattern).astype(jnp.float32)


def product(values, matrix):
    return jnp.einsum("...j,jk->...k", values, matrix, precision=lax.Precision.HIGHEST)


def general_light(conc, wet, loading):
    chl = jax.nn.softplus(jnp.einsum("f...,f->...", conc, loading, precision=lax.Precision.HIGHEST))
    levels = chl.shape[-1]
    absorbed, irradiance = light(chl, product(chl, table(levels, "prefix")), level_of(chl.shape))
    return wet * jnp.stack(absorbed), irradiance


def general_tracers(conc, rise, heat, irradiance, wet, matrix, share):
    none = jnp.zeros_like(conc[..., :1])
    top = jnp.concatenate([none, 0.5 * (conc[..., 1:] + conc[..., :-1]) * rise[..., 1:]], axis=-1)
    below = jnp.concatenate([top[..., 1:], none], axis=-1)
    mixed = jnp.einsum("ij,j...->i...", matrix, conc, precision=lax.Precision.HIGHEST)
    growth = uptake_rate * irradiance * saturation(conc[0])
    change = (
        jnp.exp(heating_speed * heat) * mixed
        + share.reshape((-1,) + (1,) * (conc.ndim - 1)) * growth + below - top
    )
    return wet * (conc + step_tracer * change)


def general_ocean(u, v, t, absorb, depth, coriolis):
    levels = t.shape[-1]
    fields = jnp.stack([u, v, t])
    north, south = exchange_rows(fields[:, 0], fields[:, -1])
    east, west = exchange_cols(fields[:, :, 0], fields[:, :, -1])
    tall = jnp.concatenate([south[:, None], fields, north[:, None]], axis=1)
    wide = jnp.concatenate([west[:, :, None], fields, east[:, :, None]], axis=2)
    around = (fields, wide[:, :, 2:], wide[:, :, :-2], tall[:, 2:], tall[:, :-2])
    above = table(levels, "above")
    u, v, t = ([x[f] for x in around] for f in range(3))
    p = [weight_pull_factor * product(x, above) for x in t]
    wet = [wet_of(depth[i], t[0].shape) for i in range(5)]

    def spread(x):
        return sum(wet[i] * (x[i] - x[0]) for i in range(1, 5))

    east = 0.5 * (u[0] + u[1]) * wet[0] * wet[1]
    west = 0.5 * (u[2] + u[0]) * wet[2] * wet[0]
    north = 0.5 * (v[0] + v[3]) * wet[0] * wet[3]
    south = 0.5 * (v[4] + v[0]) * wet[4] * wet[0]
    carry_along = 0.5 * (
        east * (t[0] + t[1]) - west * (t[2] + t[0]) + north * (t[0] + t[3]) - south * (t[4] + t[0])
    )
    zonal = 0.5 * (wet[1] * (p[1] - p[0]) + wet[2] * (p[0] - p[2]))
    merid = 0.5 * (wet[3] * (p[3] - p[0]) + wet[4] * (p[0] - p[4]))
    turn = coriolis[:, None, None]
    rise = -product(east - west + north - south, table(levels, "below"))
    return (
        wet[0] * (u[0] + advance_marine * (turn * v[0] - zonal + viscosity * spread(u) - damping * u[0])),
        wet[0] * (v[0] + advance_marine * (-turn * u[0] - merid + viscosity * spread(v) - damping * v[0])),
        wet[0] * (t[0] + advance_marine * (spreading * spread(t) - carry_along + heat_gain * (absorb[0] + absorb[1]))),
        rise,
    )


def general(linked, u, v, t, tracers, depth, tracer_depth, holder_rank, patch_index, coriolis, matrix, share, loading):
    comp_index = lax.axis_index("comp")
    first = comp_index == 0
    fields, patches, strip, levels = tracers.shape
    half = strip // 2
    indices = jnp.arange(patches, dtype=jnp.int32)
    owner_row = lax.dynamic_index_in_dim(holder_rank, patch_index, 0, keepdims=False)
    inverse_row = jnp.sum(jnp.where(owner_row[:, None] == indices[None], indices[:, None], 0), axis=0)

    def own_half(x):
        return lax.dynamic_slice_in_dim(x, comp_index * half, half, x.ndim - 2)

    partner = swap(linked)
    absorb = jnp.where(first, linked, partner)
    flux = own_half(jnp.where(first, partner, linked))
    conc = own_half(tracers)
    wet = wet_of(tracer_depth, conc.shape[1:])
    irradiance = general_light(conc, wet, loading)[1]
    grid = t.shape
    for _ in range(3):
        u, v, t, rise = general_ocean(u, v, t, absorb.reshape((2,) + grid), depth, coriolis)
        conc = general_tracers(conc, flux[0], flux[1], irradiance, wet, matrix, share)
        absorbed, irradiance = general_light(conc, wet, loading)
        both = own_half(pick(jnp.stack([rise, t]).reshape(2, patches, strip, levels), inverse_row, 1))
        send = jnp.concatenate([both, absorbed])
        back = lax.all_to_all(send, ("py", "px"), split_axis=1, concat_axis=1, tiled=True)
        flux = back[:2]
        mine = pick(back[2:], owner_row, 1)
        other = swap(mine)
        absorb = jnp.where(first, jnp.concatenate([mine, other], 2), jnp.concatenate([other, mine], 2))
    other = swap(flux)
    joined = jnp.where(first, jnp.concatenate([flux, other], 2), jnp.concatenate([other, flux], 2))
    return jnp.where(first, absorb, joined)


def shards(
    current_speeds,
    thermal_anomaly,
    solute_amounts,
    delayed_link_source,
    marine_indicator,
    floor_layer_index,
    holder_rank,
    biota_exchange_matrix,
    photic_absorb_share,
    chroma_loading,
):
    comp_index = lax.axis_index("comp")
    row_index = lax.axis_index("py")
    col_index = lax.axis_index("px")
    rows_mesh = lax.axis_size("py")
    cols_mesh = lax.axis_size("px")
    patches = rows_mesh * cols_mesh
    fields, _, columns, levels = solute_amounts.shape
    strip = columns // patches
    half = strip // 2
    patch_index = row_index * cols_mesh + col_index
    first = comp_index == 0

    linked = delayed_link_source.reshape(2, patches, strip, levels)
    tracers = solute_amounts.reshape(fields, patches, strip, levels)
    u0, v0 = current_speeds[0], current_speeds[1]

    column_depth = marine_indicator * floor_layer_index
    wrapped = jnp.concatenate([column_depth[:, -1:], column_depth, column_depth[:, :1]], axis=1)
    padded = jnp.pad(wrapped, ((1, 1), (0, 0)))
    local = lax.dynamic_slice(padded, (row_index * CY, col_index * CX), (CY + 2, CX + 2))
    depth = jnp.stack([local[1:-1, 1:-1], local[1:-1, 2:], local[1:-1, :-2], local[2:, 1:-1], local[:-2, 1:-1]])
    depth = depth[..., None]
    by_strip = (
        column_depth.reshape(rows_mesh, CY, cols_mesh, CX).transpose(0, 2, 1, 3).reshape(patches, patches, strip)
    )
    here = (holder_rank == patch_index)[:, :, None]
    tracer_depth = jnp.sum(jnp.where(here, by_strip, 0), axis=1)
    tracer_depth = lax.dynamic_slice_in_dim(tracer_depth, comp_index * half, half, 1)[..., None]
    owner_row = lax.dynamic_index_in_dim(holder_rank, patch_index, 0, keepdims=False)
    comp = jnp.concatenate([comp_index.astype(jnp.int32)[None], owner_row])
    ys = (row_index * CY + jnp.arange(CY, dtype=jnp.int32)).astype(jnp.float32)
    coriolis = coriolis_scale * (2.0 * (ys + 0.5) / (CY * rows_mesh) - 1.0)

    if half % 8:
        out = general(
            linked, u0, v0, thermal_anomaly, tracers, depth, tracer_depth, holder_rank, patch_index, coriolis,
            biota_exchange_matrix, photic_absorb_share, chroma_loading,
        )
        return out.reshape(1, 2, 1, columns, levels)

    absorb = linked[0] + linked[1]
    sent = jnp.where(
        first, jnp.stack([absorb[:, :half], absorb[:, half:]]), linked[:, :, :half]
    )
    got = swap(sent)
    start = jnp.stack([u0, v0, thermal_anomaly])
    halos0 = exchange_rows(start[:, 0], start[:, -1]) + exchange_cols(start[:, :, 0], start[:, :, -1])

    times = functools.partial(jnp.dot, precision=lax.Precision.HIGHEST)
    unit = (jnp.arange(fields) == 0).astype(jnp.float32)
    chain = [jnp.stack([chroma_loading, unit])]
    for _ in range(3):
        chain.append(times(chain[-1], biota_exchange_matrix))
    weights = jnp.stack([c[0] for c in chain] + [c[1] for c in chain[:3]])
    shares = times(weights, photic_absorb_share)

    projected, g = project(comp, tracers, weights, tracer_depth)
    kept = first_tracer(comp, projected, g, got, linked, tracer_depth, shares)
    arrived = lax.all_to_all(kept, ("py", "px"), split_axis=0, concat_axis=0, tiled=True)

    u1, v1, t1, r1, *edges = ocean(1, comp, coriolis, (u0, v0, thermal_anomaly), halos0, depth, linked, got)
    halos1 = exchange_rows(edges[0], edges[1]) + exchange_cols(edges[2], edges[3])
    u2, v2, t2, r2, *edges = ocean(2, comp, coriolis, (u1, v1, t1), halos1, depth)
    halos2 = exchange_rows(edges[0], edges[1]) + exchange_cols(edges[2], edges[3])
    faces, r3 = ocean(3, comp, coriolis, (u2, v2, t2), halos2, depth)

    patch_half = half_spec((CY,), half, levels)
    depth_half = pl.BlockSpec((5, CY, half, 1), lambda i, c: (0, 0, c[0], 0))
    piece = shape_of(CY, half, levels)
    line = shape_of(half, levels)
    side = shape_of(CY, levels)

    def absorb_step(sc, y_ref, t_ref, depth_ref, *rest):
        absorb_kernel(sc, y_ref, t_ref, *rest[:6], depth_ref, rest[6])

    t2, irr1, *edges = call(
        absorb_step, comp, (arrived, t2, depth), [VMEM, patch_half, depth_half],
        (piece, piece, line, line, side, side), [(CY, half, levels)], "absorb",
    )
    halo = exchange_rows(edges[0], edges[1]) + exchange_half_cols(edges[2], edges[3])
    heat, absorbed = call(
        two_steps_kernel, comp, (arrived, t2, irr1, t1, r1, r2, depth, shares),
        [VMEM, VMEM, VMEM, patch_half, patch_half, patch_half, depth_half, SMEM],
        (piece, shape_of(CY, 2, half, levels)), [(CY, half, levels)] * 4, "two_steps",
    )
    [back] = call(
        last_heat_kernel, comp, (t2, *halo, faces, depth, heat, r3),
        [VMEM] * 5 + [half_spec((4, CY), half, levels), depth_half, VMEM, patch_half],
        (shape_of(patches, 2, half, levels),), (), "last_heat",
    )
    flux = lax.all_to_all(back, ("py", "px"), split_axis=0, concat_axis=0, tiled=True)
    other = swap(jnp.where(first, flux, absorbed))
    [out] = call(
        join_kernel, comp, (absorbed, flux, other), [VMEM] * 3, (shape_of(2, patches, strip, levels),), (), "join"
    )
    return out.reshape(1, 2, 1, columns, levels)


def solution(mesh):
    placed = (
        P(None, "py", "px", None),
        P("py", "px", None),
        P(None, ("py", "px"), None, None),
        P("comp", None, ("py", "px"), None, None),
        P(),
        P(),
        P(),
        P(),
        P(),
        P(),
    )
    return jax.shard_map(
        shards,
        mesh=mesh,
        in_specs=placed,
        out_specs=P("comp", None, ("py", "px"), None, None),
        check_vma=False,
    )
```

profile of v0, /device:TPU:1, one launch (start us, length us, event | category | flops | bytes accessed | tf_op | source)
XLA Modules:
  0.0 157.9 jit_solution(16708651432449910636)
XLA Ops:
  0.0 1.4 slice_add_fusion
  1.6 2.1 %collective-permute-start = (f32[2,16,16,256]{3,2,1,0:T(8,128)S(1)}, f32[2,16,16,256]{3,2,1,0:T(8,128)S(1)}, u32[]{:S(2)}, u32[]{:S(2)}) collective-permute-start(f32[2,16,16,256]{3,2,1,0:T(8,128)S(1)} %slice_select_fusion), channel_id=1, source_target_pairs={{0,16},{16,0},{1,17},{17,1},{2,18},{18,2},{3,19},{19,3},{4,20},{20... | collective-permute-start | bytes 1572872 | tf_op jit(solution)/shard_map/ppermute | solution.py:465
  5.0 3.4 %copy-done.2 = f32[16,1,512,256]{3,2,1,0:T(8,128)S(1)} copy-done((f32[16,1,512,256]{3,2,1,0:T(8,128)S(1)}, f32[16,1,512,256]{3,2,1,0:T(8,128)}, u32[]{:S(2)}) %copy-start.2) | copy-done | bytes 8388632
  8.4 4.9 %project.1 = (f32[7,16,16,256]{3,2,1,0:T(8,128)S(1)}, f32[16,16,256]{2,1,0:T(8,128)S(1)}) custom-call(s32[17]{0:T(128)S(1)} %pad_add_fusion.1.sc, f32[16,16,32,256]{3,2,1,0:T(8,128)S(1)} %bitcast.73, f32[7,16]{1,0:T(8,128)S(1)} %stack.46.w_ref, s32[16,16,1]{2,1,0:T(8,128)S(1)} %copy.18.depth_ref), custom_call_target="tpu_custom_call" | custom-call | tf_op jit(solution)/shard_map/project/pallas_call | solution.py:122
  13.5 1.9 %collective-permute-done.got_ref.rest_1_ = f32[2,16,16,256]{3,2,1,0:T(8,128)S(1)} collective-permute-done((f32[2,16,16,256]{3,2,1,0:T(8,128)S(1)}, f32[2,16,16,256]{3,2,1,0:T(8,128)S(1)}, u32[]{:S(2)}, u32[]{:S(2)}) %collective-permute-start) | collective-permute-done | bytes 524320 | tf_op jit(solution)/shard_map/ppermute | solution.py:465
  15.4 4.9 %first_tracer.1 = f32[16,5,16,256]{3,2,1,0:T(8,128)} custom-call(s32[17]{0:T(128)S(1)} %pad_add_fusion.1.sc, f32[7,16,16,256]{3,2,1,0:T(8,128)S(1)} %get-tuple-element.33.y_ref, f32[16,16,256]{2,1,0:T(8,128)S(1)} %get-tuple-element.34.g_ref, f32[2,16,16,256]{3,2,1,0:T(8,128)S(1)} %collective-permute-done.got_ref.rest_1_, f32[2,16,32,256]{3,2,1,0:T(8,128)S(1)} %bitcast.71, ...), custom_call_target="tpu_custom_call" | custom-call | tf_op jit(solution)/shard_map/first_tracer/pallas_call | solution.py:171
  20.3 7.5 %all-to-all-start = ((f32[16,5,16,256]{3,2,1,0:T(8,128)}), f32[16,5,16,256]{3,2,1,0:T(8,128)}, u32[]{:S(2)}, u32[]{:S(2)}) async-start(f32[16,5,16,256]{3,2,1,0:T(8,128)} %first_tracer.1), calls=%async_computation | async-start | bytes 2621440 | tf_op jit(solution)/shard_map/all_to_all | solution.py:642
  28.0 1.8 %copy.21 = f32[2,16,32,256]{3,1,0,2:T(8,128)S(1)} copy(f32[2,16,32,256]{3,2,1,0:T(8,128)} %param.10) | data formatting | bytes 2097152 | tf_op args[0]
  30.0 2.2 %collective-permute-start.1 = (f32[3,32,256]{2,1,0:T(8,128)S(1)}, f32[3,32,256]{2,1,0:T(8,128)S(1)}, u32[]{:S(2)}, u32[]{:S(2)}) collective-permute-start(f32[3,32,256]{2,1,0:T(8,128)S(1)} %bitcast.77), channel_id=1, source_target_pairs={{4,0},{8,4},{12,8},{5,1},{9,5},{13,9},{6,2},{10,6},{14,10},{7,3},{... | collective-permute-start | bytes 294920 | tf_op jit(solution)/shard_map/ppermute | solution.py:443
  32.3 3.5 %collective-permute-start.2 = (f32[3,32,256]{2,1,0:T(8,128)S(1)}, f32[3,32,256]{2,1,0:T(8,128)S(1)}, u32[]{:S(2)}, u32[]{:S(2)}) collective-permute-start(f32[3,32,256]{2,1,0:T(8,128)S(1)} %bitcast.78), channel_id=1, source_target_pairs={{0,4},{4,8},{8,12},{1,5},{5,9},{9,13},{2,6},{6,10},{10,14},{3,7},{... | collective-permute-start | bytes 294920 | tf_op jit(solution)/shard_map/ppermute | solution.py:444
  36.4 3.2 %collective-permute-start.3 = (f32[3,16,256]{2,1,0:T(8,128)}, f32[3,16,256]{2,1,0:T(8,128)S(1)}, u32[]{:S(2)}, u32[]{:S(2)}) collective-permute-start(f32[3,16,256]{2,1,0:T(8,128)} %get-tuple-element.62), channel_id=1, source_target_pairs={{1,0},{2,1},{3,2},{0,3},{5,4},{6,5},{7,6},{4,7},{9,8},{10,9},{11,1... | collective-permute-start | bytes 147464 | tf_op jit(solution)/shard_map/ppermute | solution.py:450
  41.8 8.9 %collective-permute-done.3.east_ref = f32[3,16,256]{2,1,0:T(8,128)S(1)} collective-permute-done((f32[3,16,256]{2,1,0:T(8,128)}, f32[3,16,256]{2,1,0:T(8,128)S(1)}, u32[]{:S(2)}, u32[]{:S(2)}) %collective-permute-start.3) | collective-permute-done | bytes 49184 | tf_op jit(solution)/shard_map/ppermute | solution.py:450
  51.3 3.7 %collective-permute-done.4.west_ref = f32[3,16,256]{2,1,0:T(8,128)S(1)} collective-permute-done((f32[3,16,256]{2,1,0:T(8,128)S(1)}, f32[3,16,256]{2,1,0:T(8,128)S(1)}, u32[]{:S(2)}, u32[]{:S(2)}) %collective-permute-start.4) | collective-permute-done | bytes 49184 | tf_op jit(solution)/shard_map/ppermute | solution.py:451
  62.0 5.2 %ocean1.1 = (f32[16,32,256]{2,1,0:T(8,128)S(1)}, f32[16,32,256]{2,1,0:T(8,128)S(1)}, f32[16,32,256]{2,1,0:T(8,128)S(1)}, f32[16,32,256]{2,1,0:T(8,128)S(1)}, f32...) custom-call(s32[17]{0:T(128)S(1)} %pad_add_fusion.1.sc, ...), custom_call_target="tpu_custom_call" | custom-call | tf_op jit(solution)/shard_map/ocean1/pallas_call | solution.py:310
  68.0 2.8 %collective-permute-start.5 = (f32[3,32,256]{2,1,0:T(8,128)S(1)}, f32[3,32,256]{2,1,0:T(8,128)S(1)}, u32[]{:S(2)}, u32[]{:S(2)}) collective-permute-start(f32[3,32,256]{2,1,0:T(8,128)S(1)} %get-tuple-element.38), channel_id=1, source_target_pairs={{4,0},{8,4},{12,8},{5,1},{9,5},{13,9},{6,2},{10,6},{14,10},{7,3},{... | collective-permute-start | bytes 294920 | tf_op jit(solution)/shard_map/ppermute | solution.py:443
  70.8 3.0 %collective-permute-start.6 = (f32[3,32,256]{2,1,0:T(8,128)S(1)}, f32[3,32,256]{2,1,0:T(8,128)S(1)}, u32[]{:S(2)}, u32[]{:S(2)}) collective-permute-start(f32[3,32,256]{2,1,0:T(8,128)S(1)} %get-tuple-element.39), channel_id=1, source_target_pairs={{0,4},{4,8},{8,12},{1,5},{5,9},{9,13},{2,6},{6,10},{10,14},{3,7},{... | collective-permute-start | bytes 294920 | tf_op jit(solution)/shard_map/ppermute | solution.py:444
  74.2 6.7 %collective-permute-start.8 = (f32[3,16,256]{2,1,0:T(8,128)S(1)}, f32[3,16,256]{2,1,0:T(8,128)S(1)}, u32[]{:S(2)}, u32[]{:S(2)}) collective-permute-start(f32[3,16,256]{2,1,0:T(8,128)S(1)} %get-tuple-element.41), channel_id=1, source_target_pairs={{0,1},{1,2},{2,3},{3,0},{4,5},{5,6},{6,7},{7,4},{8,9},{9,10},{10,1... | collective-permute-start | bytes 147464 | tf_op jit(solution)/shard_map/ppermute | solution.py:451
  80.9 1.5 collective-permute-done.7.east_ref
  82.5 1.8 %collective-permute-done.8.west_ref = f32[3,16,256]{2,1,0:T(8,128)S(1)} collective-permute-done((f32[3,16,256]{2,1,0:T(8,128)S(1)}, f32[3,16,256]{2,1,0:T(8,128)S(1)}, u32[]{:S(2)}, u32[]{:S(2)}) %collective-permute-start.8) | collective-permute-done | bytes 49184 | tf_op jit(solution)/shard_map/ppermute | solution.py:451
  84.3 5.5 %ocean2.1 = (f32[16,32,256]{2,1,0:T(8,128)S(1)}, f32[16,32,256]{2,1,0:T(8,128)S(1)}, f32[16,32,256]{2,1,0:T(8,128)S(1)}, f32[16,32,256]{2,1,0:T(8,128)S(1)}, f32...) custom-call(s32[17]{0:T(128)S(1)} %pad_add_fusion.1.sc, ...), custom_call_target="tpu_custom_call" | custom-call | tf_op jit(solution)/shard_map/ocean2/pallas_call | solution.py:310
  91.3 2.2 %collective-permute-start.13 = (f32[3,32,256]{2,1,0:T(8,128)}, f32[3,32,256]{2,1,0:T(8,128)S(1)}, u32[]{:S(2)}, u32[]{:S(2)}) collective-permute-start(f32[3,32,256]{2,1,0:T(8,128)} %get-tuple-element.54), channel_id=1, source_target_pairs={{4,0},{8,4},{12,8},{5,1},{9,5},{13,9},{6,2},{10,6},{14,10},{7,3},{... | collective-permute-start | bytes 294920 | tf_op jit(solution)/shard_map/ppermute | solution.py:443
  93.6 3.3 %collective-permute-start.14 = (f32[3,32,256]{2,1,0:T(8,128)}, f32[3,32,256]{2,1,0:T(8,128)}, u32[]{:S(2)}, u32[]{:S(2)}) collective-permute-start(f32[3,32,256]{2,1,0:T(8,128)} %get-tuple-element.55), channel_id=1, source_target_pairs={{0,4},{4,8},{8,12},{1,5},{5,9},{9,13},{2,6},{6,10},{10,14},{3,7},{... | collective-permute-start | bytes 294920 | tf_op jit(solution)/shard_map/ppermute | solution.py:444
  98.4 2.7 %absorb.1 = (f32[16,16,256]{2,1,0:T(8,128)S(1)}, f32[16,16,256]{2,1,0:T(8,128)S(1)}, f32[16,256]{1,0:T(8,128)S(1)}, f32[16,256]{1,0:T(8,128)S(1)}, f32[16,256]{1,0:T(8,128)S(1)}, /*index=5*/f32[16,256]{1,0:T(8,128)S(1)}) custom-call(s32[17]{0:T(128)S(1)} %pad_add_fusion.1.sc, f32[16,5,16,256]{3,2,1,0:T(8,128)} %all-to-all-done.y_ref, ...), custom_call_target="tpu_custom_call" | custom-call | tf_op jit(solution)/shard_map/absorb/pallas_call | solution.py:426
  101.2 2.3 %collective-permute-start.9 = (f32[16,256]{1,0:T(8,128)S(1)}, f32[16,256]{1,0:T(8,128)S(1)}, u32[]{:S(2)}, u32[]{:S(2)}) collective-permute-start(f32[16,256]{1,0:T(8,128)S(1)} %get-tuple-element.48), channel_id=1, source_target_pairs={{4,0},{8,4},{12,8},{5,1},{9,5},{13,9},{6,2},{10,6},{14,10},{7,3},{... | collective-permute-start | bytes 49160 | tf_op jit(solution)/shard_map/ppermute | solution.py:443
  103.5 3.4 %collective-permute-start.10 = (f32[16,256]{1,0:T(8,128)S(1)}, f32[16,256]{1,0:T(8,128)S(1)}, u32[]{:S(2)}, u32[]{:S(2)}) collective-permute-start(f32[16,256]{1,0:T(8,128)S(1)} %get-tuple-element.49), channel_id=1, source_target_pairs={{0,4},{4,8},{8,12},{1,5},{5,9},{9,13},{2,6},{6,10},{10,14},{3,7},{... | collective-permute-start | bytes 49160 | tf_op jit(solution)/shard_map/ppermute | solution.py:444
  106.9 3.8 %collective-permute-start.11 = (f32[16,256]{1,0:T(8,128)S(1)}, f32[16,256]{1,0:T(8,128)S(1)}, u32[]{:S(2)}, u32[]{:S(2)}) collective-permute-start(f32[16,256]{1,0:T(8,128)S(1)} %get-tuple-element.50), channel_id=1, source_target_pairs={{16,0},{1,16},{17,1},{2,17},{18,2},{3,18},{19,3},{0,19},{20,4},{5,... | collective-permute-start | bytes 49160 | tf_op jit(solution)/shard_map/ppermute | solution.py:459
  110.7 3.3 %ocean3.1 = (f32[4,16,32,256]{3,2,1,0:T(8,128)S(1)}, f32[16,32,256]{2,1,0:T(8,128)S(1)}) custom-call(s32[17]{0:T(128)S(1)} %pad_add_fusion.1.sc, f32[16]{0:T(128)S(1)} %multiply_add_fusion.coriolis_ref, f32[16,32,256]{2,1,0:T(8,128)S(1)} %copy-done.11, f32[16,32,256]{2,1,0:T(8,128)S(1)} %copy-done.13, f32[16,32,256]{2,1,0:T(8,128)S(1)} %get-tuple-element.42.t_ref, ...), custom_call_target="tpu_custom_call" | custom-call | tf_op jit(solution)/shard_map/ocean3/pallas_call | solution.py:310
  114.1 8.4 %two_steps.1 = (f32[16,16,256]{2,1,0:T(8,128)S(1)}, f32[16,2,16,256]{3,2,1,0:T(8,128)S(1)}) custom-call(s32[17]{0:T(128)S(1)} %pad_add_fusion.1.sc, f32[16,5,16,256]{3,2,1,0:T(8,128)} %all-to-all-done.y_ref, f32[16,16,256]{2,1,0:T(8,128)S(1)} %get-tuple-element.43.t2_ref.t_ref, f32[16,16,256]{2,1,0:T(8,128)S(1)} %get-tuple-element.44.irr_ref, ...), custom_call_target="tpu_custom_call" | custom-call | tf_op jit(solution)/shard_map/two_steps/pallas_call | solution.py:426
  123.5 17.2 %all_to_all.10.flux_ref = f32[16,2,16,256]{3,2,1,0:T(8,128)S(1)} all-to-all(f32[16,2,16,256]{3,2,1,0:T(8,128)S(1)} %last_heat.1), channel_id=1, replica_groups=mesh['comp'=2,'py'=4,'px'=4] {'py','px'}, dimensions={0} | all-to-all | bytes 1048576 | tf_op jit(solution)/shard_map/all_to_all | solution.py:674
  140.8 4.0 %collective-permute-start.17 = (f32[16,2,16,256]{3,2,1,0:T(8,128)S(1)}, f32[16,2,16,256]{3,2,1,0:T(8,128)S(1)}, u32[]{:S(2)}, u32[]{:S(2)}) collective-permute-start(f32[16,2,16,256]{3,2,1,0:T(8,128)S(1)} %broadcast_select_fusion), channel_id=1, source_target_pairs={{0,16},{16,0},{1,17},{17,1},{2,18},{18,2},{3,19},{19,3},{4,20},{20... | collective-permute-start | bytes 1572872 | tf_op jit(solution)/shard_map/ppermute | solution.py:465
  144.8 11.5 %collective-permute-done.17.other_ref = f32[16,2,16,256]{3,2,1,0:T(8,128)S(1)} collective-permute-done((f32[16,2,16,256]{3,2,1,0:T(8,128)S(1)}, f32[16,2,16,256]{3,2,1,0:T(8,128)S(1)}, u32[]{:S(2)}, u32[]{:S(2)}) %collective-permute-start.17) | collective-permute-done | bytes 524320 | tf_op jit(solution)/shard_map/ppermute | solution.py:465
  156.3 1.6 %join.1 = f32[2,16,32,256]{3,2,1,0:T(8,128)} custom-call(s32[17]{0:T(128)S(1)} %pad_add_fusion.1.sc, f32[16,2,16,256]{3,2,1,0:T(8,128)S(1)} %get-tuple-element.47.absorbed_ref, f32[16,2,16,256]{3,2,1,0:T(8,128)S(1)} %all_to_all.10.flux_ref, f32[16,2,16,256]{3,2,1,0:T(8,128)S(1)} %collective-permute-done.17.other_ref), custom_call_target="tpu_custom_call" | custom-call | tf_op jit(solution)/shard_map/join/pallas_call | solution.py:426
  (104 shorter events, 17.7 us)
Async XLA Ops:
  0.0 3.8 %copy-start = (f32[16,16]{1,0:T(8,128)S(1)}, f32[16,16]{1,0:T(8,128)}, u32[]{:S(2)}) copy-start(f32[16,16]{1,0:T(8,128)} %param.17) | copy-start | bytes 3076
  0.0 3.8 %copy-start.24 = (f32[16]{0:T(128)S(1)}, f32[16]{0:T(128)}, u32[]{:S(2)}) copy-start(f32[16]{0:T(128)} %param.19) | copy-start | bytes 196
  0.0 4.2 %copy-start.21 = (s32[64,128]{1,0:T(8,128)S(1)}, s32[64,128]{1,0:T(8,128)}, u32[]{:S(2)}) copy-start(s32[64,128]{1,0:T(8,128)} %param.14) | copy-start | bytes 98308
  0.0 4.1 %copy-start.22 = (s32[64,128]{1,0:T(8,128)S(1)}, s32[64,128]{1,0:T(8,128)}, u32[]{:S(2)}) copy-start(s32[64,128]{1,0:T(8,128)} %param.15) | copy-start | bytes 98308
  1.4 2.9 %copy-start.23 = (s32[16,16]{1,0:T(8,128)S(1)}, s32[16,16]{1,0:T(8,128)}, u32[]{:S(2)}) copy-start(s32[16,16]{1,0:T(8,128)} %param.16) | copy-start | bytes 3076
  1.6 13.8 %collective-permute-start = (f32[2,16,16,256]{3,2,1,0:T(8,128)S(1)}, f32[2,16,16,256]{3,2,1,0:T(8,128)S(1)}, u32[]{:S(2)}, u32[]{:S(2)}) collective-permute-start(f32[2,16,16,256]{3,2,1,0:T(8,128)S(1)} %slice_select_fusion), channel_id=1, source_target_pairs={{0,16},{16,0},{1,17},{17,1},{2,18},{18,2},{3,19},{19,3},{4,20},{20... | collective-permute-start | bytes 1572872 | tf_op jit(solution)/shard_map/ppermute | solution.py:465
  5.0 3.4 %copy-start.2 = (f32[16,1,512,256]{3,2,1,0:T(8,128)S(1)}, f32[16,1,512,256]{3,2,1,0:T(8,128)}, u32[]{:S(2)}) copy-start(f32[16,1,512,256]{3,2,1,0:T(8,128)} %param.12) | copy-start | bytes 25165828
  8.4 5.0 %copy-start.25 = (f32[16]{0:T(128)S(1)}, f32[16]{0:T(128)}, u32[]{:S(2)}) copy-start(f32[16]{0:T(128)} %param.18) | copy-start | bytes 196
  15.4 4.9 %copy-start.6 = (f32[2,16,16,256]{3,2,1,0:T(8,128)}, f32[2,16,16,256]{3,2,1,0:T(8,128)S(1)}, u32[]{:S(2)}) copy-start(f32[2,16,16,256]{3,2,1,0:T(8,128)S(1)} %collective-permute-done.got_ref.rest_1_) | copy-start | bytes 1572868
  20.3 7.5 %copy-start.3 = (f32[16,32,256]{2,1,0:T(8,128)S(1)}, f32[16,32,256]{2,1,0:T(8,128)}, u32[]{:S(2)}) copy-start(f32[16,32,256]{2,1,0:T(8,128)} %t_ref.1) | copy-start | bytes 1572868
  20.3 78.2 %all-to-all-start = ((f32[16,5,16,256]{3,2,1,0:T(8,128)}), f32[16,5,16,256]{3,2,1,0:T(8,128)}, u32[]{:S(2)}, u32[]{:S(2)}) async-start(f32[16,5,16,256]{3,2,1,0:T(8,128)} %first_tracer.1), calls=%async_computation | async-start | bytes 2621440 | tf_op jit(solution)/shard_map/all_to_all | solution.py:642
  29.9 10.3 %copy-start.20 = (f32[2,16,32,256]{3,2,1,0:T(8,128)S(1)}, f32[2,16,32,256]{3,2,1,0:T(8,128)}, u32[]{:S(2)}) copy-start(f32[2,16,32,256]{3,2,1,0:T(8,128)} %param.10) | copy-start | bytes 3145732
  30.0 25.7 %collective-permute-start.1 = (f32[3,32,256]{2,1,0:T(8,128)S(1)}, f32[3,32,256]{2,1,0:T(8,128)S(1)}, u32[]{:S(2)}, u32[]{:S(2)}) collective-permute-start(f32[3,32,256]{2,1,0:T(8,128)S(1)} %bitcast.77), channel_id=1, source_target_pairs={{4,0},{8,4},{12,8},{5,1},{9,5},{13,9},{6,2},{10,6},{14,10},{7,3},{... | collective-permute-start | bytes 294920 | tf_op jit(solution)/shard_map/ppermute | solution.py:443
  32.3 23.4 %collective-permute-start.2 = (f32[3,32,256]{2,1,0:T(8,128)S(1)}, f32[3,32,256]{2,1,0:T(8,128)S(1)}, u32[]{:S(2)}, u32[]{:S(2)}) collective-permute-start(f32[3,32,256]{2,1,0:T(8,128)S(1)} %bitcast.78), channel_id=1, source_target_pairs={{0,4},{4,8},{8,12},{1,5},{5,9},{9,13},{2,6},{6,10},{10,14},{3,7},{... | collective-permute-start | bytes 294920 | tf_op jit(solution)/shard_map/ppermute | solution.py:444
  36.4 14.3 %collective-permute-start.3 = (f32[3,16,256]{2,1,0:T(8,128)}, f32[3,16,256]{2,1,0:T(8,128)S(1)}, u32[]{:S(2)}, u32[]{:S(2)}) collective-permute-start(f32[3,16,256]{2,1,0:T(8,128)} %get-tuple-element.62), channel_id=1, source_target_pairs={{1,0},{2,1},{3,2},{0,3},{5,4},{6,5},{7,6},{4,7},{9,8},{10,9},{11,1... | collective-permute-start | bytes 147464 | tf_op jit(solution)/shard_map/ppermute | solution.py:450
  39.6 15.5 %collective-permute-start.4 = (f32[3,16,256]{2,1,0:T(8,128)S(1)}, f32[3,16,256]{2,1,0:T(8,128)S(1)}, u32[]{:S(2)}, u32[]{:S(2)}) collective-permute-start(f32[3,16,256]{2,1,0:T(8,128)S(1)} %get-tuple-element.61), channel_id=1, source_target_pairs={{0,1},{1,2},{2,3},{3,0},{4,5},{5,6},{6,7},{7,4},{8,9},{9,10},{10,1... | collective-permute-start | bytes 147464 | tf_op jit(solution)/shard_map/ppermute | solution.py:451
  68.0 16.3 %collective-permute-start.5 = (f32[3,32,256]{2,1,0:T(8,128)S(1)}, f32[3,32,256]{2,1,0:T(8,128)S(1)}, u32[]{:S(2)}, u32[]{:S(2)}) collective-permute-start(f32[3,32,256]{2,1,0:T(8,128)S(1)} %get-tuple-element.38), channel_id=1, source_target_pairs={{4,0},{8,4},{12,8},{5,1},{9,5},{13,9},{6,2},{10,6},{14,10},{7,3},{... | collective-permute-start | bytes 294920 | tf_op jit(solution)/shard_map/ppermute | solution.py:443
  70.8 13.5 %collective-permute-start.6 = (f32[3,32,256]{2,1,0:T(8,128)S(1)}, f32[3,32,256]{2,1,0:T(8,128)S(1)}, u32[]{:S(2)}, u32[]{:S(2)}) collective-permute-start(f32[3,32,256]{2,1,0:T(8,128)S(1)} %get-tuple-element.39), channel_id=1, source_target_pairs={{0,4},{4,8},{8,12},{1,5},{5,9},{9,13},{2,6},{6,10},{10,14},{3,7},{... | collective-permute-start | bytes 294920 | tf_op jit(solution)/shard_map/ppermute | solution.py:444
  73.8 8.7 %collective-permute-start.7 = (f32[3,16,256]{2,1,0:T(8,128)S(1)}, f32[3,16,256]{2,1,0:T(8,128)S(1)}, u32[]{:S(2)}, u32[]{:S(2)}) collective-permute-start(f32[3,16,256]{2,1,0:T(8,128)S(1)} %get-tuple-element.40), channel_id=1, source_target_pairs={{1,0},{2,1},{3,2},{0,3},{5,4},{6,5},{7,6},{4,7},{9,8},{10,9},{11,1... | collective-permute-start | bytes 147464 | tf_op jit(solution)/shard_map/ppermute | solution.py:450
  74.2 10.1 %collective-permute-start.8 = (f32[3,16,256]{2,1,0:T(8,128)S(1)}, f32[3,16,256]{2,1,0:T(8,128)S(1)}, u32[]{:S(2)}, u32[]{:S(2)}) collective-permute-start(f32[3,16,256]{2,1,0:T(8,128)S(1)} %get-tuple-element.41), channel_id=1, source_target_pairs={{0,1},{1,2},{2,3},{3,0},{4,5},{5,6},{6,7},{7,4},{8,9},{9,10},{10,1... | collective-permute-start | bytes 147464 | tf_op jit(solution)/shard_map/ppermute | solution.py:451
  91.3 19.4 %collective-permute-start.13 = (f32[3,32,256]{2,1,0:T(8,128)}, f32[3,32,256]{2,1,0:T(8,128)S(1)}, u32[]{:S(2)}, u32[]{:S(2)}) collective-permute-start(f32[3,32,256]{2,1,0:T(8,128)} %get-tuple-element.54), channel_id=1, source_target_pairs={{4,0},{8,4},{12,8},{5,1},{9,5},{13,9},{6,2},{10,6},{14,10},{7,3},{... | collective-permute-start | bytes 294920 | tf_op jit(solution)/shard_map/ppermute | solution.py:443
  93.6 17.2 %collective-permute-start.14 = (f32[3,32,256]{2,1,0:T(8,128)}, f32[3,32,256]{2,1,0:T(8,128)}, u32[]{:S(2)}, u32[]{:S(2)}) collective-permute-start(f32[3,32,256]{2,1,0:T(8,128)} %get-tuple-element.55), channel_id=1, source_target_pairs={{0,4},{4,8},{8,12},{1,5},{5,9},{9,13},{2,6},{6,10},{10,14},{3,7},{... | collective-permute-start | bytes 294920 | tf_op jit(solution)/shard_map/ppermute | solution.py:444
  96.9 6.6 %collective-permute-start.15 = (f32[3,16,256]{2,1,0:T(8,128)}, f32[3,16,256]{2,1,0:T(8,128)}, u32[]{:S(2)}, u32[]{:S(2)}) collective-permute-start(f32[3,16,256]{2,1,0:T(8,128)} %get-tuple-element.56), channel_id=1, source_target_pairs={{1,0},{2,1},{3,2},{0,3},{5,4},{6,5},{7,6},{4,7},{9,8},{10,9},{11,1... | collective-permute-start | bytes 147464 | tf_op jit(solution)/shard_map/ppermute | solution.py:450
  98.0 8.9 %collective-permute-start.16 = (f32[3,16,256]{2,1,0:T(8,128)}, f32[3,16,256]{2,1,0:T(8,128)}, u32[]{:S(2)}, u32[]{:S(2)}) collective-permute-start(f32[3,16,256]{2,1,0:T(8,128)} %get-tuple-element.57), channel_id=1, source_target_pairs={{0,1},{1,2},{2,3},{3,0},{4,5},{5,6},{6,7},{7,4},{8,9},{9,10},{10,1... | collective-permute-start | bytes 147464 | tf_op jit(solution)/shard_map/ppermute | solution.py:451
  98.4 12.3 %copy-start.11 = (f32[16,32,256]{2,1,0:T(8,128)S(1)}, f32[16,32,256]{2,1,0:T(8,128)}, u32[]{:S(2)}) copy-start(f32[16,32,256]{2,1,0:T(8,128)} %copy-done.10) | copy-start | bytes 1572868
  98.4 12.3 %copy-start.13 = (f32[16,32,256]{2,1,0:T(8,128)S(1)}, f32[16,32,256]{2,1,0:T(8,128)}, u32[]{:S(2)}) copy-start(f32[16,32,256]{2,1,0:T(8,128)} %copy-done.12) | copy-start | bytes 1572868
  101.2 12.9 %copy-start.9 = (f32[16,32,256]{2,1,0:T(8,128)S(1)}, f32[16,32,256]{2,1,0:T(8,128)}, u32[]{:S(2)}) copy-start(f32[16,32,256]{2,1,0:T(8,128)} %copy-done.8) | copy-start | bytes 1572868
  101.2 21.3 %collective-permute-start.9 = (f32[16,256]{1,0:T(8,128)S(1)}, f32[16,256]{1,0:T(8,128)S(1)}, u32[]{:S(2)}, u32[]{:S(2)}) collective-permute-start(f32[16,256]{1,0:T(8,128)S(1)} %get-tuple-element.48), channel_id=1, source_target_pairs={{4,0},{8,4},{12,8},{5,1},{9,5},{13,9},{6,2},{10,6},{14,10},{7,3},{... | collective-permute-start | bytes 49160 | tf_op jit(solution)/shard_map/ppermute | solution.py:443
  103.5 19.0 %collective-permute-start.10 = (f32[16,256]{1,0:T(8,128)S(1)}, f32[16,256]{1,0:T(8,128)S(1)}, u32[]{:S(2)}, u32[]{:S(2)}) collective-permute-start(f32[16,256]{1,0:T(8,128)S(1)} %get-tuple-element.49), channel_id=1, source_target_pairs={{0,4},{4,8},{8,12},{1,5},{5,9},{9,13},{2,6},{6,10},{10,14},{3,7},{... | collective-permute-start | bytes 49160 | tf_op jit(solution)/shard_map/ppermute | solution.py:444
  106.9 15.5 %collective-permute-start.11 = (f32[16,256]{1,0:T(8,128)S(1)}, f32[16,256]{1,0:T(8,128)S(1)}, u32[]{:S(2)}, u32[]{:S(2)}) collective-permute-start(f32[16,256]{1,0:T(8,128)S(1)} %get-tuple-element.50), channel_id=1, source_target_pairs={{16,0},{1,16},{17,1},{2,17},{18,2},{3,18},{19,3},{0,19},{20,4},{5,... | collective-permute-start | bytes 49160 | tf_op jit(solution)/shard_map/ppermute | solution.py:459
  110.7 11.7 %collective-permute-start.12 = (f32[16,256]{1,0:T(8,128)S(1)}, f32[16,256]{1,0:T(8,128)S(1)}, u32[]{:S(2)}, u32[]{:S(2)}) collective-permute-start(f32[16,256]{1,0:T(8,128)S(1)} %get-tuple-element.51), channel_id=1, source_target_pairs={{0,16},{16,1},{1,17},{17,2},{2,18},{18,3},{3,19},{19,0},{4,20},{20... | collective-permute-start | bytes 49160 | tf_op jit(solution)/shard_map/ppermute | solution.py:460
  140.8 15.5 %collective-permute-start.17 = (f32[16,2,16,256]{3,2,1,0:T(8,128)S(1)}, f32[16,2,16,256]{3,2,1,0:T(8,128)S(1)}, u32[]{:S(2)}, u32[]{:S(2)}) collective-permute-start(f32[16,2,16,256]{3,2,1,0:T(8,128)S(1)} %broadcast_select_fusion), channel_id=1, source_target_pairs={{0,16},{16,0},{1,17},{17,1},{2,18},{18,2},{3,19},{19,3},{4,20},{20... | collective-permute-start | bytes 1572872 | tf_op jit(solution)/shard_map/ppermute | solution.py:465
  (13 other events, 11.4 us)
where the time goes:
time: 160 us; the launch traced here: 158 us
  starting transfers between devices  51.9 us (32%)
  Pallas kernels  37.5 us (23%)
  waiting for transfers between devices  29.5 us (18%)
  local copies, waits for them, and re-layouts  18.2 us (11%)
  blocking collectives  17.2 us (11%)
  other arithmetic  2.62 us (2%)
    all_to_all x1, blocking collectives, shards(): lax.all_to_all(back, ('py', 'px'), split_axis=0, concat_axis=0, tiled=True)  17.2 us
    unnamed x58, local copies, waits for them, and re-layouts  15.9 us
    pallas_call x3, Pallas kernels, ocean(): pl.pallas_call(functools.partial(ocean_kernel, advance), grid_spec=pltpu....  14 us
    pallas_call x4, Pallas kernels, call(): pl.pallas_call(kernel, grid_spec=pltpu.PrefetchScalarGridSpec(num_scalar_...  13.7 us
    ppermute x2, waiting for transfers between devices, swap(): return lax.ppermute(block, 'comp', [(0, 1), (1, 0)])  13.4 us
    ppermute x4, starting transfers between devices, exchange_rows(): south = lax.ppermute(high, 'py', [(i, i + 1) for i in range(count - 1)])  13.2 us
    ppermute x3, waiting for transfers between devices, exchange_cols(): east = lax.ppermute(low, 'px', [((i + 1) % count, i) for i in range(count)])  10.5 us
    ppermute x4, starting transfers between devices, exchange_rows(): north = lax.ppermute(low, 'py', [(i + 1, i) for i in range(count - 1)])  9.47 us
  transfers between devices with their start and end apart: 19, of which 6 were waited for; matrix products, arithmetic and copies ran while one was open for 4% of the time, Pallas kernels for 19%

commit v1 on v0

--- a/solution.py
+++ b/solution.py
@@ -23,9 +23,14 @@
 CY = 16
 CX = 32
 KEPT = (0, 1, 2, 4, 5)
-VMEM = pl.BlockSpec(memory_space=pltpu.VMEM)
 SMEM = pl.BlockSpec(memory_space=pltpu.SMEM)
-PARAMS = pltpu.CompilerParams(vmem_limit_bytes=40 * 1024 * 1024)
+PARAMS = pltpu.CompilerParams(vmem_limit_bytes=24 * 1024 * 1024)
+STREAMED = pltpu.CompilerParams(vmem_limit_bytes=60 * 1024 * 1024)
+
+
+def whole(array):
+    zeros = (0,) * len(array.shape)
+    return pl.BlockSpec(array.shape, lambda i, c: zeros)
 
 
 def shape_of(*dims):
@@ -94,15 +99,18 @@
 def project_kernel(sc, x_ref, w_ref, depth_ref, y_ref, g_ref, chl_ref):
     fields, patches, cols, levels = x_ref.shape
 
+    mixed = [k for k in range(y_ref.shape[0]) if k != 4]
+
     def one(q, carry):
-        values = [x_ref[j, q] for j in range(fields)]
-        for k in range(y_ref.shape[0]):
-            total = w_ref[k, 0] * values[0]
-            for j in range(1, fields):
-                total = total + w_ref[k, j] * values[j]
+        value = x_ref[0, q]
+        y_ref[4, q] = value
+        totals = [w_ref[k, 0] * value for k in mixed]
+        for j in range(1, fields):
+            value = x_ref[j, q]
+            totals = [t + w_ref[k, j] * value for t, k in zip(totals, mixed)]
+        for k, total in zip(mixed, totals):
             y_ref[k, q] = total
-            if k == 0:
-                chl_ref[q] = softplus(total)
+        chl_ref[q] = softplus(totals[0])
         return carry
 
     lax.fori_loop(0, patches, one, 0)
@@ -136,7 +144,7 @@
             scratch_shapes=[pltpu.VMEM((block, half, levels), jnp.float32)],
         ),
         out_shape=(shape_of(kinds, patches, half, levels), shape_of(patches, half, levels)),
-        compiler_params=PARAMS,
+        compiler_params=STREAMED,
         name="project",
     )(comp, tracers, weights, depth)
 
@@ -158,7 +166,7 @@
             out_ref[q, place] = wet * (y + step_tracer * change)
         return carry
 
-    lax.fori_loop(0, patches, one, 0)
+    lax.fori_loop(0, patches, one, 0, unroll=2)
 
 
 def half_spec(lead, cols, levels):
@@ -167,99 +175,162 @@
 
 
 def first_tracer(comp, projected, g, got, linked, depth, shares):
-    _, patches, half, levels = projected.shape
+    kinds, patches, half, levels = projected.shape
+    block = 4
     return pl.pallas_call(
         first_tracer_kernel,
         grid_spec=pltpu.PrefetchScalarGridSpec(
             num_scalar_prefetch=1,
-            grid=(1,),
-            in_specs=[VMEM, VMEM, VMEM, half_spec((2, patches), half, levels), VMEM, SMEM],
-            out_specs=VMEM,
+            grid=(patches // block,),
+            in_specs=[
+                pl.BlockSpec((kinds, block, half, levels), lambda i, c: (0, i, 0, 0)),
+                pl.BlockSpec((block, half, levels), lambda i, c: (i, 0, 0)),
+                pl.BlockSpec((2, block, half, levels), lambda i, c: (0, i, 0, 0)),
+                pl.BlockSpec((2, block, half, levels), lambda i, c: (0, i, c[0], 0)),
+                pl.BlockSpec((block, half, 1), lambda i, c: (i, 0, 0)),
+                SMEM,
+            ],
+            out_specs=pl.BlockSpec((block, len(KEPT), half, levels), lambda i, c: (i, 0, 0, 0)),
         ),
         out_shape=shape_of(patches, len(KEPT), half, levels),
-        compiler_params=PARAMS,
+        compiler_params=STREAMED,
         name="first_tracer",
     )(comp, projected, g, got, linked, depth, shares)
 
 
+def pack_kernel(sc, linked_ref, row0_ref, row1_ref, col0_ref, col1_ref, t0_ref, t1_ref, tc0_ref, tc1_ref,
+                sent_ref, low_ref, high_ref, left_ref, right_ref):
+    _, strips, strip, levels = linked_ref.shape
+    half = strip // 2
+
+    @pl.when(sc[0] == 0)
+    def _():
+        for part in range(2):
+            cols = slice(part * half, (part + 1) * half)
+            sent_ref[part] = linked_ref[0, :, cols] + linked_ref[1, :, cols]
+
+    @pl.when(sc[0] != 0)
+    def _():
+        sent_ref[...] = linked_ref[:, :, :half]
+
+    last = col1_ref.shape[2] - 1
+    for f in range(2):
+        low_ref[f] = row0_ref[f, 0]
+        high_ref[f] = row1_ref[f, 0]
+        left_ref[f] = col0_ref[f, :, 0]
+        right_ref[f] = col1_ref[f, :, last]
+    low_ref[2] = t0_ref[0]
+    high_ref[2] = t1_ref[0]
+    left_ref[2] = tc0_ref[:, 0]
+    right_ref[2] = tc1_ref[:, last]
+
+
+def pack(comp, linked, speeds, heat):
+    _, strips, strip, levels = linked.shape
+    rows, cols, _ = heat.shape
+    outs = (
+        shape_of(2, strips, strip // 2, levels), shape_of(3, cols, levels), shape_of(3, cols, levels),
+        shape_of(3, rows, levels), shape_of(3, rows, levels),
+    )
+    edge = min(8, cols)
+    return pl.pallas_call(
+        pack_kernel,
+        grid_spec=pltpu.PrefetchScalarGridSpec(
+            num_scalar_prefetch=1,
+            grid=(1,),
+            in_specs=[
+                whole(linked),
+                pl.BlockSpec((2, 1, cols, levels), lambda i, c: (0, 0, 0, 0)),
+                pl.BlockSpec((2, 1, cols, levels), lambda i, c: (0, rows - 1, 0, 0)),
+                pl.BlockSpec((2, rows, edge, levels), lambda i, c: (0, 0, 0, 0)),
+                pl.BlockSpec((2, rows, edge, levels), lambda i, c: (0, 0, cols // edge - 1, 0)),
+                pl.BlockSpec((1, cols, levels), lambda i, c: (0, 0, 0)),
+                pl.BlockSpec((1, cols, levels), lambda i, c: (rows - 1, 0, 0)),
+                pl.BlockSpec((rows, edge, levels), lambda i, c: (0, 0, 0)),
+                pl.BlockSpec((rows, edge, levels), lambda i, c: (0, cols // edge - 1, 0)),
+            ],
+            out_specs=[whole(o) for o in outs],
+        ),
+        out_shape=outs,
+        compiler_params=STREAMED,
+        name="pack",
+    )(comp, linked, speeds, speeds, speeds, speeds, heat, heat, heat, heat)
+
+
 def ocean_kernel(
-    advance, sc, coriolis_ref, u_ref, v_ref, t_ref, north_ref, south_ref, east_ref, west_ref, depth_ref,
+    advance, sc, coriolis_ref, speed_ref, t_ref, north_ref, south_ref, east_ref, west_ref, depth_ref,
     *rest,
 ):
     rest = list(rest)
+    u_ref, v_ref = speed_ref.at[0], speed_ref.at[1]
     if advance == 1:
         linked_ref, got_ref = rest[:2]
         rest = rest[2:]
-    if advance < 3:
-        un_ref, vn_ref, tn_ref, rise_ref, row0_ref, row1_ref, col0_ref, col1_ref = rest[:8]
-        p_ref, pn_ref, ps_ref, pe_ref, pw_ref, div_ref = rest[8:]
-    else:
-        face_ref, rise_ref, div_ref = rest
-    rows, cols, levels = u_ref.shape
-    if advance < 3:
-        above = level_matrix(levels, "above")
-        p_ref[...] = (
-            weight_pull_factor * level_sums(t_ref[...].reshape(rows * cols, levels), above)
-        ).reshape(rows, cols, levels)
-        for target, source in ((pn_ref, north_ref), (ps_ref, south_ref), (pe_ref, east_ref), (pw_ref, west_ref)):
-            target[...] = weight_pull_factor * level_sums(source[2], above)
-    place = lax.broadcasted_iota(jnp.int32, (cols, levels), 0)
-
-    def row(y, at):
-        shape = (cols, levels)
+    next_ref, tn_ref, rise_ref = rest[:3]
+    edge_refs = rest[3:7] if advance == 1 else ()
+    un_ref, vn_ref = next_ref.at[0], next_ref.at[1]
+    p_ref, pn_ref, ps_ref, pe_ref, pw_ref, div_ref = rest[-6:]
+    rows, cols, levels = t_ref.shape
+    above = level_matrix(levels, "above")
+    p_ref[...] = (
+        weight_pull_factor * level_sums(t_ref[...].reshape(rows * cols, levels), above)
+    ).reshape(rows, cols, levels)
+    for target, source in ((pn_ref, north_ref), (ps_ref, south_ref), (pe_ref, east_ref), (pw_ref, west_ref)):
+        target[...] = weight_pull_factor * level_sums(source[2], above)
+    lanes = min(128, levels)
+    place = lax.broadcasted_iota(jnp.int32, (cols, lanes), 0)
+    at_east, at_west = place == cols - 1, place == 0
+
+    def piece(y, at, lane):
         north_in = at < rows - 1
         south_in = at > 0
-
-        def around(ref, f):
-            x = ref[y]
-            e = east_ref[f, pl.ds(y, 1)]
-            w = west_ref[f, pl.ds(y, 1)]
+        part = slice(lane, lane + lanes)
+        level = lane + lax.broadcasted_iota(jnp.int32, (cols, lanes), 1)
+
+        def around(x, e, w, n, s):
             return (
-                x,
-                jnp.where(place == cols - 1, e, pltpu.roll(x, cols - 1, 0)),
-                jnp.where(place == 0, w, pltpu.roll(x, 1, 0)),
-                ref[y + 1] if north_in else north_ref[f],
-                ref[y - 1] if south_in else south_ref[f],
+                x, jnp.where(at_east, e, pltpu.roll(x, cols - 1, 0)), jnp.where(at_west, w, pltpu.roll(x, 1, 0)), n, s
             )
 
-        wet = [wet_of(depth_ref[i, y], shape) for i in range(5)]
-        u = around(u_ref, 0)
-        v = around(v_ref, 1)
-        east = 0.5 * (u[0] + u[1]) * wet[0] * wet[1]
-        west = 0.5 * (u[2] + u[0]) * wet[2] * wet[0]
-        north = 0.5 * (v[0] + v[3]) * wet[0] * wet[3]
-        south = 0.5 * (v[4] + v[0]) * wet[4] * wet[0]
-        div_ref[y] = east - west + north - south
-        if advance == 3:
-            for i, face in enumerate((east, west, north, south)):
-                face_ref[i, y] = face
-            return
-        t = around(t_ref, 2)
-        pe = pe_ref[pl.ds(y, 1)]
-        pw = pw_ref[pl.ds(y, 1)]
-        p0 = p_ref[y]
-        p = (
-            p0,
-            jnp.where(place == cols - 1, pe, pltpu.roll(p0, cols - 1, 0)),
-            jnp.where(place == 0, pw, pltpu.roll(p0, 1, 0)),
-            p_ref[y + 1] if north_in else pn_ref[...],
-            p_ref[y - 1] if south_in else ps_ref[...],
+        def field(ref, f):
+            return around(
+                ref[y, :, part],
+                east_ref[f, pl.ds(y, 1)][:, part],
+                west_ref[f, pl.ds(y, 1)][:, part],
+                ref[y + 1, :, part] if north_in else north_ref[f, :, part],
+                ref[y - 1, :, part] if south_in else south_ref[f, :, part],
+            )
+
+        wet = [jnp.where(level < depth_ref[i, y], 1.0, 0.0) for i in range(5)]
+        u = field(u_ref, 0)
+        v = field(v_ref, 1)
+        own = 0.5 * wet[0]
+        east = (u[0] + u[1]) * (own * wet[1])
+        west = (u[2] + u[0]) * (own * wet[2])
+        north = (v[0] + v[3]) * (own * wet[3])
+        south = (v[4] + v[0]) * (own * wet[4])
+        div_ref[y, :, part] = east - west + north - south
+        t = field(t_ref, 2)
+        p = around(
+            p_ref[y, :, part],
+            pe_ref[pl.ds(y, 1)][:, part],
+            pw_ref[pl.ds(y, 1)][:, part],
+            p_ref[y + 1, :, part] if north_in else pn_ref[:, part],
+            p_ref[y - 1, :, part] if south_in else ps_ref[:, part],
         )
+        wets = wet[1] + wet[2] + wet[3] + wet[4]
 
         def spread(x):
-            return (
-                wet[1] * (x[1] - x[0]) + wet[2] * (x[2] - x[0])
-                + wet[3] * (x[3] - x[0]) + wet[4] * (x[4] - x[0])
-            )
+            return wet[1] * x[1] + wet[2] * x[2] + wet[3] * x[3] + wet[4] * x[4] - wets * x[0]
 
         carry_along = 0.5 * (
             east * (t[0] + t[1]) - west * (t[2] + t[0]) + north * (t[0] + t[3]) - south * (t[4] + t[0])
         )
         change = spreading * spread(t) - carry_along
         if advance == 1:
+            halves = [got_ref[i, y, :, part] for i in range(2)]
             absorb = jnp.where(
-                sc[0] == 0, linked_ref[0, y] + linked_ref[1, y],
-                jnp.concatenate([got_ref[0, y], got_ref[1, y]], axis=0),
+                sc[0] == 0, linked_ref[0, y, :, part] + linked_ref[1, y, :, part], jnp.concatenate(halves, axis=0)
             )
             change = change + heat_gain * absorb
         zonal = 0.5 * (wet[1] * (p[1] - p[0]) + wet[2] * (p[0] - p[2]))
@@ -271,13 +342,15 @@
             wet[0] * (t[0] + advance_marine * change),
         )
         for f, (ref, value) in enumerate(zip((un_ref, vn_ref, tn_ref), results)):
-            ref[y] = value
-            col0_ref[f, pl.ds(y, 1)] = value[:1]
-            col1_ref[f, pl.ds(y, 1)] = value[cols - 1 :]
-            if not south_in:
-                row0_ref[f] = value
-            if not north_in:
-                row1_ref[f] = value
+            ref[y, :, part] = value
+
+    def row(y, at):
+        for lane in range(0, levels, lanes):
+            piece(y, at, lane)
+        if edge_refs:
+            for f, ref in enumerate((un_ref, vn_ref, tn_ref)):
+                edge_refs[2][f, pl.ds(y, 1)] = ref[y, :1]
+                edge_refs[3][f, pl.ds(y, 1)] = ref[y, cols - 1 :]
 
     row(0, 0)
 
@@ -287,75 +360,75 @@
 
     lax.fori_loop(1, rows - 1, inner, 0)
     row(rows - 1, rows - 1)
+    if edge_refs:
+        for f, ref in enumerate((un_ref, vn_ref, tn_ref)):
+            edge_refs[0][f] = ref[0]
+            edge_refs[1][f] = ref[rows - 1]
     sums = level_sums(div_ref[...].reshape(rows * cols, levels), level_matrix(levels, "below"))
     rise_ref[...] = -sums.reshape(rows, cols, levels)
 
 
-def ocean(advance, comp, coriolis, fields, halos, depth, linked=None, got=None):
-    rows, cols, levels = fields[0].shape
+def ocean(advance, comp, coriolis, speeds, heat, halos, depth, linked=None, got=None):
+    rows, cols, levels = heat.shape
     grid = shape_of(rows, cols, levels)
-    count = len(halos[0])
-    if advance < 3:
-        outs = (
-            grid, grid, grid, grid,
+    outs = (shape_of(2, rows, cols, levels), grid, grid)
+    if advance == 1:
+        outs += (
             shape_of(3, cols, levels), shape_of(3, cols, levels), shape_of(3, rows, levels), shape_of(3, rows, levels),
         )
-        scratch = [
-            (rows, cols, levels), (cols, levels), (cols, levels), (rows, levels), (rows, levels), (rows, cols, levels),
-        ]
-    else:
-        outs = (shape_of(4, rows, cols, levels), grid)
-        scratch = [(rows, cols, levels)]
-    args = [coriolis, *fields, *halos, depth] + ([linked, got] if advance == 1 else [])
+    scratch = [
+        (rows, cols, levels), (cols, levels), (cols, levels), (rows, levels), (rows, levels), (rows, cols, levels),
+    ]
+    args = [coriolis, speeds, heat, *halos, depth] + ([linked, got] if advance == 1 else [])
     return pl.pallas_call(
         functools.partial(ocean_kernel, advance),
         grid_spec=pltpu.PrefetchScalarGridSpec(
             num_scalar_prefetch=1,
             grid=(1,),
-            in_specs=[SMEM] + [VMEM] * (len(args) - 1),
-            out_specs=[VMEM] * len(outs),
+            in_specs=[SMEM] + [whole(a) for a in args[1:]],
+            out_specs=[whole(o) for o in outs],
             scratch_shapes=[pltpu.VMEM(s, jnp.float32) for s in scratch],
         ),
         out_shape=outs,
-        compiler_params=PARAMS,
+        compiler_params=STREAMED if advance == 1 else PARAMS,
         name=f"ocean{advance}",
     )(comp, *args)
 
 
-def absorb_kernel(sc, y_ref, t_ref, t2_ref, irr_ref, row0_ref, row1_ref, col0_ref, col1_ref, depth_ref, chl_ref):
-    patches, _, cols, levels = y_ref.shape
-    flat = (patches * cols, levels)
+def absorb_kernel(
+    sc, y_ref, t_ref, speed_ref, depth_ref, t2_ref, irr_ref, row0_ref, row1_ref, col0_ref, col1_ref, chl_ref
+):
+    rows, cols, levels = t_ref.shape
+    flat = (rows * cols, levels)
 
     def gather(s, carry):
         chl_ref[s] = softplus(y_ref[sc[1 + s], 0])
         return carry
 
-    lax.fori_loop(0, patches, gather, 0)
+    lax.fori_loop(0, rows, gather, 0, unroll=2)
     chl = chl_ref[...].reshape(flat)
     sums = level_sums(chl, level_matrix(levels, "prefix"))
     absorbed, irradiance = light(chl, sums, level_of(flat))
-    wet = wet_of(depth_ref[0], (patches, cols, levels))
-    both = (absorbed[0] + absorbed[1]).reshape(patches, cols, levels)
-    t2 = t_ref[...] + advance_marine * heat_gain * (wet * both)
-    t2_ref[...] = t2
-    irr_ref[...] = irradiance.reshape(patches, cols, levels)
-    row0_ref[...] = t2_ref[0]
-    row1_ref[...] = t2_ref[patches - 1]
-    for s in range(patches):
-        col0_ref[pl.ds(s, 1)] = t2_ref[s, :1]
-        col1_ref[pl.ds(s, 1)] = t2_ref[s, cols - 1 :]
-
-
-def two_steps_kernel(
-    sc, y_ref, t2_ref, irr_ref, t1_ref, r1_ref, r2_ref, depth_ref, share_ref,
-    heat_ref, absorbed_ref, a_ref, b_ref, n_ref, chl_ref,
+    wet = wet_of(depth_ref[0], t_ref.shape)
+    both = (absorbed[0] + absorbed[1]).reshape(t_ref.shape)
+    t2_ref[...] = t_ref[...] + advance_marine * heat_gain * (wet * both)
+    irr_ref[...] = irradiance.reshape(t_ref.shape)
+    for f, ref in enumerate((speed_ref.at[0], speed_ref.at[1], t2_ref)):
+        row0_ref[f] = ref[0]
+        row1_ref[f] = ref[rows - 1]
+        for y in range(rows):
+            col0_ref[f, pl.ds(y, 1)] = ref[y, :1]
+            col1_ref[f, pl.ds(y, 1)] = ref[y, cols - 1 :]
+
+
+def second_kernel(
+    sc, y_ref, irr_ref, t1_ref, r1_ref, depth_ref, share_ref, heat_ref, a_ref, b_ref, g_ref, n_ref, chl_ref
 ):
     patches, _, cols, levels = y_ref.shape
     flat = (patches * cols, levels)
     whole = (patches, cols, levels)
-    prefix = level_matrix(levels, "prefix")
-
-    def second(s, carry):
+
+    def one(s, carry):
         owner = sc[1 + s]
         wet = wet_of(depth_ref[0, s], (cols, levels))
         warm = jnp.exp(heating_speed * t1_ref[s])
@@ -368,46 +441,72 @@
         chl_ref[s] = softplus(a_ref[s])
         return carry
 
-    lax.fori_loop(0, patches, second, 0)
+    lax.fori_loop(0, patches, one, 0, unroll=4)
     chl = chl_ref[...].reshape(flat)
-    absorbed, irradiance = light(chl, level_sums(chl, prefix), level_of(flat))
+    absorbed, irradiance = light(chl, level_sums(chl, level_matrix(levels, "prefix")), level_of(flat))
     wet = wet_of(depth_ref[0], whole)
     heat_ref[...] = advance_marine * heat_gain * (wet * (absorbed[0] + absorbed[1]).reshape(whole))
-    n_ref[...] = uptake_rate * irradiance.reshape(whole) * saturation(n_ref[...])
-
-    def third(s, carry):
+    g_ref[...] = uptake_rate * irradiance.reshape(whole) * saturation(n_ref[...])
+
+
+def third_kernel(sc, a_ref, b_ref, g_ref, t2_ref, r2_ref, depth_ref, share_ref, band_ref, chl_ref):
+    patches, cols, levels = a_ref.shape
+    flat = (patches * cols, levels)
+    whole = (patches, cols, levels)
+
+    def one(s, carry):
         wet = wet_of(depth_ref[0, s], (cols, levels))
         warm = jnp.exp(heating_speed * t2_ref[s])
-        up = half_rise(r2_ref[s])
         a = a_ref[s]
-        change = warm * b_ref[s] + share_ref[0] * n_ref[s] + transport(up, a)
+        change = warm * b_ref[s] + share_ref[0] * g_ref[s] + transport(half_rise(r2_ref[s]), a)
         chl_ref[s] = softplus(wet * (a + step_tracer * change))
         return carry
 
-    lax.fori_loop(0, patches, third, 0)
+    lax.fori_loop(0, patches, one, 0, unroll=4)
     chl = chl_ref[...].reshape(flat)
-    absorbed, _ = light(chl, level_sums(chl, prefix), level_of(flat))
+    absorbed, _ = light(chl, level_sums(chl, level_matrix(levels, "prefix")), level_of(flat))
+    wet = wet_of(depth_ref[0], whole)
     for band in range(2):
-        absorbed_ref[:, band] = wet * absorbed[band].reshape(whole)
-
-
-def last_heat_kernel(sc, t_ref, north_ref, south_ref, east_ref, west_ref, face_ref, depth_ref, heat_ref, rise_ref, out_ref):
+        band_ref[:, band] = wet * absorbed[band].reshape(whole)
+
+
+def last_ocean_kernel(
+    sc, speed_ref, t_ref, north_ref, south_ref, east_ref, west_ref, depth_ref, heat_ref, out_ref, div_ref
+):
     rows, cols, levels = t_ref.shape
     place = lax.broadcasted_iota(jnp.int32, (cols, levels), 0)
+    sources = (speed_ref.at[0], speed_ref.at[1], t_ref)
     for y in range(rows):
         wet = [wet_of(depth_ref[i, y], (cols, levels)) for i in range(5)]
-        t = t_ref[y]
-        e = jnp.where(place == cols - 1, east_ref[pl.ds(y, 1)], pltpu.roll(t, cols - 1, 0))
-        w = jnp.where(place == 0, west_ref[pl.ds(y, 1)], pltpu.roll(t, 1, 0))
-        n = t_ref[y + 1] if y < rows - 1 else north_ref[...]
-        s = t_ref[y - 1] if y > 0 else south_ref[...]
+
+        def east_of(f):
+            return jnp.where(place == cols - 1, east_ref[f, pl.ds(y, 1)], pltpu.roll(sources[f][y], cols - 1, 0))
+
+        def west_of(f):
+            return jnp.where(place == 0, west_ref[f, pl.ds(y, 1)], pltpu.roll(sources[f][y], 1, 0))
+
+        def north_of(f):
+            return sources[f][y + 1] if y < rows - 1 else north_ref[f]
+
+        def south_of(f):
+            return sources[f][y - 1] if y > 0 else south_ref[f]
+
+        u, v, t = (ref[y] for ref in sources)
+        own = 0.5 * wet[0]
+        east = (u + east_of(0)) * (own * wet[1])
+        west = (west_of(0) + u) * (own * wet[2])
+        north = (v + north_of(1)) * (own * wet[3])
+        south = (south_of(1) + v) * (own * wet[4])
+        div_ref[y] = east - west + north - south
+        e, w, n, s = east_of(2), west_of(2), north_of(2), south_of(2)
         spread = wet[1] * (e - t) + wet[2] * (w - t) + wet[3] * (n - t) + wet[4] * (s - t)
-        carry_along = 0.5 * (
-            face_ref[0, y] * (t + e) - face_ref[1, y] * (w + t) + face_ref[2, y] * (t + n) - face_ref[3, y] * (s + t)
-        )
-        owner = sc[1 + y]
-        out_ref[owner, 0] = rise_ref[y]
-        out_ref[owner, 1] = wet[0] * (t + advance_marine * (spreading * spread - carry_along)) + heat_ref[y]
+        carry_along = 0.5 * (east * (t + e) - west * (w + t) + north * (t + n) - south * (s + t))
+        change = spreading * spread - carry_along
+        out_ref[sc[1 + y], 1] = wet[0] * (t + advance_marine * change) + heat_ref[y]
+    sums = level_sums(div_ref[...].reshape(rows * cols, levels), level_matrix(levels, "below"))
+    div_ref[...] = -sums.reshape(rows, cols, levels)
+    for y in range(rows):
+        out_ref[sc[1 + y], 0] = div_ref[y]
 
 
 def join_kernel(sc, absorbed_ref, flux_ref, other_ref, out_ref):
@@ -417,8 +516,7 @@
     rest = pl.multiple_of((1 - sc[0]) * half, half)
     for s in range(patches):
         for f in range(2):
-            mine = jnp.where(first, absorbed_ref[s, f], flux_ref[s, f])
-            out_ref[f, s, pl.ds(own, half)] = mine
+            out_ref[f, s, pl.ds(own, half)] = jnp.where(first, absorbed_ref[s, f], flux_ref[s, f])
             out_ref[f, s, pl.ds(rest, half)] = other_ref[s, f]
 
 
@@ -428,8 +526,8 @@
         grid_spec=pltpu.PrefetchScalarGridSpec(
             num_scalar_prefetch=1,
             grid=(1,),
-            in_specs=specs,
-            out_specs=[VMEM] * len(outs),
+            in_specs=[spec or whole(a) for spec, a in zip(specs, args)],
+            out_specs=[whole(o) for o in outs],
             scratch_shapes=[pltpu.VMEM(s, jnp.float32) for s in scratch],
         ),
         out_shape=outs,
@@ -459,6 +557,10 @@
     east = lax.ppermute(low, ("comp", "px"), [(b, a) for a, b in ahead])
     west = lax.ppermute(high, ("comp", "px"), ahead)
     return east, west
+
+
+def to_owners(blocks):
+    return lax.all_to_all(blocks, ("py", "px"), split_axis=0, concat_axis=0, tiled=True)
 
 
 def swap(block):
@@ -621,14 +723,8 @@
         )
         return out.reshape(1, 2, 1, columns, levels)
 
-    absorb = linked[0] + linked[1]
-    sent = jnp.where(
-        first, jnp.stack([absorb[:, :half], absorb[:, half:]]), linked[:, :, :half]
-    )
+    sent, *edges = pack(comp, linked, current_speeds, thermal_anomaly)
     got = swap(sent)
-    start = jnp.stack([u0, v0, thermal_anomaly])
-    halos0 = exchange_rows(start[:, 0], start[:, -1]) + exchange_cols(start[:, :, 0], start[:, :, -1])
-
     times = functools.partial(jnp.dot, precision=lax.Precision.HIGHEST)
     unit = (jnp.arange(fields) == 0).astype(jnp.float32)
     chain = [jnp.stack([chroma_loading, unit])]
@@ -638,43 +734,48 @@
     shares = times(weights, photic_absorb_share)
 
     projected, g = project(comp, tracers, weights, tracer_depth)
+    edges, projected, g = lax.optimization_barrier((edges, projected, g))
+    halos0 = exchange_rows(edges[0], edges[1]) + exchange_cols(edges[2], edges[3])
     kept = first_tracer(comp, projected, g, got, linked, tracer_depth, shares)
-    arrived = lax.all_to_all(kept, ("py", "px"), split_axis=0, concat_axis=0, tiled=True)
-
-    u1, v1, t1, r1, *edges = ocean(1, comp, coriolis, (u0, v0, thermal_anomaly), halos0, depth, linked, got)
+    kept, halos0 = lax.optimization_barrier((kept, halos0))
+    arrived = to_owners(kept)
+
+    speeds1, t1, r1, *edges = ocean(1, comp, coriolis, current_speeds, thermal_anomaly, halos0, depth, linked, got)
     halos1 = exchange_rows(edges[0], edges[1]) + exchange_cols(edges[2], edges[3])
-    u2, v2, t2, r2, *edges = ocean(2, comp, coriolis, (u1, v1, t1), halos1, depth)
-    halos2 = exchange_rows(edges[0], edges[1]) + exchange_cols(edges[2], edges[3])
-    faces, r3 = ocean(3, comp, coriolis, (u2, v2, t2), halos2, depth)
+    speeds2, t2, r2 = ocean(2, comp, coriolis, speeds1, t1, halos1, depth)
+    arrived, speeds2, t2 = lax.optimization_barrier((arrived, speeds2, t2))
 
     patch_half = half_spec((CY,), half, levels)
+    speeds_half = half_spec((2, CY), half, levels)
     depth_half = pl.BlockSpec((5, CY, half, 1), lambda i, c: (0, 0, c[0], 0))
     piece = shape_of(CY, half, levels)
-    line = shape_of(half, levels)
-    side = shape_of(CY, levels)
-
-    def absorb_step(sc, y_ref, t_ref, depth_ref, *rest):
-        absorb_kernel(sc, y_ref, t_ref, *rest[:6], depth_ref, rest[6])
+    scratch = (CY, half, levels)
+    line = shape_of(3, half, levels)
+    side = shape_of(3, CY, levels)
 
     t2, irr1, *edges = call(
-        absorb_step, comp, (arrived, t2, depth), [VMEM, patch_half, depth_half],
-        (piece, piece, line, line, side, side), [(CY, half, levels)], "absorb",
-    )
-    halo = exchange_rows(edges[0], edges[1]) + exchange_half_cols(edges[2], edges[3])
-    heat, absorbed = call(
-        two_steps_kernel, comp, (arrived, t2, irr1, t1, r1, r2, depth, shares),
-        [VMEM, VMEM, VMEM, patch_half, patch_half, patch_half, depth_half, SMEM],
-        (piece, shape_of(CY, 2, half, levels)), [(CY, half, levels)] * 4, "two_steps",
+        absorb_kernel, comp, (arrived, t2, speeds2, depth), [None, patch_half, speeds_half, depth_half],
+        (piece, piece, line, line, side, side), [scratch], "absorb",
+    )
+    halos2 = exchange_rows(edges[0], edges[1]) + exchange_half_cols(edges[2], edges[3])
+    heat, a, b, g = call(
+        second_kernel, comp, (arrived, irr1, t1, r1, depth, shares),
+        [None, None, patch_half, patch_half, depth_half, SMEM],
+        (piece,) * 4, [scratch] * 2, "second",
     )
     [back] = call(
-        last_heat_kernel, comp, (t2, *halo, faces, depth, heat, r3),
-        [VMEM] * 5 + [half_spec((4, CY), half, levels), depth_half, VMEM, patch_half],
-        (shape_of(patches, 2, half, levels),), (), "last_heat",
-    )
-    flux = lax.all_to_all(back, ("py", "px"), split_axis=0, concat_axis=0, tiled=True)
+        last_ocean_kernel, comp, (speeds2, t2, *halos2, depth, heat),
+        [speeds_half] + [None] * 5 + [depth_half, None],
+        (shape_of(patches, 2, half, levels),), [scratch], "last_ocean",
+    )
+    flux = to_owners(back)
+    [absorbed] = call(
+        third_kernel, comp, (a, b, g, t2, r2, depth, shares),
+        [None] * 4 + [patch_half, depth_half, SMEM], (shape_of(CY, 2, half, levels),), [scratch], "third",
+    )
     other = swap(jnp.where(first, flux, absorbed))
     [out] = call(
-        join_kernel, comp, (absorbed, flux, other), [VMEM] * 3, (shape_of(2, patches, strip, levels),), (), "join"
+        join_kernel, comp, (absorbed, flux, other), [None] * 3, (shape_of(2, patches, strip, levels),), (), "join"
     )
     return out.reshape(1, 2, 1, columns, levels)
 

time: 160 us -> 134 us (0.84)
  blocking collectives: 17.2 us -> 0 us
  starting transfers between devices: 51.9 us -> 43.1 us
  local copies, waits for them, and re-layouts: 18.2 us -> 16.4 us
    all_to_all x1 -> x0, blocking collectives: 17.2 us -> none  [shards(): lax.all_to_all(back, ('py', 'px'), split_axis=0, concat_axis=0, tiled=True)]
    all_to_all x1 -> x2, waiting for transfers between devices: 0.01 us -> 10.7 us  [to_owners(): lax.all_to_all(blocks, ('py', 'px'), split_axis=0, concat_axis=0, tiled=T...]
    ppermute x3 -> x2, waiting for transfers between devices: 10.5 us -> 2.9 us  [exchange_cols(): east = lax.ppermute(low, 'px', [((i + 1) % count, i) for i in range(count)])]
    ppermute x3 -> x2, starting transfers between devices: 7.17 us -> 0.01 us  [exchange_cols(): lax.ppermute(high, 'px', [(i, (i + 1) % count) for i in range(count)])]
    all_to_all x1 -> x2, starting transfers between devices: 7.46 us -> 14.2 us  [to_owners(): lax.all_to_all(blocks, ('py', 'px'), split_axis=0, concat_axis=0, tiled=T...]
    ppermute x1, starting transfers between devices: 3.81 us -> 0.06 us  [exchange_half_cols(): east = lax.ppermute(low, ('comp', 'px'), [(b, a) for a, b in ahead])]
    unnamed x58 -> x74, local copies, waits for them, and re-layouts: 15.9 us -> 12.1 us
    pallas_call x4 -> x5, Pallas kernels: 13.7 us -> 10 us  [call(): pl.pallas_call(kernel, grid_spec=pltpu.PrefetchScalarGridSpec(num_scalar_...]
  transfers between devices with their start and end apart: 19 -> 16, of which waited for: 6 -> 5; matrix products, arithmetic and copies ran while one was open for 4% -> 4% of each run, Pallas kernels for 19% -> 23%
where the time goes in v1:
time: 134 us; the launch traced here: 131 us
  starting transfers between devices  43.1 us (32%)
  Pallas kernels  39 us (29%)
  waiting for transfers between devices  29.6 us (22%)
  local copies, waits for them, and re-layouts  16.4 us (12%)
  other arithmetic  1.57 us (1%)
    all_to_all x2, starting transfers between devices, to_owners(): lax.all_to_all(blocks, ('py', 'px'), split_axis=0, concat_axis=0, tiled=T...  14.2 us
    pallas_call x2, Pallas kernels, ocean(): pl.pallas_call(functools.partial(ocean_kernel, advance), grid_spec=pltpu....  13.8 us
    unnamed x74, local copies, waits for them, and re-layouts  12.1 us
    ppermute x2, waiting for transfers between devices, swap(): return lax.ppermute(block, 'comp', [(0, 1), (1, 0)])  11.4 us
    all_to_all x2, waiting for transfers between devices, to_owners(): lax.all_to_all(blocks, ('py', 'px'), split_axis=0, concat_axis=0, tiled=T...  10.7 us
    pallas_call x5, Pallas kernels, call(): pl.pallas_call(kernel, grid_spec=pltpu.PrefetchScalarGridSpec(num_scalar_...  10 us
    ppermute x3, starting transfers between devices, exchange_rows(): south = lax.ppermute(high, 'py', [(i, i + 1) for i in range(count - 1)])  9.58 us
    ppermute x3, starting transfers between devices, exchange_rows(): north = lax.ppermute(low, 'py', [(i + 1, i) for i in range(count - 1)])  7.93 us
  transfers between devices with their start and end apart: 16, of which 5 were waited for; matrix products, arithmetic and copies ran while one was open for 4% of the time, Pallas kernels for 23%

profile of v1, /device:TPU:1, one launch (start us, length us, event | category | flops | bytes accessed | tf_op | source)
XLA Modules:
  0.0 131.0 jit_solution(4765944978836310067)
XLA Ops:
  1.4 3.2 %pack.1 = (f32[2,16,16,256]{3,2,1,0:T(8,128)}, f32[3,32,256]{2,1,0:T(8,128)}, f32[3,32,256]{2,1,0:T(8,128)}, f32[3,16,256]{2,1,0:T(8,128)}, f32[3,16,256]{2,1,0:T(8,128)}) custom-call(s32[17]{0:T(128)} %pad_add_fusion.1.sc, f32[2,16,32,256]{3,2,1,0:T(8,128)} %bitcast.48, f32[2,16,32,256]{3,2,1,0:T(8,128)} %speed_ref.1, f32[2,16,32,256]{3,2,1,0:T(8,128)} %speed_ref.1, ...), custom_call_target="tpu_custom_call" | custom-call | tf_op jit(solution)/shard_map/pack/pallas_call | solution.py:236
  4.6 2.0 %collective-permute-start = (f32[2,16,16,256]{3,2,1,0:T(8,128)}, f32[2,16,16,256]{3,2,1,0:T(8,128)S(1)}, u32[]{:S(2)}, u32[]{:S(2)}) collective-permute-start(f32[2,16,16,256]{3,2,1,0:T(8,128)} %get-tuple-element.54), channel_id=1, source_target_pairs={{0,16},{16,0},{1,17},{17,1},{2,18},{18,2},{3,19},{19,3},{4,20},{20... | collective-permute-start | bytes 1572872 | tf_op jit(solution)/shard_map/ppermute | solution.py:567
  9.0 6.7 %project.1 = (f32[7,16,16,256]{3,2,1,0:T(8,128)}, f32[16,16,256]{2,1,0:T(8,128)}) custom-call(s32[17]{0:T(128)} %pad_add_fusion.1.sc, f32[16,16,32,256]{3,2,1,0:T(8,128)} %bitcast.51, f32[7,16]{1,0:T(8,128)} %stack.30.w_ref, s32[16,16,1]{2,1,0:T(8,128)} %copy.14.depth_ref), custom_call_target="tpu_custom_call" | custom-call | tf_op jit(solution)/shard_map/project/pallas_call | solution.py:130
  15.8 3.4 %collective-permute-start.3 = (f32[3,16,256]{2,1,0:T(8,128)S(1)}, f32[3,16,256]{2,1,0:T(8,128)S(1)}, u32[]{:S(2)}, u32[]{:S(2)}) collective-permute-start(f32[3,16,256]{2,1,0:T(8,128)S(1)} %copy-done.34), channel_id=1, source_target_pairs={{1,0},{2,1},{3,2},{0,3},{5,4},{6,5},{7,6},{4,7},{9,8},{10,9},{11,1... | collective-permute-start | bytes 147464 | tf_op jit(solution)/shard_map/ppermute | solution.py:548
  19.1 3.1 %collective-permute-start.1 = (f32[3,32,256]{2,1,0:T(8,128)S(1)}, f32[3,32,256]{2,1,0:T(8,128)S(1)}, u32[]{:S(2)}, u32[]{:S(2)}) collective-permute-start(f32[3,32,256]{2,1,0:T(8,128)S(1)} %copy-done.32), channel_id=1, source_target_pairs={{4,0},{8,4},{12,8},{5,1},{9,5},{13,9},{6,2},{10,6},{14,10},{7,3},{... | collective-permute-start | bytes 294920 | tf_op jit(solution)/shard_map/ppermute | solution.py:541
  22.3 3.0 %collective-permute-start.2 = (f32[3,32,256]{2,1,0:T(8,128)S(1)}, f32[3,32,256]{2,1,0:T(8,128)S(1)}, u32[]{:S(2)}, u32[]{:S(2)}) collective-permute-start(f32[3,32,256]{2,1,0:T(8,128)S(1)} %copy-done.31), channel_id=1, source_target_pairs={{0,4},{4,8},{8,12},{1,5},{5,9},{9,13},{2,6},{6,10},{10,14},{3,7},{... | collective-permute-start | bytes 294920 | tf_op jit(solution)/shard_map/ppermute | solution.py:542
  26.8 5.3 %first_tracer.1 = f32[16,5,16,256]{3,2,1,0:T(8,128)} custom-call(s32[17]{0:T(128)} %pad_add_fusion.1.sc, f32[7,16,16,256]{3,2,1,0:T(8,128)} %get-tuple-element.52.y_ref, f32[16,16,256]{2,1,0:T(8,128)} %get-tuple-element.53.g_ref, f32[2,16,16,256]{3,2,1,0:T(8,128)} %copy-done.20, f32[2,16,32,256]{3,2,1,0:T(8,128)} %bitcast.49, s32[16,16,1]{2,1,0:T(8,128)} %copy.14.depth_ref, ...), custom_call_target="tpu_custom_call" | custom-call | tf_op jit(solution)/shard_map/first_tracer/pallas_call | solution.py:180
  32.8 5.4 %all-to-all-start = ((f32[16,5,16,256]{3,2,1,0:T(8,128)}), f32[16,5,16,256]{3,2,1,0:T(8,128)S(1)}, u32[]{:S(2)}, u32[]{:S(2)}) async-start(f32[16,5,16,256]{3,2,1,0:T(8,128)} %first_tracer.1), calls=%async_computation | async-start | bytes 2621440 | tf_op jit(solution)/shard_map/all_to_all | solution.py:563
  38.8 1.6 %copy.16.depth_ref = s32[5,16,32,1]{3,2,1,0:T(8,128)} copy(s32[5,16,32,1]{2,1,0,3:T(8,128)S(1)} %bitcast.52) | data formatting | bytes 20480 | tf_op jit(solution)/shard_map/broadcast_in_dim | solution.py:707
  41.1 8.5 %ocean1.1 = (f32[2,16,32,256]{3,2,1,0:T(8,128)}, f32[16,32,256]{2,1,0:T(8,128)}, f32[16,32,256]{2,1,0:T(8,128)}, f32[3,32,256]{2,1,0:T(8,128)}, f32[3,32,256]{2,...) custom-call(s32[17]{0:T(128)} %pad_add_fusion.1.sc, f32[16]{0:T(128)} %multiply_add_fusion.coriolis_ref, ...), custom_call_target="tpu_custom_call" | custom-call | tf_op jit(solution)/shard_map/ocean1/pallas_call | solution.py:383
  49.5 2.0 %collective-permute-start.5 = (f32[3,32,256]{2,1,0:T(8,128)}, f32[3,32,256]{2,1,0:T(8,128)S(1)}, u32[]{:S(2)}, u32[]{:S(2)}) collective-permute-start(f32[3,32,256]{2,1,0:T(8,128)} %get-tuple-element.66), channel_id=1, source_target_pairs={{4,0},{8,4},{12,8},{5,1},{9,5},{13,9},{6,2},{10,6},{14,10},{7,3},{... | collective-permute-start | bytes 294920 | tf_op jit(solution)/shard_map/ppermute | solution.py:541
  51.5 3.5 %collective-permute-start.6 = (f32[3,32,256]{2,1,0:T(8,128)}, f32[3,32,256]{2,1,0:T(8,128)S(1)}, u32[]{:S(2)}, u32[]{:S(2)}) collective-permute-start(f32[3,32,256]{2,1,0:T(8,128)} %get-tuple-element.67), channel_id=1, source_target_pairs={{0,4},{4,8},{8,12},{1,5},{5,9},{9,13},{2,6},{6,10},{10,14},{3,7},{... | collective-permute-start | bytes 294920 | tf_op jit(solution)/shard_map/ppermute | solution.py:542
  55.1 3.2 %collective-permute-start.7 = (f32[3,16,256]{2,1,0:T(8,128)}, f32[3,16,256]{2,1,0:T(8,128)S(1)}, u32[]{:S(2)}, u32[]{:S(2)}) collective-permute-start(f32[3,16,256]{2,1,0:T(8,128)} %get-tuple-element.68), channel_id=1, source_target_pairs={{1,0},{2,1},{3,2},{0,3},{5,4},{6,5},{7,6},{4,7},{9,8},{10,9},{11,1... | collective-permute-start | bytes 147464 | tf_op jit(solution)/shard_map/ppermute | solution.py:548
  58.3 2.9 %collective-permute-done.7.east_ref = f32[3,16,256]{2,1,0:T(8,128)S(1)} collective-permute-done((f32[3,16,256]{2,1,0:T(8,128)}, f32[3,16,256]{2,1,0:T(8,128)S(1)}, u32[]{:S(2)}, u32[]{:S(2)}) %collective-permute-start.7) | collective-permute-done | bytes 49184 | tf_op jit(solution)/shard_map/ppermute | solution.py:548
  61.2 4.4 %collective-permute-done.8.west_ref = f32[3,16,256]{2,1,0:T(8,128)S(1)} collective-permute-done((f32[3,16,256]{2,1,0:T(8,128)}, f32[3,16,256]{2,1,0:T(8,128)S(1)}, u32[]{:S(2)}, u32[]{:S(2)}) %collective-permute-start.8) | collective-permute-done | bytes 49184 | tf_op jit(solution)/shard_map/ppermute | solution.py:549
  65.6 1.0 copy-done.5
  66.7 1.2 copy-done.7
  67.9 5.3 %ocean2.1 = (f32[2,16,32,256]{3,2,1,0:T(8,128)S(1)}, f32[16,32,256]{2,1,0:T(8,128)S(1)}, f32[16,32,256]{2,1,0:T(8,128)S(1)}) custom-call(s32[17]{0:T(128)S(1)} %copy-done.17, f32[16]{0:T(128)S(1)} %copy-done.19, f32[2,16,32,256]{3,2,1,0:T(8,128)S(1)} %copy-done.7, f32[16,32,256]{2,1,0:T(8,128)S(1)} %copy-done.5, ...), custom_call_target="tpu_custom_call" | custom-call | tf_op jit(solution)/shard_map/ocean2/pallas_call | solution.py:383
  75.0 1.2 copy-done.3
  76.2 1.0 copy-done.10
  77.2 1.3 %absorb.1 = (f32[16,16,256]{2,1,0:T(8,128)S(1)}, f32[16,16,256]{2,1,0:T(8,128)S(1)}, f32[3,16,256]{2,1,0:T(8,128)S(1)}, f32[3,16,256]{2,1,0:T(8,128)S(1)}, f32[3...) custom-call(s32[17]{0:T(128)S(1)} %copy-done.17, f32[16,5,16,256]{3,2,1,0:T(8,128)S(1)} %all-to-all-done.y_ref, ...), custom_call_target="tpu_custom_call" | custom-call | tf_op jit(solution)/shard_map/absorb/pallas_call | solution.py:524
  78.6 2.8 %collective-permute-start.9 = (f32[3,16,256]{2,1,0:T(8,128)S(1)}, f32[3,16,256]{2,1,0:T(8,128)S(1)}, u32[]{:S(2)}, u32[]{:S(2)}) collective-permute-start(f32[3,16,256]{2,1,0:T(8,128)S(1)} %get-tuple-element.82), channel_id=1, source_target_pairs={{4,0},{8,4},{12,8},{5,1},{9,5},{13,9},{6,2},{10,6},{14,10},{7,3},{... | collective-permute-start | bytes 147464 | tf_op jit(solution)/shard_map/ppermute | solution.py:541
  81.4 3.0 %collective-permute-start.10 = (f32[3,16,256]{2,1,0:T(8,128)S(1)}, f32[3,16,256]{2,1,0:T(8,128)S(1)}, u32[]{:S(2)}, u32[]{:S(2)}) collective-permute-start(f32[3,16,256]{2,1,0:T(8,128)S(1)} %get-tuple-element.83), channel_id=1, source_target_pairs={{0,4},{4,8},{8,12},{1,5},{5,9},{9,13},{2,6},{6,10},{10,14},{3,7},{... | collective-permute-start | bytes 147464 | tf_op jit(solution)/shard_map/ppermute | solution.py:542
  84.4 1.5 %collective-permute-start.12 = (f32[3,16,256]{2,1,0:T(8,128)S(1)}, f32[3,16,256]{2,1,0:T(8,128)S(1)}, u32[]{:S(2)}, u32[]{:S(2)}) collective-permute-start(f32[3,16,256]{2,1,0:T(8,128)S(1)} %get-tuple-element.85), channel_id=1, source_target_pairs={{0,16},{16,1},{1,17},{17,2},{2,18},{18,3},{3,19},{19,0},{4,20},{20... | collective-permute-start | bytes 147464 | tf_op jit(solution)/shard_map/ppermute | solution.py:558
  85.9 2.6 %second.1 = (f32[16,16,256]{2,1,0:T(8,128)S(1)}, f32[16,16,256]{2,1,0:T(8,128)S(1)}, f32[16,16,256]{2,1,0:T(8,128)S(1)}, f32[16,16,256]{2,1,0:T(8,128)S(1)}) custom-call(s32[17]{0:T(128)S(1)} %copy-done.17, f32[16,5,16,256]{3,2,1,0:T(8,128)S(1)} %all-to-all-done.y_ref, f32[16,16,256]{2,1,0:T(8,128)S(1)} %get-tuple-element.75.irr_ref, ...), custom_call_target="tpu_custom_call" | custom-call | tf_op jit(solution)/shard_map/second/pallas_call | solution.py:524
  90.7 2.2 %last_ocean.1 = f32[16,2,16,256]{3,2,1,0:T(8,128)} custom-call(s32[17]{0:T(128)S(1)} %copy-done.17, f32[2,16,32,256]{3,2,1,0:T(8,128)S(1)} %copy-done.4, f32[16,16,256]{2,1,0:T(8,128)S(1)} %get-tuple-element.80.t2_ref.t_ref, f32[3,16,256]{2,1,0:T(8,128)S(1)} %collective-permute-done.9.north_ref, f32[3,16,256]{2,1,0:T(8,128)S(1)} %collective-permute-done.10.south_ref, ...), custom_call_target="tpu_custom_call" | custom-call | tf_op jit(solution)/shard_map/last_ocean/pallas_call | solution.py:524
  92.9 8.8 %all-to-all-start.1 = ((f32[16,2,16,256]{3,2,1,0:T(8,128)}), f32[16,2,16,256]{3,2,1,0:T(8,128)S(1)}, u32[]{:S(2)}, u32[]{:S(2)}) async-start(f32[16,2,16,256]{3,2,1,0:T(8,128)} %last_ocean.1), calls=%async_computation.1 | async-start | bytes 1048576 | tf_op jit(solution)/shard_map/all_to_all | solution.py:563
  103.6 2.3 %third.1.absorbed_ref = f32[16,2,16,256]{3,2,1,0:T(8,128)S(1)} custom-call(s32[17]{0:T(128)S(1)} %copy-done.17, f32[16,16,256]{2,1,0:T(8,128)S(1)} %copy-done.12, f32[16,16,256]{2,1,0:T(8,128)S(1)} %copy-done.14, f32[16,16,256]{2,1,0:T(8,128)S(1)} %copy-done.16, f32[16,16,256]{2,1,0:T(8,128)S(1)} %get-tuple-element.80.t2_ref.t_ref, ...), custom_call_target="tpu_custom_call" | custom-call | tf_op jit(solution)/shard_map/third/pallas_call | solution.py:524
  105.9 10.7 %all-to-all-done.1.flux_ref = f32[16,2,16,256]{3,2,1,0:T(8,128)S(1)} async-done(((f32[16,2,16,256]{3,2,1,0:T(8,128)}), f32[16,2,16,256]{3,2,1,0:T(8,128)S(1)}, u32[]{:S(2)}, u32[]{:S(2)}) %all-to-all-start.1) | async-done | bytes 524320 | tf_op jit(solution)/shard_map/all_to_all | solution.py:563
  116.8 1.2 collective-permute-start.13
  118.0 11.4 %collective-permute-done.13.other_ref = f32[16,2,16,256]{3,2,1,0:T(8,128)S(1)} collective-permute-done((f32[16,2,16,256]{3,2,1,0:T(8,128)S(1)}, f32[16,2,16,256]{3,2,1,0:T(8,128)S(1)}, u32[]{:S(2)}, u32[]{:S(2)}) %collective-permute-start.13) | collective-permute-done | bytes 524320 | tf_op jit(solution)/shard_map/ppermute | solution.py:567
  129.5 1.6 %join.1 = f32[2,16,32,256]{3,2,1,0:T(8,128)} custom-call(s32[17]{0:T(128)S(1)} %copy-done.17, f32[16,2,16,256]{3,2,1,0:T(8,128)S(1)} %third.1.absorbed_ref, f32[16,2,16,256]{3,2,1,0:T(8,128)S(1)} %all-to-all-done.1.flux_ref, f32[16,2,16,256]{3,2,1,0:T(8,128)S(1)} %collective-permute-done.13.other_ref), custom_call_target="tpu_custom_call" | custom-call | tf_op jit(solution)/shard_map/join/pallas_call | solution.py:524
  (106 shorter events, 13.0 us)
Async XLA Ops:
  0.0 6.7 %copy-start = (f32[16,16]{1,0:T(8,128)S(1)}, f32[16,16]{1,0:T(8,128)}, u32[]{:S(2)}) copy-start(f32[16,16]{1,0:T(8,128)} %param.17) | copy-start | bytes 3076
  1.4 5.7 %copy-start.26 = (s32[64,128]{1,0:T(8,128)S(1)}, s32[64,128]{1,0:T(8,128)}, u32[]{:S(2)}) copy-start(s32[64,128]{1,0:T(8,128)} %param.14) | copy-start | bytes 98308
  1.4 5.7 %copy-start.27 = (s32[64,128]{1,0:T(8,128)S(1)}, s32[64,128]{1,0:T(8,128)}, u32[]{:S(2)}) copy-start(s32[64,128]{1,0:T(8,128)} %param.15) | copy-start | bytes 98308
  4.6 21.4 %collective-permute-start = (f32[2,16,16,256]{3,2,1,0:T(8,128)}, f32[2,16,16,256]{3,2,1,0:T(8,128)S(1)}, u32[]{:S(2)}, u32[]{:S(2)}) collective-permute-start(f32[2,16,16,256]{3,2,1,0:T(8,128)} %get-tuple-element.54), channel_id=1, source_target_pairs={{0,16},{16,0},{1,17},{17,1},{2,18},{18,2},{3,19},{19,3},{4,20},{20... | collective-permute-start | bytes 1572872 | tf_op jit(solution)/shard_map/ppermute | solution.py:567
  9.0 6.8 %copy-start.34 = (f32[3,16,256]{2,1,0:T(8,128)S(1)}, f32[3,16,256]{2,1,0:T(8,128)}, u32[]{:S(2)}) copy-start(f32[3,16,256]{2,1,0:T(8,128)} %get-tuple-element.57) | copy-start | bytes 147460
  9.0 10.1 %copy-start.33 = (f32[3,16,256]{2,1,0:T(8,128)S(1)}, f32[3,16,256]{2,1,0:T(8,128)}, u32[]{:S(2)}) copy-start(f32[3,16,256]{2,1,0:T(8,128)} %get-tuple-element.58) | copy-start | bytes 147460
  9.0 10.1 %copy-start.32 = (f32[3,32,256]{2,1,0:T(8,128)S(1)}, f32[3,32,256]{2,1,0:T(8,128)}, u32[]{:S(2)}) copy-start(f32[3,32,256]{2,1,0:T(8,128)} %get-tuple-element.55) | copy-start | bytes 294916
  9.0 13.3 %copy-start.31 = (f32[3,32,256]{2,1,0:T(8,128)S(1)}, f32[3,32,256]{2,1,0:T(8,128)}, u32[]{:S(2)}) copy-start(f32[3,32,256]{2,1,0:T(8,128)} %get-tuple-element.56) | copy-start | bytes 294916
  9.0 16.3 %copy-start.25 = (f32[7,16]{1,0:T(8,128)S(1)}, f32[7,16]{1,0:T(8,128)}, u32[]{:S(2)}) copy-start(f32[7,16]{1,0:T(8,128)} %stack.30.w_ref) | copy-start | bytes 1348
  9.0 16.3 %copy-start.30 = (f32[16]{0:T(128)S(1)}, f32[16]{0:T(128)}, u32[]{:S(2)}) copy-start(f32[16]{0:T(128)} %param.18) | copy-start | bytes 196
  15.8 16.3 %collective-permute-start.3 = (f32[3,16,256]{2,1,0:T(8,128)S(1)}, f32[3,16,256]{2,1,0:T(8,128)S(1)}, u32[]{:S(2)}, u32[]{:S(2)}) collective-permute-start(f32[3,16,256]{2,1,0:T(8,128)S(1)} %copy-done.34), channel_id=1, source_target_pairs={{1,0},{2,1},{3,2},{0,3},{5,4},{6,5},{7,6},{4,7},{9,8},{10,9},{11,1... | collective-permute-start | bytes 147464 | tf_op jit(solution)/shard_map/ppermute | solution.py:548
  19.1 12.9 %collective-permute-start.4 = (f32[3,16,256]{2,1,0:T(8,128)S(1)}, f32[3,16,256]{2,1,0:T(8,128)S(1)}, u32[]{:S(2)}, u32[]{:S(2)}) collective-permute-start(f32[3,16,256]{2,1,0:T(8,128)S(1)} %copy-done.33), channel_id=1, source_target_pairs={{0,1},{1,2},{2,3},{3,0},{4,5},{5,6},{6,7},{7,4},{8,9},{9,10},{10,1... | collective-permute-start | bytes 147464 | tf_op jit(solution)/shard_map/ppermute | solution.py:549
  19.1 13.0 %collective-permute-start.1 = (f32[3,32,256]{2,1,0:T(8,128)S(1)}, f32[3,32,256]{2,1,0:T(8,128)S(1)}, u32[]{:S(2)}, u32[]{:S(2)}) collective-permute-start(f32[3,32,256]{2,1,0:T(8,128)S(1)} %copy-done.32), channel_id=1, source_target_pairs={{4,0},{8,4},{12,8},{5,1},{9,5},{13,9},{6,2},{10,6},{14,10},{7,3},{... | collective-permute-start | bytes 294920 | tf_op jit(solution)/shard_map/ppermute | solution.py:541
  22.3 9.8 %collective-permute-start.2 = (f32[3,32,256]{2,1,0:T(8,128)S(1)}, f32[3,32,256]{2,1,0:T(8,128)S(1)}, u32[]{:S(2)}, u32[]{:S(2)}) collective-permute-start(f32[3,32,256]{2,1,0:T(8,128)S(1)} %copy-done.31), channel_id=1, source_target_pairs={{0,4},{4,8},{8,12},{1,5},{5,9},{9,13},{2,6},{6,10},{10,14},{3,7},{... | collective-permute-start | bytes 294920 | tf_op jit(solution)/shard_map/ppermute | solution.py:542
  32.8 42.2 %all-to-all-start = ((f32[16,5,16,256]{3,2,1,0:T(8,128)}), f32[16,5,16,256]{3,2,1,0:T(8,128)S(1)}, u32[]{:S(2)}, u32[]{:S(2)}) async-start(f32[16,5,16,256]{3,2,1,0:T(8,128)} %first_tracer.1), calls=%async_computation | async-start | bytes 2621440 | tf_op jit(solution)/shard_map/all_to_all | solution.py:563
  41.0 24.5 %copy-start.1 = (s32[5,16,32,1]{3,2,1,0:T(8,128)S(1)}, s32[5,16,32,1]{3,2,1,0:T(8,128)}, u32[]{:S(2)}) copy-start(s32[5,16,32,1]{3,2,1,0:T(8,128)} %copy.16.depth_ref) | copy-start | bytes 30724
  41.0 24.6 %copy-start.17 = (s32[17]{0:T(128)S(1)}, s32[17]{0:T(128)}, u32[]{:S(2)}) copy-start(s32[17]{0:T(128)} %pad_add_fusion.1.sc) | copy-start | bytes 208
  41.0 24.6 %copy-start.19 = (f32[16]{0:T(128)S(1)}, f32[16]{0:T(128)}, u32[]{:S(2)}) copy-start(f32[16]{0:T(128)} %multiply_add_fusion.coriolis_ref) | copy-start | bytes 196
  49.5 16.1 %collective-permute-start.5 = (f32[3,32,256]{2,1,0:T(8,128)}, f32[3,32,256]{2,1,0:T(8,128)S(1)}, u32[]{:S(2)}, u32[]{:S(2)}) collective-permute-start(f32[3,32,256]{2,1,0:T(8,128)} %get-tuple-element.66), channel_id=1, source_target_pairs={{4,0},{8,4},{12,8},{5,1},{9,5},{13,9},{6,2},{10,6},{14,10},{7,3},{... | collective-permute-start | bytes 294920 | tf_op jit(solution)/shard_map/ppermute | solution.py:541
  51.5 14.0 %collective-permute-start.6 = (f32[3,32,256]{2,1,0:T(8,128)}, f32[3,32,256]{2,1,0:T(8,128)S(1)}, u32[]{:S(2)}, u32[]{:S(2)}) collective-permute-start(f32[3,32,256]{2,1,0:T(8,128)} %get-tuple-element.67), channel_id=1, source_target_pairs={{0,4},{4,8},{8,12},{1,5},{5,9},{9,13},{2,6},{6,10},{10,14},{3,7},{... | collective-permute-start | bytes 294920 | tf_op jit(solution)/shard_map/ppermute | solution.py:542
  55.1 6.1 %collective-permute-start.7 = (f32[3,16,256]{2,1,0:T(8,128)}, f32[3,16,256]{2,1,0:T(8,128)S(1)}, u32[]{:S(2)}, u32[]{:S(2)}) collective-permute-start(f32[3,16,256]{2,1,0:T(8,128)} %get-tuple-element.68), channel_id=1, source_target_pairs={{1,0},{2,1},{3,2},{0,3},{5,4},{6,5},{7,6},{4,7},{9,8},{10,9},{11,1... | collective-permute-start | bytes 147464 | tf_op jit(solution)/shard_map/ppermute | solution.py:548
  58.3 7.3 %collective-permute-start.8 = (f32[3,16,256]{2,1,0:T(8,128)}, f32[3,16,256]{2,1,0:T(8,128)S(1)}, u32[]{:S(2)}, u32[]{:S(2)}) collective-permute-start(f32[3,16,256]{2,1,0:T(8,128)} %get-tuple-element.69), channel_id=1, source_target_pairs={{0,1},{1,2},{2,3},{3,0},{4,5},{5,6},{6,7},{7,4},{8,9},{9,10},{10,1... | collective-permute-start | bytes 147464 | tf_op jit(solution)/shard_map/ppermute | solution.py:549
  77.2 8.7 %copy-start.6 = (f32[16,32,256]{2,1,0:T(8,128)S(1)}, f32[16,32,256]{2,1,0:T(8,128)}, u32[]{:S(2)}) copy-start(f32[16,32,256]{2,1,0:T(8,128)} %get-tuple-element.65.t_ref.t1_ref) | copy-start | bytes 1572868
  77.2 8.7 %copy-start.8 = (f32[16,32,256]{2,1,0:T(8,128)S(1)}, f32[16,32,256]{2,1,0:T(8,128)}, u32[]{:S(2)}) copy-start(f32[16,32,256]{2,1,0:T(8,128)} %get-tuple-element.76.r1_ref) | copy-start | bytes 1572868
  77.2 8.7 %copy-start.18 = (f32[7]{0:T(128)S(1)}, f32[7]{0:T(128)}, u32[]{:S(2)}) copy-start(f32[7]{0:T(128)} %convolution_bitcast_fusion.share_ref) | copy-start | bytes 88
  78.6 12.0 %collective-permute-start.9 = (f32[3,16,256]{2,1,0:T(8,128)S(1)}, f32[3,16,256]{2,1,0:T(8,128)S(1)}, u32[]{:S(2)}, u32[]{:S(2)}) collective-permute-start(f32[3,16,256]{2,1,0:T(8,128)S(1)} %get-tuple-element.82), channel_id=1, source_target_pairs={{4,0},{8,4},{12,8},{5,1},{9,5},{13,9},{6,2},{10,6},{14,10},{7,3},{... | collective-permute-start | bytes 147464 | tf_op jit(solution)/shard_map/ppermute | solution.py:541
  81.4 9.2 %collective-permute-start.10 = (f32[3,16,256]{2,1,0:T(8,128)S(1)}, f32[3,16,256]{2,1,0:T(8,128)S(1)}, u32[]{:S(2)}, u32[]{:S(2)}) collective-permute-start(f32[3,16,256]{2,1,0:T(8,128)S(1)} %get-tuple-element.83), channel_id=1, source_target_pairs={{0,4},{4,8},{8,12},{1,5},{5,9},{9,13},{2,6},{6,10},{10,14},{3,7},{... | collective-permute-start | bytes 147464 | tf_op jit(solution)/shard_map/ppermute | solution.py:542
  84.4 6.2 %collective-permute-start.11 = (f32[3,16,256]{2,1,0:T(8,128)S(1)}, f32[3,16,256]{2,1,0:T(8,128)S(1)}, u32[]{:S(2)}, u32[]{:S(2)}) collective-permute-start(f32[3,16,256]{2,1,0:T(8,128)S(1)} %get-tuple-element.84), channel_id=1, source_target_pairs={{16,0},{1,16},{17,1},{2,17},{18,2},{3,18},{19,3},{0,19},{20,4},{5,... | collective-permute-start | bytes 147464 | tf_op jit(solution)/shard_map/ppermute | solution.py:557
  84.4 6.3 %collective-permute-start.12 = (f32[3,16,256]{2,1,0:T(8,128)S(1)}, f32[3,16,256]{2,1,0:T(8,128)S(1)}, u32[]{:S(2)}, u32[]{:S(2)}) collective-permute-start(f32[3,16,256]{2,1,0:T(8,128)S(1)} %get-tuple-element.85), channel_id=1, source_target_pairs={{0,16},{16,1},{1,17},{17,2},{2,18},{18,3},{3,19},{19,0},{4,20},{20... | collective-permute-start | bytes 147464 | tf_op jit(solution)/shard_map/ppermute | solution.py:558
  90.7 11.0 %copy-start.12 = (f32[16,16,256]{2,1,0:T(8,128)S(1)}, f32[16,16,256]{2,1,0:T(8,128)}, u32[]{:S(2)}) copy-start(f32[16,16,256]{2,1,0:T(8,128)} %copy-done.11) | copy-start | bytes 786436
  92.9 23.8 %all-to-all-start.1 = ((f32[16,2,16,256]{3,2,1,0:T(8,128)}), f32[16,2,16,256]{3,2,1,0:T(8,128)S(1)}, u32[]{:S(2)}, u32[]{:S(2)}) async-start(f32[16,2,16,256]{3,2,1,0:T(8,128)} %last_ocean.1), calls=%async_computation.1 | async-start | bytes 1048576 | tf_op jit(solution)/shard_map/all_to_all | solution.py:563
  116.8 12.7 %collective-permute-start.13 = (f32[16,2,16,256]{3,2,1,0:T(8,128)S(1)}, f32[16,2,16,256]{3,2,1,0:T(8,128)S(1)}, u32[]{:S(2)}, u32[]{:S(2)}) collective-permute-start(f32[16,2,16,256]{3,2,1,0:T(8,128)S(1)} %broadcast_select_fusion), channel_id=1, source_target_pairs={{0,16},{16,0},{1,17},{17,1},{2,18},{18,2},{3,19},{19,3},{4,20},{20... | collective-permute-start | bytes 1572872 | tf_op jit(solution)/shard_map/ppermute | solution.py:567
  (19 other events, 29.1 us)

commit v2 on v1

--- a/solution.py
+++ b/solution.py
@@ -25,6 +25,7 @@
 KEPT = (0, 1, 2, 4, 5)
 SMEM = pl.BlockSpec(memory_space=pltpu.SMEM)
 PARAMS = pltpu.CompilerParams(vmem_limit_bytes=24 * 1024 * 1024)
+PROJECT = pltpu.CompilerParams(vmem_limit_bytes=57 * 1024 * 1024)
 STREAMED = pltpu.CompilerParams(vmem_limit_bytes=60 * 1024 * 1024)
 
 
@@ -144,7 +145,7 @@
             scratch_shapes=[pltpu.VMEM((block, half, levels), jnp.float32)],
         ),
         out_shape=(shape_of(kinds, patches, half, levels), shape_of(patches, half, levels)),
-        compiler_params=STREAMED,
+        compiler_params=PROJECT,
         name="project",
     )(comp, tracers, weights, depth)
 
@@ -193,7 +194,7 @@
             out_specs=pl.BlockSpec((block, len(KEPT), half, levels), lambda i, c: (i, 0, 0, 0)),
         ),
         out_shape=shape_of(patches, len(KEPT), half, levels),
-        compiler_params=STREAMED,
+        compiler_params=PARAMS,
         name="first_tracer",
     )(comp, projected, g, got, linked, depth, shares)
 
@@ -502,25 +503,33 @@
         spread = wet[1] * (e - t) + wet[2] * (w - t) + wet[3] * (n - t) + wet[4] * (s - t)
         carry_along = 0.5 * (east * (t + e) - west * (w + t) + north * (t + n) - south * (s + t))
         change = spreading * spread - carry_along
-        out_ref[sc[1 + y], 1] = wet[0] * (t + advance_marine * change) + heat_ref[y]
+        out_ref[1, sc[1 + y], 1] = wet[0] * (t + advance_marine * change) + heat_ref[y]
     sums = level_sums(div_ref[...].reshape(rows * cols, levels), level_matrix(levels, "below"))
     div_ref[...] = -sums.reshape(rows, cols, levels)
     for y in range(rows):
-        out_ref[sc[1 + y], 0] = div_ref[y]
+        out_ref[1, sc[1 + y], 0] = div_ref[y]
+    out_ref[0] = jnp.zeros(out_ref.shape[1:], jnp.float32)
 
 
 def join_kernel(sc, absorbed_ref, flux_ref, other_ref, out_ref):
     patches, _, half, levels = absorbed_ref.shape
-    first = sc[0] == 0
-    own = pl.multiple_of(sc[0] * half, half)
-    rest = pl.multiple_of((1 - sc[0]) * half, half)
-    for s in range(patches):
-        for f in range(2):
-            out_ref[f, s, pl.ds(own, half)] = jnp.where(first, absorbed_ref[s, f], flux_ref[s, f])
-            out_ref[f, s, pl.ds(rest, half)] = other_ref[s, f]
-
-
-def call(kernel, comp, args, specs, outs, scratch=(), name=None):
+
+    @pl.when(sc[0] == 0)
+    def _():
+        for s in range(patches):
+            for f in range(2):
+                out_ref[f, s, :half] = absorbed_ref[s, f]
+                out_ref[f, s, half:] = other_ref[s, f]
+
+    @pl.when(sc[0] != 0)
+    def _():
+        for s in range(patches):
+            for f in range(2):
+                for part in range(2):
+                    out_ref[f, s, part * half : (part + 1) * half] = flux_ref[part, s, f]
+
+
+def call(kernel, comp, args, specs, outs, scratch=(), name=None, params=PARAMS):
     return pl.pallas_call(
         kernel,
         grid_spec=pltpu.PrefetchScalarGridSpec(
@@ -531,15 +540,15 @@
             scratch_shapes=[pltpu.VMEM(s, jnp.float32) for s in scratch],
         ),
         out_shape=outs,
-        compiler_params=PARAMS,
+        compiler_params=params,
         name=name,
     )(comp, *args)
 
 
 def exchange_rows(low, high):
     count = lax.axis_size("py")
-    north = lax.ppermute(low, "py", [(i + 1, i) for i in range(count - 1)])
-    south = lax.ppermute(high, "py", [(i, i + 1) for i in range(count - 1)])
+    north = lax.ppermute(low, "py", [((i + 1) % count, i) for i in range(count)])
+    south = lax.ppermute(high, "py", [(i, (i + 1) % count) for i in range(count)])
     return north, south
 
 
@@ -712,7 +721,8 @@
     tracer_depth = jnp.sum(jnp.where(here, by_strip, 0), axis=1)
     tracer_depth = lax.dynamic_slice_in_dim(tracer_depth, comp_index * half, half, 1)[..., None]
     owner_row = lax.dynamic_index_in_dim(holder_rank, patch_index, 0, keepdims=False)
-    comp = jnp.concatenate([comp_index.astype(jnp.int32)[None], owner_row])
+    side_index = comp_index.astype(jnp.int32)[None]
+    comp = jnp.concatenate([side_index, owner_row])
     ys = (row_index * CY + jnp.arange(CY, dtype=jnp.int32)).astype(jnp.float32)
     coriolis = coriolis_scale * (2.0 * (ys + 0.5) / (CY * rows_mesh) - 1.0)
 
@@ -723,7 +733,7 @@
         )
         return out.reshape(1, 2, 1, columns, levels)
 
-    sent, *edges = pack(comp, linked, current_speeds, thermal_anomaly)
+    sent, *edges = pack(side_index, linked, current_speeds, thermal_anomaly)
     got = swap(sent)
     times = functools.partial(jnp.dot, precision=lax.Precision.HIGHEST)
     unit = (jnp.arange(fields) == 0).astype(jnp.float32)
@@ -733,10 +743,10 @@
     weights = jnp.stack([c[0] for c in chain] + [c[1] for c in chain[:3]])
     shares = times(weights, photic_absorb_share)
 
-    projected, g = project(comp, tracers, weights, tracer_depth)
+    projected, g = project(side_index, tracers, weights, tracer_depth)
     edges, projected, g = lax.optimization_barrier((edges, projected, g))
     halos0 = exchange_rows(edges[0], edges[1]) + exchange_cols(edges[2], edges[3])
-    kept = first_tracer(comp, projected, g, got, linked, tracer_depth, shares)
+    kept = first_tracer(side_index, projected, g, got, linked, tracer_depth, shares)
     kept, halos0 = lax.optimization_barrier((kept, halos0))
     arrived = to_owners(kept)
 
@@ -751,11 +761,12 @@
     piece = shape_of(CY, half, levels)
     scratch = (CY, half, levels)
     line = shape_of(3, half, levels)
+    first_field = pl.BlockSpec((patches, 1, half, levels), lambda i, c: (0, 0, 0, 0))
     side = shape_of(3, CY, levels)
 
     t2, irr1, *edges = call(
-        absorb_kernel, comp, (arrived, t2, speeds2, depth), [None, patch_half, speeds_half, depth_half],
-        (piece, piece, line, line, side, side), [scratch], "absorb",
+        absorb_kernel, comp, (arrived, t2, speeds2, depth), [first_field, patch_half, speeds_half, depth_half],
+        (piece, piece, line, line, side, side), [scratch], "absorb", STREAMED,
     )
     halos2 = exchange_rows(edges[0], edges[1]) + exchange_half_cols(edges[2], edges[3])
     heat, a, b, g = call(
@@ -766,14 +777,16 @@
     [back] = call(
         last_ocean_kernel, comp, (speeds2, t2, *halos2, depth, heat),
         [speeds_half] + [None] * 5 + [depth_half, None],
-        (shape_of(patches, 2, half, levels),), [scratch], "last_ocean",
-    )
-    flux = to_owners(back)
+        (shape_of(2, patches, 2, half, levels),), [scratch], "last_ocean",
+    )
+    flux = lax.all_to_all(
+        back.reshape(2 * patches, 2, half, levels), ("comp", "py", "px"), split_axis=0, concat_axis=0, tiled=True
+    ).reshape(2, patches, 2, half, levels)
     [absorbed] = call(
         third_kernel, comp, (a, b, g, t2, r2, depth, shares),
         [None] * 4 + [patch_half, depth_half, SMEM], (shape_of(CY, 2, half, levels),), [scratch], "third",
     )
-    other = swap(jnp.where(first, flux, absorbed))
+    other = swap(absorbed)
     [out] = call(
         join_kernel, comp, (absorbed, flux, other), [None] * 3, (shape_of(2, patches, strip, levels),), (), "join"
     )

time: 134 us -> 123 us (0.918); the launches traced: 131 us -> 122 us
  starting transfers between devices: 43.1 us -> 32.2 us
  local copies, waits for them, and re-layouts: 16.4 us -> 19.2 us
    ppermute x6, starting transfers between devices: 17.5 us -> 6.22 us  [the longest x3 3.94 us: exchange_rows(): lax.ppermute(high, 'py', [(i, (i + 1) % count) for i in range(count)])]
    all_to_all x2 -> x1, waiting for transfers between devices: 10.7 us -> 0.01 us  [to_owners(): lax.all_to_all(blocks, ('py', 'px'), split_axis=0, concat_axis=0, tiled=T...]
    all_to_all x0 -> x1, starting transfers between devices: none -> 9.23 us  [shards(): lax.all_to_all(back.reshape(2 * patches, 2, half, levels), ('comp', 'py',...]
    all_to_all x2 -> x1, starting transfers between devices: 14.2 us -> 5.32 us  [to_owners(): lax.all_to_all(blocks, ('py', 'px'), split_axis=0, concat_axis=0, tiled=T...]
    ppermute x2, waiting for transfers between devices: 11.4 us -> 18.3 us  [swap(): return lax.ppermute(block, 'comp', [(0, 1), (1, 0)])]
    unnamed x74 -> x88, local copies, waits for them, and re-layouts: 12.1 us -> 15.7 us
    ppermute x2, waiting for transfers between devices: 2.9 us -> 6.17 us  [exchange_cols(): east = lax.ppermute(low, 'px', [((i + 1) % count, i) for i in range(count)])]
    pallas_call x5, Pallas kernels: 10 us -> 12.7 us  [call(): pl.pallas_call(kernel, grid_spec=pltpu.PrefetchScalarGridSpec(num_scalar_...]
  transfers between devices with their start and end apart: 16 -> 16, of which waited for: 5 -> 4; matrix products, arithmetic and copies ran while one was open for 4% -> 5% of each run, Pallas kernels for 23% -> 23%
where the time goes in v2:
time: 123 us; the launch traced here: 122 us
  Pallas kernels  38.3 us (31%)
  starting transfers between devices  32.2 us (26%)
  waiting for transfers between devices  30.2 us (25%)
  local copies, waits for them, and re-layouts  19.2 us (16%)
  other arithmetic  1.52 us (1%)
    ppermute x2, waiting for transfers between devices, swap(): return lax.ppermute(block, 'comp', [(0, 1), (1, 0)])  18.3 us
    unnamed x88, local copies, waits for them, and re-layouts  15.7 us
    pallas_call x2, Pallas kernels, ocean(): pl.pallas_call(functools.partial(ocean_kernel, advance), grid_spec=pltpu....  13.7 us
    pallas_call x5, Pallas kernels, call(): pl.pallas_call(kernel, grid_spec=pltpu.PrefetchScalarGridSpec(num_scalar_...  12.7 us
    all_to_all x1, starting transfers between devices, shards(): lax.all_to_all(back.reshape(2 * patches, 2, half, levels), ('comp', 'py',...  9.23 us
    ppermute x2, starting transfers between devices, exchange_cols(): east = lax.ppermute(low, 'px', [((i + 1) % count, i) for i in range(count)])  6.54 us
    ppermute x2, waiting for transfers between devices, exchange_cols(): east = lax.ppermute(low, 'px', [((i + 1) % count, i) for i in range(count)])  6.17 us
    pallas_call x1, Pallas kernels, project(): pl.pallas_call(project_kernel, grid_spec=pltpu.PrefetchScalarGridSpec(num...  6.03 us
  transfers between devices with their start and end apart: 16, of which 4 were waited for; matrix products, arithmetic and copies ran while one was open for 5% of the time, Pallas kernels for 23%

profile of v2, /device:TPU:1, one launch (start us, length us, event | category | flops | bytes accessed | tf_op | source)
XLA Modules:
  0.0 122.4 jit_solution(2296693470785705612)
XLA Ops:
  0.0 2.5 %pack.1 = (f32[2,16,16,256]{3,2,1,0:T(8,128)}, f32[3,32,256]{2,1,0:T(8,128)}, f32[3,32,256]{2,1,0:T(8,128)}, f32[3,16,256]{2,1,0:T(8,128)}, f32[3,16,256]{2,1,0:T(8,128)}) custom-call(s32[1]{0:T(128)} %bitcast.sc, f32[2,16,32,256]{3,2,1,0:T(8,128)} %bitcast.50, f32[2,16,32,256]{3,2,1,0:T(8,128)} %speed_ref.1, f32[2,16,32,256]{3,2,1,0:T(8,128)} %speed_ref.1, ...), custom_call_target="tpu_custom_call" | custom-call | tf_op jit(solution)/shard_map/pack/pallas_call | solution.py:237
  2.5 2.0 %collective-permute-start = (f32[2,16,16,256]{3,2,1,0:T(8,128)}, f32[2,16,16,256]{3,2,1,0:T(8,128)S(1)}, u32[]{:S(2)}, u32[]{:S(2)}) collective-permute-start(f32[2,16,16,256]{3,2,1,0:T(8,128)} %get-tuple-element.54), channel_id=1, source_target_pairs={{0,16},{16,0},{1,17},{17,1},{2,18},{18,2},{3,19},{19,3},{4,20},{20... | collective-permute-start | bytes 1572872 | tf_op jit(solution)/shard_map/ppermute | solution.py:576
  6.9 6.0 %project.1 = (f32[7,16,16,256]{3,2,1,0:T(8,128)}, f32[16,16,256]{2,1,0:T(8,128)}) custom-call(s32[1]{0:T(128)} %bitcast.sc, f32[16,16,32,256]{3,2,1,0:T(8,128)} %bitcast.54, f32[7,16]{1,0:T(8,128)} %stack.30.w_ref, s32[16,16,1]{2,1,0:T(8,128)} %copy.14.depth_ref), custom_call_target="tpu_custom_call" | custom-call | tf_op jit(solution)/shard_map/project/pallas_call | solution.py:131
  13.0 3.4 %collective-permute-start.3 = (f32[3,16,256]{2,1,0:T(8,128)S(1)}, f32[3,16,256]{2,1,0:T(8,128)S(1)}, u32[]{:S(2)}, u32[]{:S(2)}) collective-permute-start(f32[3,16,256]{2,1,0:T(8,128)S(1)} %copy-done.41), channel_id=1, source_target_pairs={{1,0},{2,1},{3,2},{0,3},{5,4},{6,5},{7,6},{4,7},{9,8},{10,9},{11,1... | collective-permute-start | bytes 147464 | tf_op jit(solution)/shard_map/ppermute | solution.py:557
  16.3 1.3 %collective-permute-start.1 = (f32[3,32,256]{2,1,0:T(8,128)S(1)}, f32[3,32,256]{2,1,0:T(8,128)S(1)}, u32[]{:S(2)}, u32[]{:S(2)}) collective-permute-start(f32[3,32,256]{2,1,0:T(8,128)S(1)} %copy-done.39), channel_id=1, source_target_pairs={{4,0},{8,4},{12,8},{0,12},{5,1},{9,5},{13,9},{1,13},{6,2},{10,6},{... | collective-permute-start | bytes 294920 | tf_op jit(solution)/shard_map/ppermute | solution.py:550
  17.6 1.2 collective-permute-start.2
  19.0 1.5 %copy-done.11 = f32[7,16,16,256]{3,2,1,0:T(8,128)S(1)} copy-done((f32[7,16,16,256]{3,2,1,0:T(8,128)S(1)}, f32[7,16,16,256]{3,2,1,0:T(8,128)}, u32[]{:S(2)}) %copy-start.11) | copy-done | bytes 1835032
  21.4 3.3 %first_tracer.1 = f32[16,5,16,256]{3,2,1,0:T(8,128)} custom-call(s32[1]{0:T(128)} %bitcast.sc, f32[7,16,16,256]{3,2,1,0:T(8,128)S(1)} %copy-done.11, f32[16,16,256]{2,1,0:T(8,128)S(1)} %copy-done.24, f32[2,16,16,256]{3,2,1,0:T(8,128)S(1)} %collective-permute-done.got_ref.rest_1_, f32[2,16,32,256]{3,2,1,0:T(8,128)S(1)} %bitcast.52, ...), custom_call_target="tpu_custom_call" | custom-call | tf_op jit(solution)/shard_map/first_tracer/pallas_call | solution.py:181
  25.5 5.3 %all-to-all-start = ((f32[16,5,16,256]{3,2,1,0:T(8,128)}), f32[16,5,16,256]{3,2,1,0:T(8,128)S(1)}, u32[]{:S(2)}, u32[]{:S(2)}) async-start(f32[16,5,16,256]{3,2,1,0:T(8,128)} %first_tracer.1), calls=%async_computation | async-start | bytes 2621440 | tf_op jit(solution)/shard_map/all_to_all | solution.py:572
  31.4 1.6 %copy.16.depth_ref = s32[5,16,32,1]{3,2,1,0:T(8,128)} copy(s32[5,16,32,1]{2,1,0,3:T(8,128)S(1)} %bitcast.55) | data formatting | bytes 20480 | tf_op jit(solution)/shard_map/broadcast_in_dim | solution.py:716
  34.4 8.4 %ocean1.1 = (f32[2,16,32,256]{3,2,1,0:T(8,128)}, f32[16,32,256]{2,1,0:T(8,128)}, f32[16,32,256]{2,1,0:T(8,128)}, f32[3,32,256]{2,1,0:T(8,128)}, f32[3,32,256]{2,...) custom-call(s32[17]{0:T(128)} %pad_add_fusion.1.sc, f32[16]{0:T(128)} %multiply_add_fusion.coriolis_ref, ...), custom_call_target="tpu_custom_call" | custom-call | tf_op jit(solution)/shard_map/ocean1/pallas_call | solution.py:384
  42.8 1.6 %collective-permute-start.6 = (f32[3,32,256]{2,1,0:T(8,128)}, f32[3,32,256]{2,1,0:T(8,128)S(1)}, u32[]{:S(2)}, u32[]{:S(2)}) collective-permute-start(f32[3,32,256]{2,1,0:T(8,128)} %get-tuple-element.67), channel_id=1, source_target_pairs={{0,4},{4,8},{8,12},{12,0},{1,5},{5,9},{9,13},{13,1},{2,6},{6,10},{... | collective-permute-start | bytes 294920 | tf_op jit(solution)/shard_map/ppermute | solution.py:551
  44.5 3.2 %collective-permute-start.7 = (f32[3,16,256]{2,1,0:T(8,128)}, f32[3,16,256]{2,1,0:T(8,128)S(1)}, u32[]{:S(2)}, u32[]{:S(2)}) collective-permute-start(f32[3,16,256]{2,1,0:T(8,128)} %get-tuple-element.68), channel_id=1, source_target_pairs={{1,0},{2,1},{3,2},{0,3},{5,4},{6,5},{7,6},{4,7},{9,8},{10,9},{11,1... | collective-permute-start | bytes 147464 | tf_op jit(solution)/shard_map/ppermute | solution.py:557
  47.7 6.2 %collective-permute-done.7.east_ref = f32[3,16,256]{2,1,0:T(8,128)S(1)} collective-permute-done((f32[3,16,256]{2,1,0:T(8,128)}, f32[3,16,256]{2,1,0:T(8,128)S(1)}, u32[]{:S(2)}, u32[]{:S(2)}) %collective-permute-start.7) | collective-permute-done | bytes 49184 | tf_op jit(solution)/shard_map/ppermute | solution.py:557
  53.8 4.4 %collective-permute-done.8.west_ref = f32[3,16,256]{2,1,0:T(8,128)S(1)} collective-permute-done((f32[3,16,256]{2,1,0:T(8,128)}, f32[3,16,256]{2,1,0:T(8,128)S(1)}, u32[]{:S(2)}, u32[]{:S(2)}) %collective-permute-start.8) | collective-permute-done | bytes 49184 | tf_op jit(solution)/shard_map/ppermute | solution.py:558
  58.2 1.0 copy-done.8
  59.3 1.2 copy-done.14
  60.5 5.3 %ocean2.1 = (f32[2,16,32,256]{3,2,1,0:T(8,128)S(1)}, f32[16,32,256]{2,1,0:T(8,128)S(1)}, f32[16,32,256]{2,1,0:T(8,128)S(1)}) custom-call(s32[17]{0:T(128)S(1)} %copy-done.25, f32[16]{0:T(128)S(1)} %copy-done.27, f32[2,16,32,256]{3,2,1,0:T(8,128)S(1)} %copy-done.14, f32[16,32,256]{2,1,0:T(8,128)S(1)} %copy-done.8, ...), custom_call_target="tpu_custom_call" | custom-call | tf_op jit(solution)/shard_map/ocean2/pallas_call | solution.py:384
  68.4 1.1 copy-done.3
  69.5 3.8 %absorb.1 = (f32[16,16,256]{2,1,0:T(8,128)}, f32[16,16,256]{2,1,0:T(8,128)}, f32[3,16,256]{2,1,0:T(8,128)}, f32[3,16,256]{2,1,0:T(8,128)}, f32[3,16,256]{2,1,0:T(8,128)}, /*index=5*/f32[3,16,256]{2,1,0:T(8,128)}) custom-call(s32[17]{0:T(128)} %pad_add_fusion.1.sc, f32[16,5,16,256]{3,2,1,0:T(8,128)} %copy-done.3, f32[16,32,256]{2,1,0:T(8,128)} %copy-done.18, ...), custom_call_target="tpu_custom_call" | custom-call | tf_op jit(solution)/shard_map/absorb/pallas_call | solution.py:533
  74.2 1.1 collective-permute-start.10
  75.4 1.4 %collective-permute-start.12 = (f32[3,16,256]{2,1,0:T(8,128)}, f32[3,16,256]{2,1,0:T(8,128)S(1)}, u32[]{:S(2)}, u32[]{:S(2)}) collective-permute-start(f32[3,16,256]{2,1,0:T(8,128)} %get-tuple-element.85), channel_id=1, source_target_pairs={{0,16},{16,1},{1,17},{17,2},{2,18},{18,3},{3,19},{19,0},{4,20},{20... | collective-permute-start | bytes 147464 | tf_op jit(solution)/shard_map/ppermute | solution.py:567
  76.8 1.3 %copy-done.4 = f32[16,5,16,256]{3,2,1,0:T(8,128)S(1)} copy-done((f32[16,5,16,256]{3,2,1,0:T(8,128)S(1)}, f32[16,5,16,256]{3,2,1,0:T(8,128)}, u32[]{:S(2)}) %copy-start.4) | copy-done | bytes 1310744
  78.1 1.0 copy-done.15
  80.1 2.6 %second.1 = (f32[16,16,256]{2,1,0:T(8,128)S(1)}, f32[16,16,256]{2,1,0:T(8,128)S(1)}, f32[16,16,256]{2,1,0:T(8,128)S(1)}, f32[16,16,256]{2,1,0:T(8,128)S(1)}) custom-call(s32[17]{0:T(128)S(1)} %copy-done.26, f32[16,5,16,256]{3,2,1,0:T(8,128)S(1)} %copy-done.4, f32[16,16,256]{2,1,0:T(8,128)S(1)} %copy-done.23, f32[16,32,256]{2,1,0:T(8,128)S(1)} %copy-done.9, ...), custom_call_target="tpu_custom_call" | custom-call | tf_op jit(solution)/shard_map/second/pallas_call | solution.py:533
  82.7 2.4 %last_ocean.1 = f32[2,16,2,16,256]{4,3,2,1,0:T(8,128)} custom-call(s32[17]{0:T(128)S(1)} %copy-done.26, f32[2,16,32,256]{3,2,1,0:T(8,128)S(1)} %copy-done.7, f32[16,16,256]{2,1,0:T(8,128)S(1)} %copy-done.13, f32[3,16,256]{2,1,0:T(8,128)S(1)} %collective-permute-done.9.north_ref, f32[3,16,256]{2,1,0:T(8,128)S(1)} %collective-permute-done.10.south_ref, ...), custom_call_target="tpu_custom_call" | custom-call | tf_op jit(solution)/shard_map/last_ocean/pallas_call | solution.py:533
  85.2 9.2 %all-to-all-start.1 = ((f32[32,2,16,256]{3,2,1,0:T(8,128)}), f32[32,2,16,256]{3,2,1,0:T(8,128)S(1)}, u32[]{:S(2)}, u32[]{:S(2)}) async-start(f32[32,2,16,256]{3,2,1,0:T(8,128)} %bitcast.17), calls=%async_computation.1 | async-start | bytes 2097152 | tf_op jit(solution)/shard_map/all_to_all | solution.py:782
  97.3 2.3 %third.1.absorbed_ref = f32[16,2,16,256]{3,2,1,0:T(8,128)S(1)} custom-call(s32[17]{0:T(128)S(1)} %copy-done.26, f32[16,16,256]{2,1,0:T(8,128)S(1)} %get-tuple-element.77.a_ref, f32[16,16,256]{2,1,0:T(8,128)S(1)} %copy-done.20, f32[16,16,256]{2,1,0:T(8,128)S(1)} %copy-done.22, f32[16,16,256]{2,1,0:T(8,128)S(1)} %copy-done.13, f32[16,32,256]{2,1,0:T(8,128)S(1)} %copy-done.17, ...), custom_call_target="tpu_custom_call" | custom-call | tf_op jit(solution)/shard_map/third/pallas_call | solution.py:533
  99.7 1.5 %collective-permute-start.13 = (f32[16,2,16,256]{3,2,1,0:T(8,128)S(1)}, f32[16,2,16,256]{3,2,1,0:T(8,128)S(1)}, u32[]{:S(2)}, u32[]{:S(2)}) collective-permute-start(f32[16,2,16,256]{3,2,1,0:T(8,128)S(1)} %third.1.absorbed_ref), channel_id=1, source_target_pairs={{0,16},{16,0},{1,17},{17,1},{2,18},{18,2},{3,19},{19,3},{4,20},{20... | collective-permute-start | bytes 1572872 | tf_op jit(solution)/shard_map/ppermute | solution.py:576
  101.1 18.3 %collective-permute-done.13.other_ref = f32[16,2,16,256]{3,2,1,0:T(8,128)S(1)} collective-permute-done((f32[16,2,16,256]{3,2,1,0:T(8,128)S(1)}, f32[16,2,16,256]{3,2,1,0:T(8,128)S(1)}, u32[]{:S(2)}, u32[]{:S(2)}) %collective-permute-start.13) | collective-permute-done | bytes 524320 | tf_op jit(solution)/shard_map/ppermute | solution.py:576
  119.4 1.3 %all-to-all-done.1 = f32[32,2,16,256]{3,2,1,0:T(8,128)S(1)} async-done(((f32[32,2,16,256]{3,2,1,0:T(8,128)}), f32[32,2,16,256]{3,2,1,0:T(8,128)S(1)}, u32[]{:S(2)}, u32[]{:S(2)}) %all-to-all-start.1) | async-done | bytes 1048608 | tf_op jit(solution)/shard_map/all_to_all | solution.py:782
  120.8 1.6 %join.1 = f32[2,16,32,256]{3,2,1,0:T(8,128)} custom-call(s32[17]{0:T(128)S(1)} %copy-done.26, f32[16,2,16,256]{3,2,1,0:T(8,128)S(1)} %third.1.absorbed_ref, f32[2,16,2,16,256]{4,3,2,1,0:T(8,128)S(1)} %bitcast.53, f32[16,2,16,256]{3,2,1,0:T(8,128)S(1)} %collective-permute-done.13.other_ref), custom_call_target="tpu_custom_call" | custom-call | tf_op jit(solution)/shard_map/join/pallas_call | solution.py:533
  (119 shorter events, 13.6 us)
Async XLA Ops:
  0.0 4.9 %copy-start.33 = (s32[64,128]{1,0:T(8,128)S(1)}, s32[64,128]{1,0:T(8,128)}, u32[]{:S(2)}) copy-start(s32[64,128]{1,0:T(8,128)} %param.14) | copy-start | bytes 98308
  0.0 4.9 %copy-start.34 = (s32[64,128]{1,0:T(8,128)S(1)}, s32[64,128]{1,0:T(8,128)}, u32[]{:S(2)}) copy-start(s32[64,128]{1,0:T(8,128)} %param.15) | copy-start | bytes 98308
  2.5 16.5 %collective-permute-start = (f32[2,16,16,256]{3,2,1,0:T(8,128)}, f32[2,16,16,256]{3,2,1,0:T(8,128)S(1)}, u32[]{:S(2)}, u32[]{:S(2)}) collective-permute-start(f32[2,16,16,256]{3,2,1,0:T(8,128)} %get-tuple-element.54), channel_id=1, source_target_pairs={{0,16},{16,0},{1,17},{17,1},{2,18},{18,2},{3,19},{19,3},{4,20},{20... | collective-permute-start | bytes 1572872 | tf_op jit(solution)/shard_map/ppermute | solution.py:576
  6.9 6.1 %copy-start.41 = (f32[3,16,256]{2,1,0:T(8,128)S(1)}, f32[3,16,256]{2,1,0:T(8,128)}, u32[]{:S(2)}) copy-start(f32[3,16,256]{2,1,0:T(8,128)} %get-tuple-element.57) | copy-start | bytes 147460
  6.9 9.4 %copy-start.40 = (f32[3,16,256]{2,1,0:T(8,128)S(1)}, f32[3,16,256]{2,1,0:T(8,128)}, u32[]{:S(2)}) copy-start(f32[3,16,256]{2,1,0:T(8,128)} %get-tuple-element.58) | copy-start | bytes 147460
  6.9 9.4 %copy-start.39 = (f32[3,32,256]{2,1,0:T(8,128)S(1)}, f32[3,32,256]{2,1,0:T(8,128)}, u32[]{:S(2)}) copy-start(f32[3,32,256]{2,1,0:T(8,128)} %get-tuple-element.55) | copy-start | bytes 294916
  6.9 10.7 %copy-start.38 = (f32[3,32,256]{2,1,0:T(8,128)S(1)}, f32[3,32,256]{2,1,0:T(8,128)}, u32[]{:S(2)}) copy-start(f32[3,32,256]{2,1,0:T(8,128)} %get-tuple-element.56) | copy-start | bytes 294916
  6.9 11.9 %copy-start.32 = (f32[7,16]{1,0:T(8,128)S(1)}, f32[7,16]{1,0:T(8,128)}, u32[]{:S(2)}) copy-start(f32[7,16]{1,0:T(8,128)} %stack.30.w_ref) | copy-start | bytes 1348
  6.9 11.9 %copy-start.37 = (f32[16]{0:T(128)S(1)}, f32[16]{0:T(128)}, u32[]{:S(2)}) copy-start(f32[16]{0:T(128)} %param.18) | copy-start | bytes 196
  6.9 12.1 %copy-start.5 = (f32[1,2,1,512,256]{4,3,2,1,0:T(8,128)S(1)}, f32[1,2,1,512,256]{4,3,2,1,0:T(8,128)}, u32[]{:S(2)}) copy-start(f32[1,2,1,512,256]{4,3,2,1,0:T(8,128)} %param.13) | copy-start | bytes 3145732
  6.9 12.0 %copy-start.12 = (s32[16,16,1]{2,1,0:T(8,128)S(1)}, s32[16,16,1]{2,1,0:T(8,128)}, u32[]{:S(2)}) copy-start(s32[16,16,1]{2,1,0:T(8,128)} %copy.14.depth_ref) | copy-start | bytes 3076
  13.0 11.8 %collective-permute-start.3 = (f32[3,16,256]{2,1,0:T(8,128)S(1)}, f32[3,16,256]{2,1,0:T(8,128)S(1)}, u32[]{:S(2)}, u32[]{:S(2)}) collective-permute-start(f32[3,16,256]{2,1,0:T(8,128)S(1)} %copy-done.41), channel_id=1, source_target_pairs={{1,0},{2,1},{3,2},{0,3},{5,4},{6,5},{7,6},{4,7},{9,8},{10,9},{11,1... | collective-permute-start | bytes 147464 | tf_op jit(solution)/shard_map/ppermute | solution.py:557
  16.3 8.5 %collective-permute-start.4 = (f32[3,16,256]{2,1,0:T(8,128)S(1)}, f32[3,16,256]{2,1,0:T(8,128)S(1)}, u32[]{:S(2)}, u32[]{:S(2)}) collective-permute-start(f32[3,16,256]{2,1,0:T(8,128)S(1)} %copy-done.40), channel_id=1, source_target_pairs={{0,1},{1,2},{2,3},{3,0},{4,5},{5,6},{6,7},{7,4},{8,9},{9,10},{10,1... | collective-permute-start | bytes 147464 | tf_op jit(solution)/shard_map/ppermute | solution.py:558
  16.3 8.5 %collective-permute-start.1 = (f32[3,32,256]{2,1,0:T(8,128)S(1)}, f32[3,32,256]{2,1,0:T(8,128)S(1)}, u32[]{:S(2)}, u32[]{:S(2)}) collective-permute-start(f32[3,32,256]{2,1,0:T(8,128)S(1)} %copy-done.39), channel_id=1, source_target_pairs={{4,0},{8,4},{12,8},{0,12},{5,1},{9,5},{13,9},{1,13},{6,2},{10,6},{... | collective-permute-start | bytes 294920 | tf_op jit(solution)/shard_map/ppermute | solution.py:550
  17.6 7.2 %collective-permute-start.2 = (f32[3,32,256]{2,1,0:T(8,128)S(1)}, f32[3,32,256]{2,1,0:T(8,128)S(1)}, u32[]{:S(2)}, u32[]{:S(2)}) collective-permute-start(f32[3,32,256]{2,1,0:T(8,128)S(1)} %copy-done.38), channel_id=1, source_target_pairs={{0,4},{4,8},{8,12},{12,0},{1,5},{5,9},{9,13},{13,1},{2,6},{6,10},{... | collective-permute-start | bytes 294920 | tf_op jit(solution)/shard_map/ppermute | solution.py:551
  25.5 42.9 %all-to-all-start = ((f32[16,5,16,256]{3,2,1,0:T(8,128)}), f32[16,5,16,256]{3,2,1,0:T(8,128)S(1)}, u32[]{:S(2)}, u32[]{:S(2)}) async-start(f32[16,5,16,256]{3,2,1,0:T(8,128)} %first_tracer.1), calls=%async_computation | async-start | bytes 2621440 | tf_op jit(solution)/shard_map/all_to_all | solution.py:572
  34.3 23.9 %copy-start.1 = (s32[5,16,32,1]{3,2,1,0:T(8,128)S(1)}, s32[5,16,32,1]{3,2,1,0:T(8,128)}, u32[]{:S(2)}) copy-start(s32[5,16,32,1]{3,2,1,0:T(8,128)} %copy.16.depth_ref) | copy-start | bytes 30724
  34.4 23.9 %copy-start.25 = (s32[17]{0:T(128)S(1)}, s32[17]{0:T(128)}, u32[]{:S(2)}) copy-start(s32[17]{0:T(128)} %pad_add_fusion.1.sc) | copy-start | bytes 208
  34.4 23.9 %copy-start.27 = (f32[16]{0:T(128)S(1)}, f32[16]{0:T(128)}, u32[]{:S(2)}) copy-start(f32[16]{0:T(128)} %multiply_add_fusion.coriolis_ref) | copy-start | bytes 196
  42.7 15.5 %collective-permute-start.5 = (f32[3,32,256]{2,1,0:T(8,128)}, f32[3,32,256]{2,1,0:T(8,128)S(1)}, u32[]{:S(2)}, u32[]{:S(2)}) collective-permute-start(f32[3,32,256]{2,1,0:T(8,128)} %get-tuple-element.66), channel_id=1, source_target_pairs={{4,0},{8,4},{12,8},{0,12},{5,1},{9,5},{13,9},{1,13},{6,2},{10,6},{... | collective-permute-start | bytes 294920 | tf_op jit(solution)/shard_map/ppermute | solution.py:550
  42.8 15.4 %collective-permute-start.6 = (f32[3,32,256]{2,1,0:T(8,128)}, f32[3,32,256]{2,1,0:T(8,128)S(1)}, u32[]{:S(2)}, u32[]{:S(2)}) collective-permute-start(f32[3,32,256]{2,1,0:T(8,128)} %get-tuple-element.67), channel_id=1, source_target_pairs={{0,4},{4,8},{8,12},{12,0},{1,5},{5,9},{9,13},{13,1},{2,6},{6,10},{... | collective-permute-start | bytes 294920 | tf_op jit(solution)/shard_map/ppermute | solution.py:551
  44.5 9.4 %collective-permute-start.7 = (f32[3,16,256]{2,1,0:T(8,128)}, f32[3,16,256]{2,1,0:T(8,128)S(1)}, u32[]{:S(2)}, u32[]{:S(2)}) collective-permute-start(f32[3,16,256]{2,1,0:T(8,128)} %get-tuple-element.68), channel_id=1, source_target_pairs={{1,0},{2,1},{3,2},{0,3},{5,4},{6,5},{7,6},{4,7},{9,8},{10,9},{11,1... | collective-permute-start | bytes 147464 | tf_op jit(solution)/shard_map/ppermute | solution.py:557
  47.7 10.5 %collective-permute-start.8 = (f32[3,16,256]{2,1,0:T(8,128)}, f32[3,16,256]{2,1,0:T(8,128)S(1)}, u32[]{:S(2)}, u32[]{:S(2)}) collective-permute-start(f32[3,16,256]{2,1,0:T(8,128)} %get-tuple-element.69), channel_id=1, source_target_pairs={{0,1},{1,2},{2,3},{3,0},{4,5},{5,6},{6,7},{7,4},{8,9},{9,10},{10,1... | collective-permute-start | bytes 147464 | tf_op jit(solution)/shard_map/ppermute | solution.py:558
  69.5 7.3 %copy-start.2 = (s32[5,16,32,1]{3,2,1,0:T(8,128)S(1)}, s32[5,16,32,1]{3,2,1,0:T(8,128)}, u32[]{:S(2)}) copy-start(s32[5,16,32,1]{3,2,1,0:T(8,128)} %copy.16.depth_ref) | copy-start | bytes 30724
  69.5 7.3 %copy-start.9 = (f32[16,32,256]{2,1,0:T(8,128)S(1)}, f32[16,32,256]{2,1,0:T(8,128)}, u32[]{:S(2)}) copy-start(f32[16,32,256]{2,1,0:T(8,128)} %get-tuple-element.65.t_ref.t1_ref) | copy-start | bytes 1572868
  69.5 7.3 %copy-start.26 = (s32[17]{0:T(128)S(1)}, s32[17]{0:T(128)}, u32[]{:S(2)}) copy-start(s32[17]{0:T(128)} %pad_add_fusion.1.sc) | copy-start | bytes 208
  73.3 9.4 %collective-permute-start.9 = (f32[3,16,256]{2,1,0:T(8,128)}, f32[3,16,256]{2,1,0:T(8,128)S(1)}, u32[]{:S(2)}, u32[]{:S(2)}) collective-permute-start(f32[3,16,256]{2,1,0:T(8,128)} %get-tuple-element.82), channel_id=1, source_target_pairs={{4,0},{8,4},{12,8},{0,12},{5,1},{9,5},{13,9},{1,13},{6,2},{10,6},{... | collective-permute-start | bytes 147464 | tf_op jit(solution)/shard_map/ppermute | solution.py:550
  74.2 8.5 %collective-permute-start.10 = (f32[3,16,256]{2,1,0:T(8,128)}, f32[3,16,256]{2,1,0:T(8,128)S(1)}, u32[]{:S(2)}, u32[]{:S(2)}) collective-permute-start(f32[3,16,256]{2,1,0:T(8,128)} %get-tuple-element.83), channel_id=1, source_target_pairs={{0,4},{4,8},{8,12},{12,0},{1,5},{5,9},{9,13},{13,1},{2,6},{6,10},{... | collective-permute-start | bytes 147464 | tf_op jit(solution)/shard_map/ppermute | solution.py:551
  75.3 7.4 %collective-permute-start.11 = (f32[3,16,256]{2,1,0:T(8,128)}, f32[3,16,256]{2,1,0:T(8,128)S(1)}, u32[]{:S(2)}, u32[]{:S(2)}) collective-permute-start(f32[3,16,256]{2,1,0:T(8,128)} %get-tuple-element.84), channel_id=1, source_target_pairs={{16,0},{1,16},{17,1},{2,17},{18,2},{3,18},{19,3},{0,19},{20,4},{5,... | collective-permute-start | bytes 147464 | tf_op jit(solution)/shard_map/ppermute | solution.py:566
  75.4 7.3 %collective-permute-start.12 = (f32[3,16,256]{2,1,0:T(8,128)}, f32[3,16,256]{2,1,0:T(8,128)S(1)}, u32[]{:S(2)}, u32[]{:S(2)}) collective-permute-start(f32[3,16,256]{2,1,0:T(8,128)} %get-tuple-element.85), channel_id=1, source_target_pairs={{0,16},{16,1},{1,17},{17,2},{2,18},{18,3},{3,19},{19,0},{4,20},{20... | collective-permute-start | bytes 147464 | tf_op jit(solution)/shard_map/ppermute | solution.py:567
  85.2 35.6 %all-to-all-start.1 = ((f32[32,2,16,256]{3,2,1,0:T(8,128)}), f32[32,2,16,256]{3,2,1,0:T(8,128)S(1)}, u32[]{:S(2)}, u32[]{:S(2)}) async-start(f32[32,2,16,256]{3,2,1,0:T(8,128)} %bitcast.17), calls=%async_computation.1 | async-start | bytes 2097152 | tf_op jit(solution)/shard_map/all_to_all | solution.py:782
  99.7 19.8 %collective-permute-start.13 = (f32[16,2,16,256]{3,2,1,0:T(8,128)S(1)}, f32[16,2,16,256]{3,2,1,0:T(8,128)S(1)}, u32[]{:S(2)}, u32[]{:S(2)}) collective-permute-start(f32[16,2,16,256]{3,2,1,0:T(8,128)S(1)} %third.1.absorbed_ref), channel_id=1, source_target_pairs={{0,16},{16,0},{1,17},{17,1},{2,18},{18,2},{3,19},{19,3},{4,20},{20... | collective-permute-start | bytes 1572872 | tf_op jit(solution)/shard_map/ppermute | solution.py:576
  (26 other events, 44.6 us)

commit v3 on v2

--- a/solution.py
+++ b/solution.py
@@ -24,8 +24,8 @@
 CX = 32
 KEPT = (0, 1, 2, 4, 5)
 SMEM = pl.BlockSpec(memory_space=pltpu.SMEM)
-PARAMS = pltpu.CompilerParams(vmem_limit_bytes=24 * 1024 * 1024)
-PROJECT = pltpu.CompilerParams(vmem_limit_bytes=57 * 1024 * 1024)
+PARAMS = pltpu.CompilerParams(vmem_limit_bytes=20 * 1024 * 1024)
+HBM = pl.BlockSpec(memory_space=pltpu.HBM)
 STREAMED = pltpu.CompilerParams(vmem_limit_bytes=60 * 1024 * 1024)
 
 
@@ -97,57 +97,63 @@
     return jnp.where(k > 0, 0.5 * rise, 0.0)
 
 
-def project_kernel(sc, x_ref, w_ref, depth_ref, y_ref, g_ref, chl_ref):
-    fields, patches, cols, levels = x_ref.shape
-
+def project_kernel(sc, x_hbm, w_ref, y_ref, g_ref, x_ref, chl_ref, sems):
+    pieces, fields, block, cols, levels = x_ref.shape
+    own = pl.ds(pl.multiple_of(sc[0] * cols, cols), cols)
+    copies = [
+        pltpu.make_async_copy(x_hbm.at[:, pl.ds(i * block, block), own], x_ref.at[i], sems.at[i]) for i in range(pieces)
+    ]
+    for copy in copies:
+        copy.start()
     mixed = [k for k in range(y_ref.shape[0]) if k != 4]
-
-    def one(q, carry):
-        value = x_ref[0, q]
-        y_ref[4, q] = value
-        totals = [w_ref[k, 0] * value for k in mixed]
-        for j in range(1, fields):
-            value = x_ref[j, q]
-            totals = [t + w_ref[k, j] * value for t, k in zip(totals, mixed)]
-        for k, total in zip(mixed, totals):
-            y_ref[k, q] = total
-        chl_ref[q] = softplus(totals[0])
-        return carry
-
-    lax.fori_loop(0, patches, one, 0)
-    flat = (patches * cols, levels)
-    chl = chl_ref[...].reshape(flat)
-    sums = level_sums(chl, level_matrix(levels, "prefix"))
-    _, irradiance = light(chl, sums, level_of(flat))
-    n = x_ref[0].reshape(flat)
-    g_ref[...] = (uptake_rate * irradiance * saturation(n)).reshape(patches, cols, levels)
-
-
-def project(comp, tracers, weights, depth):
+    prefix = level_matrix(levels, "prefix")
+    flat = (block * cols, levels)
+    for i, copy in enumerate(copies):
+        copy.wait()
+
+        def one(q, carry):
+            at = i * block + q
+            value = x_ref[i, 0, q]
+            y_ref[4, at] = value
+            totals = [w_ref[k, 0] * value for k in mixed]
+            for j in range(1, fields):
+                value = x_ref[i, j, q]
+                totals = [t + w_ref[k, j] * value for t, k in zip(totals, mixed)]
+            for k, total in zip(mixed, totals):
+                y_ref[k, at] = total
+            chl_ref[q] = softplus(totals[0])
+            return carry
+
+        lax.fori_loop(0, block, one, 0)
+        chl = chl_ref[...].reshape(flat)
+        _, irradiance = light(chl, level_sums(chl, prefix), level_of(flat))
+        n = x_ref[i, 0].reshape(flat)
+        g_ref[i * block : (i + 1) * block] = (uptake_rate * irradiance * saturation(n)).reshape(block, cols, levels)
+
+
+def project(comp, tracers, weights):
     fields, patches, strip, levels = tracers.shape
     half = strip // 2
-    block = 4
-    kinds = weights.shape[0]
+    pieces = 4
+    block = patches // pieces
+    outs = (shape_of(weights.shape[0], patches, half, levels), shape_of(patches, half, levels))
     return pl.pallas_call(
         project_kernel,
         grid_spec=pltpu.PrefetchScalarGridSpec(
             num_scalar_prefetch=1,
-            grid=(patches // block,),
-            in_specs=[
-                pl.BlockSpec((fields, block, half, levels), lambda i, c: (0, i, c[0], 0)),
-                SMEM,
-                pl.BlockSpec((block, half, 1), lambda i, c: (i, 0, 0)),
+            grid=(1,),
+            in_specs=[HBM, SMEM],
+            out_specs=[whole(o) for o in outs],
+            scratch_shapes=[
+                pltpu.VMEM((pieces, fields, block, half, levels), jnp.float32),
+                pltpu.VMEM((block, half, levels), jnp.float32),
+                pltpu.SemaphoreType.DMA((pieces,)),
             ],
-            out_specs=[
-                pl.BlockSpec((kinds, block, half, levels), lambda i, c: (0, i, 0, 0)),
-                pl.BlockSpec((block, half, levels), lambda i, c: (i, 0, 0)),
-            ],
-            scratch_shapes=[pltpu.VMEM((block, half, levels), jnp.float32)],
         ),
-        out_shape=(shape_of(kinds, patches, half, levels), shape_of(patches, half, levels)),
-        compiler_params=PROJECT,
+        out_shape=outs,
+        compiler_params=PARAMS,
         name="project",
-    )(comp, tracers, weights, depth)
+    )(comp, tracers, weights)
 
 
 def first_tracer_kernel(sc, y_ref, g_ref, got_ref, own_ref, depth_ref, share_ref, out_ref):
@@ -263,10 +269,16 @@
     *rest,
 ):
     rest = list(rest)
-    u_ref, v_ref = speed_ref.at[0], speed_ref.at[1]
+    copies = []
     if advance == 1:
         linked_ref, got_ref = rest[:2]
-        rest = rest[2:]
+        *rest, heat_in, speed_in, linked_in, sems = rest[2:]
+        for i, (source, target) in enumerate(((t_ref, heat_in), (speed_ref, speed_in), (linked_ref, linked_in))):
+            copies.append(pltpu.make_async_copy(source, target, sems.at[i]))
+            copies[-1].start()
+        t_ref, speed_ref, linked_ref = heat_in, speed_in, linked_in
+        copies[0].wait()
+    u_ref, v_ref = speed_ref.at[0], speed_ref.at[1]
     next_ref, tn_ref, rise_ref = rest[:3]
     edge_refs = rest[3:7] if advance == 1 else ()
     un_ref, vn_ref = next_ref.at[0], next_ref.at[1]
@@ -278,6 +290,8 @@
     ).reshape(rows, cols, levels)
     for target, source in ((pn_ref, north_ref), (ps_ref, south_ref), (pe_ref, east_ref), (pw_ref, west_ref)):
         target[...] = weight_pull_factor * level_sums(source[2], above)
+    for copy in copies[1:]:
+        copy.wait()
     lanes = min(128, levels)
     place = lax.broadcasted_iota(jnp.int32, (cols, lanes), 0)
     at_east, at_west = place == cols - 1, place == 0
@@ -380,30 +394,38 @@
     scratch = [
         (rows, cols, levels), (cols, levels), (cols, levels), (rows, levels), (rows, levels), (rows, cols, levels),
     ]
+    scratch = [pltpu.VMEM(s, jnp.float32) for s in scratch]
+    if advance == 1:
+        scratch += [pltpu.VMEM(x.shape, jnp.float32) for x in (heat, speeds, linked)] + [pltpu.SemaphoreType.DMA((3,))]
     args = [coriolis, speeds, heat, *halos, depth] + ([linked, got] if advance == 1 else [])
     return pl.pallas_call(
         functools.partial(ocean_kernel, advance),
         grid_spec=pltpu.PrefetchScalarGridSpec(
             num_scalar_prefetch=1,
             grid=(1,),
-            in_specs=[SMEM] + [whole(a) for a in args[1:]],
+            in_specs=[SMEM] + [
+                HBM if advance == 1 and any(x is y for y in (speeds, heat, linked)) else whole(x) for x in args[1:]
+            ],
             out_specs=[whole(o) for o in outs],
-            scratch_shapes=[pltpu.VMEM(s, jnp.float32) for s in scratch],
+            scratch_shapes=scratch,
         ),
         out_shape=outs,
-        compiler_params=STREAMED if advance == 1 else PARAMS,
+        compiler_params=PARAMS,
         name=f"ocean{advance}",
     )(comp, *args)
 
 
 def absorb_kernel(
-    sc, y_ref, t_ref, speed_ref, depth_ref, t2_ref, irr_ref, row0_ref, row1_ref, col0_ref, col1_ref, chl_ref
+    sc, y_hbm, t_ref, speed_ref, depth_ref, t2_ref, irr_ref, row0_ref, row1_ref, col0_ref, col1_ref, chl_ref, y_ref, sem
 ):
     rows, cols, levels = t_ref.shape
     flat = (rows * cols, levels)
+    copy = pltpu.make_async_copy(y_hbm.at[:, 0], y_ref, sem)
+    copy.start()
+    copy.wait()
 
     def gather(s, carry):
-        chl_ref[s] = softplus(y_ref[sc[1 + s], 0])
+        chl_ref[s] = softplus(y_ref[sc[1 + s]])
         return carry
 
     lax.fori_loop(0, rows, gather, 0, unroll=2)
@@ -529,7 +551,7 @@
                     out_ref[f, s, part * half : (part + 1) * half] = flux_ref[part, s, f]
 
 
-def call(kernel, comp, args, specs, outs, scratch=(), name=None, params=PARAMS):
+def call(kernel, comp, args, specs, outs, scratch=(), name=None, sems=()):
     return pl.pallas_call(
         kernel,
         grid_spec=pltpu.PrefetchScalarGridSpec(
@@ -537,10 +559,10 @@
             grid=(1,),
             in_specs=[spec or whole(a) for spec, a in zip(specs, args)],
             out_specs=[whole(o) for o in outs],
-            scratch_shapes=[pltpu.VMEM(s, jnp.float32) for s in scratch],
+            scratch_shapes=[pltpu.VMEM(s, jnp.float32) for s in scratch] + list(sems),
         ),
         out_shape=outs,
-        compiler_params=params,
+        compiler_params=PARAMS,
         name=name,
     )(comp, *args)
 
@@ -566,6 +588,14 @@
     east = lax.ppermute(low, ("comp", "px"), [(b, a) for a, b in ahead])
     west = lax.ppermute(high, ("comp", "px"), ahead)
     return east, west
+
+
+def in_hbm(x):
+    return pltpu.with_memory_space_constraint(x, pltpu.HBM)
+
+
+def in_vmem(x):
+    return pltpu.with_memory_space_constraint(x, pltpu.VMEM)
 
 
 def to_owners(blocks):
@@ -733,6 +763,9 @@
         )
         return out.reshape(1, 2, 1, columns, levels)
 
+    linked, tracers, current_speeds, thermal_anomaly = (
+        in_hbm(x) for x in (linked, tracers, current_speeds, thermal_anomaly)
+    )
     sent, *edges = pack(side_index, linked, current_speeds, thermal_anomaly)
     got = swap(sent)
     times = functools.partial(jnp.dot, precision=lax.Precision.HIGHEST)
@@ -743,8 +776,9 @@
     weights = jnp.stack([c[0] for c in chain] + [c[1] for c in chain[:3]])
     shares = times(weights, photic_absorb_share)
 
-    projected, g = project(side_index, tracers, weights, tracer_depth)
+    projected, g = project(side_index, tracers, weights)
     edges, projected, g = lax.optimization_barrier((edges, projected, g))
+    projected, g = in_vmem(projected), in_vmem(g)
     halos0 = exchange_rows(edges[0], edges[1]) + exchange_cols(edges[2], edges[3])
     kept = first_tracer(side_index, projected, g, got, linked, tracer_depth, shares)
     kept, halos0 = lax.optimization_barrier((kept, halos0))
@@ -752,8 +786,10 @@
 
     speeds1, t1, r1, *edges = ocean(1, comp, coriolis, current_speeds, thermal_anomaly, halos0, depth, linked, got)
     halos1 = exchange_rows(edges[0], edges[1]) + exchange_cols(edges[2], edges[3])
+    speeds1, t1, r1 = in_vmem(speeds1), in_vmem(t1), in_hbm(r1)
     speeds2, t2, r2 = ocean(2, comp, coriolis, speeds1, t1, halos1, depth)
     arrived, speeds2, t2 = lax.optimization_barrier((arrived, speeds2, t2))
+    speeds2, t2, r2 = in_hbm(speeds2), in_hbm(t2), in_hbm(r2)
 
     patch_half = half_spec((CY,), half, levels)
     speeds_half = half_spec((2, CY), half, levels)
@@ -761,12 +797,11 @@
     piece = shape_of(CY, half, levels)
     scratch = (CY, half, levels)
     line = shape_of(3, half, levels)
-    first_field = pl.BlockSpec((patches, 1, half, levels), lambda i, c: (0, 0, 0, 0))
     side = shape_of(3, CY, levels)
 
     t2, irr1, *edges = call(
-        absorb_kernel, comp, (arrived, t2, speeds2, depth), [first_field, patch_half, speeds_half, depth_half],
-        (piece, piece, line, line, side, side), [scratch], "absorb", STREAMED,
+        absorb_kernel, comp, (arrived, t2, speeds2, depth), [HBM, patch_half, speeds_half, depth_half],
+        (piece, piece, line, line, side, side), [scratch] * 2, "absorb", [pltpu.SemaphoreType.DMA],
     )
     halos2 = exchange_rows(edges[0], edges[1]) + exchange_half_cols(edges[2], edges[3])
     heat, a, b, g = call(

time: 123 us -> 115 us (0.935)
  local copies, waits for them, and re-layouts: 19.2 us -> 7.95 us
  waiting for transfers between devices: 30.2 us -> 35.3 us
  Pallas kernels: 38.3 us -> 36.9 us
    unnamed x88 -> x48, local copies, waits for them, and re-layouts: 15.7 us -> 6.7 us
    ppermute x1, waiting for transfers between devices: 0.01 us -> 2.27 us  [exchange_half_cols(): west = lax.ppermute(high, ('comp', 'px'), ahead)]
    ppermute x2, waiting for transfers between devices: 6.17 us -> 8.35 us  [exchange_cols(): east = lax.ppermute(low, 'px', [((i + 1) % count, i) for i in range(count)])]
    pallas_call x2, Pallas kernels: 13.7 us -> 11.9 us  [ocean(): pl.pallas_call(functools.partial(ocean_kernel, advance), grid_spec=pltpu....]
    all_to_all x1, starting transfers between devices: 5.32 us -> 7.01 us  [to_owners(): lax.all_to_all(blocks, ('py', 'px'), split_axis=0, concat_axis=0, tiled=T...]
  transfers between devices with their start and end apart: 16 -> 16, of which waited for: 4 -> 5; matrix products, arithmetic and copies ran while one was open for 5% -> 2% of each run, Pallas kernels for 23% -> 24%
where the time goes in v3:
time: 115 us; the launch traced here: 114 us
  Pallas kernels  36.9 us (32%)
  waiting for transfers between devices  35.3 us (31%)
  starting transfers between devices  32.9 us (29%)
  local copies, waits for them, and re-layouts  7.95 us (7%)
    ppermute x2, waiting for transfers between devices, swap(): return lax.ppermute(block, 'comp', [(0, 1), (1, 0)])  18.7 us
    pallas_call x5, Pallas kernels, call(): pl.pallas_call(kernel, grid_spec=pltpu.PrefetchScalarGridSpec(num_scalar_...  13.3 us
    pallas_call x2, Pallas kernels, ocean(): pl.pallas_call(functools.partial(ocean_kernel, advance), grid_spec=pltpu....  11.9 us
    ppermute x2, waiting for transfers between devices, exchange_cols(): east = lax.ppermute(low, 'px', [((i + 1) % count, i) for i in range(count)])  8.35 us
    all_to_all x1, starting transfers between devices, shards(): lax.all_to_all(back.reshape(2 * patches, 2, half, levels), ('comp', 'py',...  8.09 us
    all_to_all x1, starting transfers between devices, to_owners(): lax.all_to_all(blocks, ('py', 'px'), split_axis=0, concat_axis=0, tiled=T...  7.01 us
    unnamed x48, local copies, waits for them, and re-layouts  6.7 us
    ppermute x2, starting transfers between devices, exchange_cols(): east = lax.ppermute(low, 'px', [((i + 1) % count, i) for i in range(count)])  6.56 us
  transfers between devices with their start and end apart: 16, of which 5 were waited for; matrix products, arithmetic and copies ran while one was open for 2% of the time, Pallas kernels for 24%

profile of v3, /device:TPU:1, one launch (start us, length us, event | category | flops | bytes accessed | tf_op | source)
XLA Modules:
  0.0 114.3 jit_solution(7949950235936602312)
XLA Ops:
  0.0 2.5 %pack.1 = (f32[2,16,16,256]{3,2,1,0:T(8,128)}, f32[3,32,256]{2,1,0:T(8,128)}, f32[3,32,256]{2,1,0:T(8,128)}, f32[3,16,256]{2,1,0:T(8,128)}, f32[3,16,256]{2,1,0:T(8,128)}) custom-call(s32[1]{0:T(128)} %bitcast.sc, f32[2,16,32,256]{3,2,1,0:T(8,128)} %bitcast.51, f32[2,16,32,256]{3,2,1,0:T(8,128)} %speed_ref.1, f32[2,16,32,256]{3,2,1,0:T(8,128)} %speed_ref.1, ...), custom_call_target="tpu_custom_call" | custom-call | tf_op jit(solution)/shard_map/pack/pallas_call | solution.py:243
  2.5 2.0 %collective-permute-start = (f32[2,16,16,256]{3,2,1,0:T(8,128)}, f32[2,16,16,256]{3,2,1,0:T(8,128)S(1)}, u32[]{:S(2)}, u32[]{:S(2)}) collective-permute-start(f32[2,16,16,256]{3,2,1,0:T(8,128)} %get-tuple-element.54), channel_id=1, source_target_pairs={{0,16},{16,0},{1,17},{17,1},{2,18},{18,2},{3,19},{19,3},{4,20},{20... | collective-permute-start | bytes 1572872 | tf_op jit(solution)/shard_map/ppermute | solution.py:606
  5.0 5.0 %project.1 = (f32[7,16,16,256]{3,2,1,0:T(8,128)S(1)}, f32[16,16,256]{2,1,0:T(8,128)S(1)}) custom-call(s32[1]{0:T(128)} %bitcast.sc, f32[16,16,32,256]{3,2,1,0:T(8,128)} %bitcast.54, f32[7,16]{1,0:T(8,128)S(1)} %stack.30.w_ref), custom_call_target="tpu_custom_call" | custom-call | tf_op jit(solution)/shard_map/project/pallas_call | solution.py:140
  10.0 3.4 %collective-permute-start.3 = (f32[3,16,256]{2,1,0:T(8,128)S(1)}, f32[3,16,256]{2,1,0:T(8,128)S(1)}, u32[]{:S(2)}, u32[]{:S(2)}) collective-permute-start(f32[3,16,256]{2,1,0:T(8,128)S(1)} %copy-done.21), channel_id=1, source_target_pairs={{1,0},{2,1},{3,2},{0,3},{5,4},{6,5},{7,6},{4,7},{9,8},{10,9},{11,1... | collective-permute-start | bytes 147464 | tf_op jit(solution)/shard_map/ppermute | solution.py:579
  13.4 1.3 %collective-permute-start.1 = (f32[3,32,256]{2,1,0:T(8,128)S(1)}, f32[3,32,256]{2,1,0:T(8,128)S(1)}, u32[]{:S(2)}, u32[]{:S(2)}) collective-permute-start(f32[3,32,256]{2,1,0:T(8,128)S(1)} %copy-done.19), channel_id=1, source_target_pairs={{4,0},{8,4},{12,8},{0,12},{5,1},{9,5},{13,9},{1,13},{6,2},{10,6},{... | collective-permute-start | bytes 294920 | tf_op jit(solution)/shard_map/ppermute | solution.py:572
  14.7 1.2 %collective-permute-start.2 = (f32[3,32,256]{2,1,0:T(8,128)S(1)}, f32[3,32,256]{2,1,0:T(8,128)S(1)}, u32[]{:S(2)}, u32[]{:S(2)}) collective-permute-start(f32[3,32,256]{2,1,0:T(8,128)S(1)} %copy-done.18), channel_id=1, source_target_pairs={{0,4},{4,8},{8,12},{12,0},{1,5},{5,9},{9,13},{13,1},{2,6},{6,10},{... | collective-permute-start | bytes 294920 | tf_op jit(solution)/shard_map/ppermute | solution.py:573
  16.7 4.3 %first_tracer.1 = f32[16,5,16,256]{3,2,1,0:T(8,128)} custom-call(s32[1]{0:T(128)} %bitcast.sc, f32[7,16,16,256]{3,2,1,0:T(8,128)S(1)} %get-tuple-element.52.y_ref, f32[16,16,256]{2,1,0:T(8,128)S(1)} %get-tuple-element.53.g_ref, f32[2,16,16,256]{3,2,1,0:T(8,128)S(1)} %collective-permute-done.got_ref.rest_1_, f32[2,16,32,256]{3,2,1,0:T(8,128)} %bitcast.52, ...), custom_call_target="tpu_custom_call" | custom-call | tf_op jit(solution)/shard_map/first_tracer/pallas_call | solution.py:187
  21.1 7.0 %all-to-all-start = ((f32[16,5,16,256]{3,2,1,0:T(8,128)}), f32[16,5,16,256]{3,2,1,0:T(8,128)S(1)}, u32[]{:S(2)}, u32[]{:S(2)}) async-start(f32[16,5,16,256]{3,2,1,0:T(8,128)} %first_tracer.1), calls=%async_computation | async-start | bytes 2621440 | tf_op jit(solution)/shard_map/all_to_all | solution.py:602
  29.3 1.0 copy-done.3
  30.4 6.5 %ocean1.1 = (f32[2,16,32,256]{3,2,1,0:T(8,128)S(1)}, f32[16,32,256]{2,1,0:T(8,128)S(1)}, f32[16,32,256]{2,1,0:T(8,128)S(1)}, f32[3,32,256]{2,1,0:T(8,128)S(1)}, ...) custom-call(s32[17]{0:T(128)S(1)} %pad_add_fusion.1.sc, ...), custom_call_target="tpu_custom_call" | custom-call | tf_op jit(solution)/shard_map/ocean1/pallas_call | solution.py:401
  36.9 0.8 copy-done.4
  37.9 1.6 %collective-permute-start.6 = (f32[3,32,256]{2,1,0:T(8,128)S(1)}, f32[3,32,256]{2,1,0:T(8,128)S(1)}, u32[]{:S(2)}, u32[]{:S(2)}) collective-permute-start(f32[3,32,256]{2,1,0:T(8,128)S(1)} %get-tuple-element.67), channel_id=1, source_target_pairs={{0,4},{4,8},{8,12},{12,0},{1,5},{5,9},{9,13},{13,1},{2,6},{6,10},{... | collective-permute-start | bytes 294920 | tf_op jit(solution)/shard_map/ppermute | solution.py:573
  39.5 3.2 %collective-permute-start.7 = (f32[3,16,256]{2,1,0:T(8,128)S(1)}, f32[3,16,256]{2,1,0:T(8,128)S(1)}, u32[]{:S(2)}, u32[]{:S(2)}) collective-permute-start(f32[3,16,256]{2,1,0:T(8,128)S(1)} %get-tuple-element.68), channel_id=1, source_target_pairs={{1,0},{2,1},{3,2},{0,3},{5,4},{6,5},{7,6},{4,7},{9,8},{10,9},{11,1... | collective-permute-start | bytes 147464 | tf_op jit(solution)/shard_map/ppermute | solution.py:579
  42.7 8.4 %collective-permute-done.7.east_ref = f32[3,16,256]{2,1,0:T(8,128)S(1)} collective-permute-done((f32[3,16,256]{2,1,0:T(8,128)S(1)}, f32[3,16,256]{2,1,0:T(8,128)S(1)}, u32[]{:S(2)}, u32[]{:S(2)}) %collective-permute-start.7) | collective-permute-done | bytes 49184 | tf_op jit(solution)/shard_map/ppermute | solution.py:579
  51.0 4.4 %collective-permute-done.8.west_ref = f32[3,16,256]{2,1,0:T(8,128)S(1)} collective-permute-done((f32[3,16,256]{2,1,0:T(8,128)S(1)}, f32[3,16,256]{2,1,0:T(8,128)S(1)}, u32[]{:S(2)}, u32[]{:S(2)}) %collective-permute-start.8) | collective-permute-done | bytes 49184 | tf_op jit(solution)/shard_map/ppermute | solution.py:580
  55.4 5.3 %ocean2.1 = (f32[2,16,32,256]{3,2,1,0:T(8,128)S(1)}, f32[16,32,256]{2,1,0:T(8,128)S(1)}, f32[16,32,256]{2,1,0:T(8,128)S(1)}) custom-call(s32[17]{0:T(128)S(1)} %pad_add_fusion.1.sc, f32[16]{0:T(128)S(1)} %multiply_add_fusion.coriolis_ref, f32[2,16,32,256]{3,2,1,0:T(8,128)S(1)} %get-tuple-element.64.speed_ref, ...), custom_call_target="tpu_custom_call" | custom-call | tf_op jit(solution)/shard_map/ocean2/pallas_call | solution.py:401
  60.8 1.0 copy-done.1
  63.4 2.4 %absorb.1 = (f32[16,16,256]{2,1,0:T(8,128)S(1)}, f32[16,16,256]{2,1,0:T(8,128)S(1)}, f32[3,16,256]{2,1,0:T(8,128)S(1)}, f32[3,16,256]{2,1,0:T(8,128)S(1)}, f32[3...) custom-call(s32[17]{0:T(128)S(1)} %pad_add_fusion.1.sc, f32[16,5,16,256]{3,2,1,0:T(8,128)S(1)} %all-to-all-done.y_hbm.y_ref, ...), custom_call_target="tpu_custom_call" | custom-call | tf_op jit(solution)/shard_map/absorb/pallas_call | solution.py:555
  65.8 0.9 collective-permute-start.9
  66.7 1.1 collective-permute-start.10
  68.5 0.8 collective-permute-start.12
  69.3 3.0 %second.1 = (f32[16,16,256]{2,1,0:T(8,128)S(1)}, f32[16,16,256]{2,1,0:T(8,128)S(1)}, f32[16,16,256]{2,1,0:T(8,128)S(1)}, f32[16,16,256]{2,1,0:T(8,128)S(1)}) custom-call(s32[17]{0:T(128)S(1)} %pad_add_fusion.1.sc, f32[16,5,16,256]{3,2,1,0:T(8,128)S(1)} %all-to-all-done.y_hbm.y_ref, f32[16,16,256]{2,1,0:T(8,128)S(1)} %get-tuple-element.75.irr_ref, ...), custom_call_target="tpu_custom_call" | custom-call | tf_op jit(solution)/shard_map/second/pallas_call | solution.py:555
  72.4 2.3 %collective-permute-done.12.west_ref = f32[3,16,256]{2,1,0:T(8,128)S(1)} collective-permute-done((f32[3,16,256]{2,1,0:T(8,128)S(1)}, f32[3,16,256]{2,1,0:T(8,128)S(1)}, u32[]{:S(2)}, u32[]{:S(2)}) %collective-permute-start.12) | collective-permute-done | bytes 49184 | tf_op jit(solution)/shard_map/ppermute | solution.py:589
  74.7 3.5 %last_ocean.1 = f32[2,16,2,16,256]{4,3,2,1,0:T(8,128)} custom-call(s32[17]{0:T(128)S(1)} %pad_add_fusion.1.sc, f32[2,16,32,256]{3,2,1,0:T(8,128)} %copy-done.1, f32[16,16,256]{2,1,0:T(8,128)S(1)} %get-tuple-element.80.t2_ref.t_ref, f32[3,16,256]{2,1,0:T(8,128)S(1)} %collective-permute-done.9.north_ref, f32[3,16,256]{2,1,0:T(8,128)S(1)} %collective-permute-done.10.south_ref, ...), custom_call_target="tpu_custom_call" | custom-call | tf_op jit(solution)/shard_map/last_ocean/pallas_call | solution.py:555
  78.2 8.1 %all-to-all-start.1 = ((f32[32,2,16,256]{3,2,1,0:T(8,128)}), f32[32,2,16,256]{3,2,1,0:T(8,128)S(1)}, u32[]{:S(2)}, u32[]{:S(2)}) async-start(f32[32,2,16,256]{3,2,1,0:T(8,128)} %bitcast.17), calls=%async_computation.1 | async-start | bytes 2097152 | tf_op jit(solution)/shard_map/all_to_all | solution.py:817
  86.3 0.9 copy-done.10
  87.3 0.9 copy-done.12
  88.2 2.7 %third.1.absorbed_ref = f32[16,2,16,256]{3,2,1,0:T(8,128)S(1)} custom-call(s32[17]{0:T(128)S(1)} %pad_add_fusion.1.sc, f32[16,16,256]{2,1,0:T(8,128)S(1)} %copy-done.8, f32[16,16,256]{2,1,0:T(8,128)S(1)} %copy-done.10, f32[16,16,256]{2,1,0:T(8,128)S(1)} %copy-done.12, f32[16,16,256]{2,1,0:T(8,128)S(1)} %get-tuple-element.80.t2_ref.t_ref, ...), custom_call_target="tpu_custom_call" | custom-call | tf_op jit(solution)/shard_map/third/pallas_call | solution.py:555
  91.0 1.4 %collective-permute-start.13 = (f32[16,2,16,256]{3,2,1,0:T(8,128)S(1)}, f32[16,2,16,256]{3,2,1,0:T(8,128)S(1)}, u32[]{:S(2)}, u32[]{:S(2)}) collective-permute-start(f32[16,2,16,256]{3,2,1,0:T(8,128)S(1)} %third.1.absorbed_ref), channel_id=1, source_target_pairs={{0,16},{16,0},{1,17},{17,1},{2,18},{18,2},{3,19},{19,3},{4,20},{20... | collective-permute-start | bytes 1572872 | tf_op jit(solution)/shard_map/ppermute | solution.py:606
  92.4 18.7 %collective-permute-done.13.other_ref = f32[16,2,16,256]{3,2,1,0:T(8,128)S(1)} collective-permute-done((f32[16,2,16,256]{3,2,1,0:T(8,128)S(1)}, f32[16,2,16,256]{3,2,1,0:T(8,128)S(1)}, u32[]{:S(2)}, u32[]{:S(2)}) %collective-permute-start.13) | collective-permute-done | bytes 524320 | tf_op jit(solution)/shard_map/ppermute | solution.py:606
  111.1 1.6 %all-to-all-done.1 = f32[32,2,16,256]{3,2,1,0:T(8,128)S(1)} async-done(((f32[32,2,16,256]{3,2,1,0:T(8,128)}), f32[32,2,16,256]{3,2,1,0:T(8,128)S(1)}, u32[]{:S(2)}, u32[]{:S(2)}) %all-to-all-start.1) | async-done | bytes 1048608 | tf_op jit(solution)/shard_map/all_to_all | solution.py:817
  112.7 1.6 %join.1 = f32[2,16,32,256]{3,2,1,0:T(8,128)} custom-call(s32[17]{0:T(128)S(1)} %pad_add_fusion.1.sc, f32[16,2,16,256]{3,2,1,0:T(8,128)S(1)} %third.1.absorbed_ref, f32[2,16,2,16,256]{4,3,2,1,0:T(8,128)S(1)} %bitcast.50, f32[16,2,16,256]{3,2,1,0:T(8,128)S(1)} %collective-permute-done.13.other_ref), custom_call_target="tpu_custom_call" | custom-call | tf_op jit(solution)/shard_map/join/pallas_call | solution.py:555
  (79 shorter events, 4.9 us)
Async XLA Ops:
  0.0 4.5 %copy-start = (f32[16,16]{1,0:T(8,128)S(1)}, f32[16,16]{1,0:T(8,128)}, u32[]{:S(2)}) copy-start(f32[16,16]{1,0:T(8,128)} %param.17) | copy-start | bytes 3076
  0.0 4.5 %copy-start.16 = (f32[16]{0:T(128)S(1)}, f32[16]{0:T(128)}, u32[]{:S(2)}) copy-start(f32[16]{0:T(128)} %param.19) | copy-start | bytes 196
  2.5 14.2 %collective-permute-start = (f32[2,16,16,256]{3,2,1,0:T(8,128)}, f32[2,16,16,256]{3,2,1,0:T(8,128)S(1)}, u32[]{:S(2)}, u32[]{:S(2)}) collective-permute-start(f32[2,16,16,256]{3,2,1,0:T(8,128)} %get-tuple-element.54), channel_id=1, source_target_pairs={{0,16},{16,0},{1,17},{17,1},{2,18},{18,2},{3,19},{19,3},{4,20},{20... | collective-permute-start | bytes 1572872 | tf_op jit(solution)/shard_map/ppermute | solution.py:606
  4.9 5.1 %copy-start.21 = (f32[3,16,256]{2,1,0:T(8,128)S(1)}, f32[3,16,256]{2,1,0:T(8,128)}, u32[]{:S(2)}) copy-start(f32[3,16,256]{2,1,0:T(8,128)} %get-tuple-element.57) | copy-start | bytes 147460
  5.0 8.4 %copy-start.20 = (f32[3,16,256]{2,1,0:T(8,128)S(1)}, f32[3,16,256]{2,1,0:T(8,128)}, u32[]{:S(2)}) copy-start(f32[3,16,256]{2,1,0:T(8,128)} %get-tuple-element.58) | copy-start | bytes 147460
  5.0 8.4 %copy-start.19 = (f32[3,32,256]{2,1,0:T(8,128)S(1)}, f32[3,32,256]{2,1,0:T(8,128)}, u32[]{:S(2)}) copy-start(f32[3,32,256]{2,1,0:T(8,128)} %get-tuple-element.55) | copy-start | bytes 294916
  5.0 9.7 %copy-start.18 = (f32[3,32,256]{2,1,0:T(8,128)S(1)}, f32[3,32,256]{2,1,0:T(8,128)}, u32[]{:S(2)}) copy-start(f32[3,32,256]{2,1,0:T(8,128)} %get-tuple-element.56) | copy-start | bytes 294916
  5.0 10.9 %copy-start.15 = (s32[16,16]{1,0:T(8,128)S(1)}, s32[16,16]{1,0:T(8,128)}, u32[]{:S(2)}) copy-start(s32[16,16]{1,0:T(8,128)} %param.16) | copy-start | bytes 3076
  5.0 11.0 %copy-start.13 = (s32[64,128]{1,0:T(8,128)S(1)}, s32[64,128]{1,0:T(8,128)}, u32[]{:S(2)}) copy-start(s32[64,128]{1,0:T(8,128)} %param.14) | copy-start | bytes 98308
  5.0 11.0 %copy-start.14 = (s32[64,128]{1,0:T(8,128)S(1)}, s32[64,128]{1,0:T(8,128)}, u32[]{:S(2)}) copy-start(s32[64,128]{1,0:T(8,128)} %param.15) | copy-start | bytes 98308
  5.0 11.1 %copy-start.17 = (f32[16]{0:T(128)S(1)}, f32[16]{0:T(128)}, u32[]{:S(2)}) copy-start(f32[16]{0:T(128)} %param.18) | copy-start | bytes 196
  10.0 11.0 %collective-permute-start.3 = (f32[3,16,256]{2,1,0:T(8,128)S(1)}, f32[3,16,256]{2,1,0:T(8,128)S(1)}, u32[]{:S(2)}, u32[]{:S(2)}) collective-permute-start(f32[3,16,256]{2,1,0:T(8,128)S(1)} %copy-done.21), channel_id=1, source_target_pairs={{1,0},{2,1},{3,2},{0,3},{5,4},{6,5},{7,6},{4,7},{9,8},{10,9},{11,1... | collective-permute-start | bytes 147464 | tf_op jit(solution)/shard_map/ppermute | solution.py:579
  13.4 7.7 %collective-permute-start.4 = (f32[3,16,256]{2,1,0:T(8,128)S(1)}, f32[3,16,256]{2,1,0:T(8,128)S(1)}, u32[]{:S(2)}, u32[]{:S(2)}) collective-permute-start(f32[3,16,256]{2,1,0:T(8,128)S(1)} %copy-done.20), channel_id=1, source_target_pairs={{0,1},{1,2},{2,3},{3,0},{4,5},{5,6},{6,7},{7,4},{8,9},{9,10},{10,1... | collective-permute-start | bytes 147464 | tf_op jit(solution)/shard_map/ppermute | solution.py:580
  13.4 7.7 %collective-permute-start.1 = (f32[3,32,256]{2,1,0:T(8,128)S(1)}, f32[3,32,256]{2,1,0:T(8,128)S(1)}, u32[]{:S(2)}, u32[]{:S(2)}) collective-permute-start(f32[3,32,256]{2,1,0:T(8,128)S(1)} %copy-done.19), channel_id=1, source_target_pairs={{4,0},{8,4},{12,8},{0,12},{5,1},{9,5},{13,9},{1,13},{6,2},{10,6},{... | collective-permute-start | bytes 294920 | tf_op jit(solution)/shard_map/ppermute | solution.py:572
  14.7 6.4 %collective-permute-start.2 = (f32[3,32,256]{2,1,0:T(8,128)S(1)}, f32[3,32,256]{2,1,0:T(8,128)S(1)}, u32[]{:S(2)}, u32[]{:S(2)}) collective-permute-start(f32[3,32,256]{2,1,0:T(8,128)S(1)} %copy-done.18), channel_id=1, source_target_pairs={{0,4},{4,8},{8,12},{12,0},{1,5},{5,9},{9,13},{13,1},{2,6},{6,10},{... | collective-permute-start | bytes 294920 | tf_op jit(solution)/shard_map/ppermute | solution.py:573
  16.7 4.3 %copy-start.2 = (f32[2,16,16,256]{3,2,1,0:T(8,128)}, f32[2,16,16,256]{3,2,1,0:T(8,128)S(1)}, u32[]{:S(2)}) copy-start(f32[2,16,16,256]{3,2,1,0:T(8,128)S(1)} %collective-permute-done.got_ref.rest_1_) | copy-start | bytes 1572868
  21.1 42.3 %all-to-all-start = ((f32[16,5,16,256]{3,2,1,0:T(8,128)}), f32[16,5,16,256]{3,2,1,0:T(8,128)S(1)}, u32[]{:S(2)}, u32[]{:S(2)}) async-start(f32[16,5,16,256]{3,2,1,0:T(8,128)} %first_tracer.1), calls=%async_computation | async-start | bytes 2621440 | tf_op jit(solution)/shard_map/all_to_all | solution.py:602
  29.3 1.0 copy-start.3
  37.7 17.7 %collective-permute-start.5 = (f32[3,32,256]{2,1,0:T(8,128)S(1)}, f32[3,32,256]{2,1,0:T(8,128)S(1)}, u32[]{:S(2)}, u32[]{:S(2)}) collective-permute-start(f32[3,32,256]{2,1,0:T(8,128)S(1)} %get-tuple-element.66), channel_id=1, source_target_pairs={{4,0},{8,4},{12,8},{0,12},{5,1},{9,5},{13,9},{1,13},{6,2},{10,6},{... | collective-permute-start | bytes 294920 | tf_op jit(solution)/shard_map/ppermute | solution.py:572
  37.9 17.6 %collective-permute-start.6 = (f32[3,32,256]{2,1,0:T(8,128)S(1)}, f32[3,32,256]{2,1,0:T(8,128)S(1)}, u32[]{:S(2)}, u32[]{:S(2)}) collective-permute-start(f32[3,32,256]{2,1,0:T(8,128)S(1)} %get-tuple-element.67), channel_id=1, source_target_pairs={{0,4},{4,8},{8,12},{12,0},{1,5},{5,9},{9,13},{13,1},{2,6},{6,10},{... | collective-permute-start | bytes 294920 | tf_op jit(solution)/shard_map/ppermute | solution.py:573
  39.5 11.5 %collective-permute-start.7 = (f32[3,16,256]{2,1,0:T(8,128)S(1)}, f32[3,16,256]{2,1,0:T(8,128)S(1)}, u32[]{:S(2)}, u32[]{:S(2)}) collective-permute-start(f32[3,16,256]{2,1,0:T(8,128)S(1)} %get-tuple-element.68), channel_id=1, source_target_pairs={{1,0},{2,1},{3,2},{0,3},{5,4},{6,5},{7,6},{4,7},{9,8},{10,9},{11,1... | collective-permute-start | bytes 147464 | tf_op jit(solution)/shard_map/ppermute | solution.py:579
  42.7 12.8 %collective-permute-start.8 = (f32[3,16,256]{2,1,0:T(8,128)S(1)}, f32[3,16,256]{2,1,0:T(8,128)S(1)}, u32[]{:S(2)}, u32[]{:S(2)}) collective-permute-start(f32[3,16,256]{2,1,0:T(8,128)S(1)} %get-tuple-element.69), channel_id=1, source_target_pairs={{0,1},{1,2},{2,3},{3,0},{4,5},{5,6},{6,7},{7,4},{8,9},{9,10},{10,1... | collective-permute-start | bytes 147464 | tf_op jit(solution)/shard_map/ppermute | solution.py:580
  65.8 6.6 %collective-permute-start.9 = (f32[3,16,256]{2,1,0:T(8,128)S(1)}, f32[3,16,256]{2,1,0:T(8,128)S(1)}, u32[]{:S(2)}, u32[]{:S(2)}) collective-permute-start(f32[3,16,256]{2,1,0:T(8,128)S(1)} %get-tuple-element.82), channel_id=1, source_target_pairs={{4,0},{8,4},{12,8},{0,12},{5,1},{9,5},{13,9},{1,13},{6,2},{10,6},{... | collective-permute-start | bytes 147464 | tf_op jit(solution)/shard_map/ppermute | solution.py:572
  66.7 5.7 %collective-permute-start.10 = (f32[3,16,256]{2,1,0:T(8,128)S(1)}, f32[3,16,256]{2,1,0:T(8,128)S(1)}, u32[]{:S(2)}, u32[]{:S(2)}) collective-permute-start(f32[3,16,256]{2,1,0:T(8,128)S(1)} %get-tuple-element.83), channel_id=1, source_target_pairs={{0,4},{4,8},{8,12},{12,0},{1,5},{5,9},{9,13},{13,1},{2,6},{6,10},{... | collective-permute-start | bytes 147464 | tf_op jit(solution)/shard_map/ppermute | solution.py:573
  67.9 4.5 %collective-permute-start.11 = (f32[3,16,256]{2,1,0:T(8,128)S(1)}, f32[3,16,256]{2,1,0:T(8,128)S(1)}, u32[]{:S(2)}, u32[]{:S(2)}) collective-permute-start(f32[3,16,256]{2,1,0:T(8,128)S(1)} %get-tuple-element.84), channel_id=1, source_target_pairs={{16,0},{1,16},{17,1},{2,17},{18,2},{3,18},{19,3},{0,19},{20,4},{5,... | collective-permute-start | bytes 147464 | tf_op jit(solution)/shard_map/ppermute | solution.py:588
  68.5 6.2 %collective-permute-start.12 = (f32[3,16,256]{2,1,0:T(8,128)S(1)}, f32[3,16,256]{2,1,0:T(8,128)S(1)}, u32[]{:S(2)}, u32[]{:S(2)}) collective-permute-start(f32[3,16,256]{2,1,0:T(8,128)S(1)} %get-tuple-element.85), channel_id=1, source_target_pairs={{0,16},{16,1},{1,17},{17,2},{2,18},{18,3},{3,19},{19,0},{4,20},{20... | collective-permute-start | bytes 147464 | tf_op jit(solution)/shard_map/ppermute | solution.py:589
  72.4 5.8 %copy-start.7 = (f32[16,16,256]{2,1,0:T(8,128)}, f32[16,16,256]{2,1,0:T(8,128)S(1)}, u32[]{:S(2)}) copy-start(f32[16,16,256]{2,1,0:T(8,128)S(1)} %get-tuple-element.77.a_ref) | copy-start | bytes 786436
  72.4 5.8 %copy-start.9 = (f32[16,16,256]{2,1,0:T(8,128)}, f32[16,16,256]{2,1,0:T(8,128)S(1)}, u32[]{:S(2)}) copy-start(f32[16,16,256]{2,1,0:T(8,128)S(1)} %get-tuple-element.78.b_ref) | copy-start | bytes 786436
  72.4 5.8 %copy-start.11 = (f32[16,16,256]{2,1,0:T(8,128)}, f32[16,16,256]{2,1,0:T(8,128)S(1)}, u32[]{:S(2)}) copy-start(f32[16,16,256]{2,1,0:T(8,128)S(1)} %get-tuple-element.79.g_ref) | copy-start | bytes 786436
  78.2 8.1 %copy-start.8 = (f32[16,16,256]{2,1,0:T(8,128)S(1)}, f32[16,16,256]{2,1,0:T(8,128)}, u32[]{:S(2)}) copy-start(f32[16,16,256]{2,1,0:T(8,128)} %copy-done.7) | copy-start | bytes 786436
  78.2 34.5 %all-to-all-start.1 = ((f32[32,2,16,256]{3,2,1,0:T(8,128)}), f32[32,2,16,256]{3,2,1,0:T(8,128)S(1)}, u32[]{:S(2)}, u32[]{:S(2)}) async-start(f32[32,2,16,256]{3,2,1,0:T(8,128)} %bitcast.17), calls=%async_computation.1 | async-start | bytes 2097152 | tf_op jit(solution)/shard_map/all_to_all | solution.py:817
  91.0 20.1 %collective-permute-start.13 = (f32[16,2,16,256]{3,2,1,0:T(8,128)S(1)}, f32[16,2,16,256]{3,2,1,0:T(8,128)S(1)}, u32[]{:S(2)}, u32[]{:S(2)}) collective-permute-start(f32[16,2,16,256]{3,2,1,0:T(8,128)S(1)} %third.1.absorbed_ref), channel_id=1, source_target_pairs={{0,16},{16,0},{1,17},{17,1},{2,18},{18,2},{3,19},{19,3},{4,20},{20... | collective-permute-start | bytes 1572872 | tf_op jit(solution)/shard_map/ppermute | solution.py:606
  (6 other events, 5.3 us)

commit v4 on v3

--- a/solution.py
+++ b/solution.py
@@ -24,7 +24,7 @@
 CX = 32
 KEPT = (0, 1, 2, 4, 5)
 SMEM = pl.BlockSpec(memory_space=pltpu.SMEM)
-PARAMS = pltpu.CompilerParams(vmem_limit_bytes=20 * 1024 * 1024)
+PARAMS = pltpu.CompilerParams(vmem_limit_bytes=28 * 1024 * 1024)
 HBM = pl.BlockSpec(memory_space=pltpu.HBM)
 STREAMED = pltpu.CompilerParams(vmem_limit_bytes=60 * 1024 * 1024)
 
@@ -220,24 +220,58 @@
     def _():
         sent_ref[...] = linked_ref[:, :, :half]
 
-    last = col1_ref.shape[2] - 1
+    last = col1_ref.shape[2]
+    tall = strips - 2
+    for i in range(2):
+        for f in range(2):
+            left_ref[f, i] = col0_ref[f, :, i]
+            right_ref[f, i] = col1_ref[f, :, last - 2 + i]
+        left_ref[2, i] = tc0_ref[:, i]
+        right_ref[2, i] = tc1_ref[:, last - 2 + i]
+        left_ref[3, i] = linked_ref[0, :, i] + linked_ref[1, :, i]
+        right_ref[3, i] = linked_ref[0, :, strip - 2 + i] + linked_ref[1, :, strip - 2 + i]
     for f in range(2):
-        low_ref[f] = row0_ref[f, 0]
-        high_ref[f] = row1_ref[f, 0]
-        left_ref[f] = col0_ref[f, :, 0]
-        right_ref[f] = col1_ref[f, :, last]
-    low_ref[2] = t0_ref[0]
-    high_ref[2] = t1_ref[0]
-    left_ref[2] = tc0_ref[:, 0]
-    right_ref[2] = tc1_ref[:, last]
+        low_ref[f] = row0_ref[f]
+        high_ref[f] = row1_ref[f]
+    low_ref[2] = t0_ref[...]
+    high_ref[2] = t1_ref[...]
+    low_ref[3] = linked_ref[0, :2] + linked_ref[1, :2]
+    high_ref[3] = linked_ref[0, tall:] + linked_ref[1, tall:]
+
+
+def corner_kernel(sc, left_ref, right_ref, north_ref, south_ref, low_ref, high_ref):
+    rows = left_ref.shape[2]
+    cols = north_ref.shape[2]
+    for source, target, at in ((left_ref, low_ref, 0), (right_ref, high_ref, cols - 2)):
+        for f in range(source.shape[0]):
+            for i in range(2):
+                target[f, i, :rows] = source[f, i]
+                target[f, i, rows : rows + 1] = south_ref[f, 1, at + i : at + i + 1]
+                target[f, i, rows + 1 :] = north_ref[f, 0, at + i : at + i + 1]
+
+
+def ring_places(rows, cols):
+    tall = -(-(rows + 2) // 8) * 8
+    return 2 * cols, 2 * cols + tall, 2 * cols + 2 * tall
+
+
+def ring_kernel(sc, north_ref, south_ref, east_ref, west_ref, ring_ref):
+    cols = north_ref.shape[2]
+    tall = east_ref.shape[2]
+    at_east, at_west, _ = ring_places(tall - 2, cols)
+    ring_ref[...] = jnp.zeros(ring_ref.shape, jnp.float32)
+    ring_ref[:cols] = south_ref[3, 1]
+    ring_ref[cols : 2 * cols] = north_ref[3, 0]
+    ring_ref[at_east : at_east + tall] = east_ref[3, 0]
+    ring_ref[at_west : at_west + tall] = west_ref[3, 1]
 
 
 def pack(comp, linked, speeds, heat):
     _, strips, strip, levels = linked.shape
     rows, cols, _ = heat.shape
     outs = (
-        shape_of(2, strips, strip // 2, levels), shape_of(3, cols, levels), shape_of(3, cols, levels),
-        shape_of(3, rows, levels), shape_of(3, rows, levels),
+        shape_of(2, strips, strip // 2, levels), shape_of(4, 2, cols, levels), shape_of(4, 2, cols, levels),
+        shape_of(4, 2, rows, levels), shape_of(4, 2, rows, levels),
     )
     edge = min(8, cols)
     return pl.pallas_call(
@@ -247,12 +281,12 @@
             grid=(1,),
             in_specs=[
                 whole(linked),
-                pl.BlockSpec((2, 1, cols, levels), lambda i, c: (0, 0, 0, 0)),
-                pl.BlockSpec((2, 1, cols, levels), lambda i, c: (0, rows - 1, 0, 0)),
+                pl.BlockSpec((2, 2, cols, levels), lambda i, c: (0, 0, 0, 0)),
+                pl.BlockSpec((2, 2, cols, levels), lambda i, c: (0, rows // 2 - 1, 0, 0)),
                 pl.BlockSpec((2, rows, edge, levels), lambda i, c: (0, 0, 0, 0)),
                 pl.BlockSpec((2, rows, edge, levels), lambda i, c: (0, 0, cols // edge - 1, 0)),
-                pl.BlockSpec((1, cols, levels), lambda i, c: (0, 0, 0)),
-                pl.BlockSpec((1, cols, levels), lambda i, c: (rows - 1, 0, 0)),
+                pl.BlockSpec((2, cols, levels), lambda i, c: (0, 0, 0)),
+                pl.BlockSpec((2, cols, levels), lambda i, c: (rows // 2 - 1, 0, 0)),
                 pl.BlockSpec((rows, edge, levels), lambda i, c: (0, 0, 0)),
                 pl.BlockSpec((rows, edge, levels), lambda i, c: (0, cols // edge - 1, 0)),
             ],
@@ -264,75 +298,90 @@
     )(comp, linked, speeds, speeds, speeds, speeds, heat, heat, heat, heat)
 
 
-def ocean_kernel(
-    advance, sc, coriolis_ref, speed_ref, t_ref, north_ref, south_ref, east_ref, west_ref, depth_ref,
-    *rest,
-):
-    rest = list(rest)
-    copies = []
-    if advance == 1:
-        linked_ref, got_ref = rest[:2]
-        *rest, heat_in, speed_in, linked_in, sems = rest[2:]
-        for i, (source, target) in enumerate(((t_ref, heat_in), (speed_ref, speed_in), (linked_ref, linked_in))):
-            copies.append(pltpu.make_async_copy(source, target, sems.at[i]))
-            copies[-1].start()
-        t_ref, speed_ref, linked_ref = heat_in, speed_in, linked_in
-        copies[0].wait()
-    u_ref, v_ref = speed_ref.at[0], speed_ref.at[1]
-    next_ref, tn_ref, rise_ref = rest[:3]
-    edge_refs = rest[3:7] if advance == 1 else ()
-    un_ref, vn_ref = next_ref.at[0], next_ref.at[1]
-    p_ref, pn_ref, ps_ref, pe_ref, pw_ref, div_ref = rest[-6:]
-    rows, cols, levels = t_ref.shape
-    above = level_matrix(levels, "above")
-    p_ref[...] = (
-        weight_pull_factor * level_sums(t_ref[...].reshape(rows * cols, levels), above)
-    ).reshape(rows, cols, levels)
-    for target, source in ((pn_ref, north_ref), (ps_ref, south_ref), (pe_ref, east_ref), (pw_ref, west_ref)):
-        target[...] = weight_pull_factor * level_sums(source[2], above)
+def wide_rows(speed_hbm, heat_hbm, linked_hbm, got_ref, north_ref, south_ref, east_ref, west_ref, own_ref, other_ref,
+              first, x_ref, absorb_ref, ring_absorb_ref, linked_ref, sems):
+    rows, cols, levels = heat_hbm.shape
+    width = x_ref.shape[2]
+    inner = (pl.ds(2, rows), pl.ds(0, cols))
+    copies = [
+        pltpu.make_async_copy(linked_hbm, linked_ref, sems.at[0]),
+        pltpu.make_async_copy(heat_hbm, x_ref.at[2, *inner], sems.at[1]),
+        pltpu.make_async_copy(speed_hbm.at[0], x_ref.at[0, *inner], sems.at[2]),
+        pltpu.make_async_copy(speed_hbm.at[1], x_ref.at[1, *inner], sems.at[3]),
+    ]
+    for copy in copies:
+        copy.start()
+    place = lax.broadcasted_iota(jnp.int32, (width - cols, levels), 0)
+    none = jnp.zeros((width - cols, levels), jnp.float32)
+    line = [rows, *range(rows), rows + 1]
+    for f in range(3):
+        x_ref[f, :2, :cols] = south_ref[f]
+        x_ref[f, rows + 2 :, :cols] = north_ref[f]
+        x_ref[f, 0, cols:] = none
+        x_ref[f, rows + 3, cols:] = none
+        for o, r in enumerate(line):
+            cells = none
+            for i in range(2):
+                cells = jnp.where(place == i, east_ref[f, i, r : r + 1], cells)
+                cells = jnp.where(place == width - cols - 2 + i, west_ref[f, i, r : r + 1], cells)
+            x_ref[f, o + 1, cols:] = cells
+    ring_absorb_ref[...] = jnp.where(first, own_ref[...], other_ref[...])
+    absorb_ref[0, :cols] = ring_absorb_ref[:cols]
+    absorb_ref[rows + 1, :cols] = ring_absorb_ref[cols : 2 * cols]
+    at_east, at_west, _ = ring_places(rows, cols)
+    for o, r in enumerate(line):
+        e = ring_absorb_ref[at_east + r : at_east + r + 1]
+        w = ring_absorb_ref[at_west + r : at_west + r + 1]
+        absorb_ref[o, cols:] = jnp.where(place == 0, e, jnp.where(place == width - cols - 1, w, 0.0))
+    copies[0].wait()
+    for y in range(rows):
+        absorb_ref[y + 1, :cols] = jnp.where(
+            first, linked_ref[0, y] + linked_ref[1, y], jnp.concatenate([got_ref[0, y], got_ref[1, y]], axis=0)
+        )
     for copy in copies[1:]:
         copy.wait()
+
+
+def ocean_kernel(advance, sc, coriolis_ref, *refs):
+    if advance == 1:
+        *sources, depth_ref, next_ref, tn_ref, inner_ref, rise_ref, x_ref, absorb_ref = refs[: -5]
+        ring_absorb_ref, linked_ref, sems, p_ref, div_ref = refs[-5:]
+        wide_rows(*sources, sc[0] == 0, x_ref, absorb_ref, ring_absorb_ref, linked_ref, sems)
+        fields = [x_ref.at[f] for f in range(3)]
+    else:
+        speed_ref, t_ref, depth_ref, next_ref, tn_ref, rise_ref, p_ref, div_ref = refs
+        fields = [speed_ref.at[0], speed_ref.at[1], t_ref]
+    tall, width, levels = p_ref.shape
+    rows, cols = rise_ref.shape[:2]
+    out_width = tn_ref.shape[1]
+    p_ref[...] = (
+        weight_pull_factor * level_sums(fields[2][...].reshape(tall * width, levels), level_matrix(levels, "above"))
+    ).reshape(tall, width, levels)
     lanes = min(128, levels)
-    place = lax.broadcasted_iota(jnp.int32, (cols, lanes), 0)
-    at_east, at_west = place == cols - 1, place == 0
-
-    def piece(y, at, lane):
-        north_in = at < rows - 1
-        south_in = at > 0
+
+    def piece(o, lane):
         part = slice(lane, lane + lanes)
-        level = lane + lax.broadcasted_iota(jnp.int32, (cols, lanes), 1)
-
-        def around(x, e, w, n, s):
-            return (
-                x, jnp.where(at_east, e, pltpu.roll(x, cols - 1, 0)), jnp.where(at_west, w, pltpu.roll(x, 1, 0)), n, s
-            )
-
-        def field(ref, f):
-            return around(
-                ref[y, :, part],
-                east_ref[f, pl.ds(y, 1)][:, part],
-                west_ref[f, pl.ds(y, 1)][:, part],
-                ref[y + 1, :, part] if north_in else north_ref[f, :, part],
-                ref[y - 1, :, part] if south_in else south_ref[f, :, part],
-            )
-
-        wet = [jnp.where(level < depth_ref[i, y], 1.0, 0.0) for i in range(5)]
-        u = field(u_ref, 0)
-        v = field(v_ref, 1)
+        level = lane + lax.broadcasted_iota(jnp.int32, (width, lanes), 1)
+
+        def beside(x):
+            return pltpu.roll(x, width - 1, 0), pltpu.roll(x, 1, 0)
+
+        def field(ref):
+            x = ref[o + 1, :, part]
+            return (x, *beside(x), ref[o + 2, :, part], ref[o, :, part])
+
+        def wet_at(d):
+            return jnp.where(level < depth_ref[d], 1.0, 0.0)
+
+        here = wet_at(o + advance)
+        wet = (here, *beside(here), wet_at(o + advance + 1), wet_at(o + advance - 1))
+        u, v, t, p = (field(ref) for ref in (*fields, p_ref))
         own = 0.5 * wet[0]
         east = (u[0] + u[1]) * (own * wet[1])
         west = (u[2] + u[0]) * (own * wet[2])
         north = (v[0] + v[3]) * (own * wet[3])
         south = (v[4] + v[0]) * (own * wet[4])
-        div_ref[y, :, part] = east - west + north - south
-        t = field(t_ref, 2)
-        p = around(
-            p_ref[y, :, part],
-            pe_ref[pl.ds(y, 1)][:, part],
-            pw_ref[pl.ds(y, 1)][:, part],
-            p_ref[y + 1, :, part] if north_in else pn_ref[:, part],
-            p_ref[y - 1, :, part] if south_in else ps_ref[:, part],
-        )
+        div_ref[o, :, part] = east - west + north - south
         wets = wet[1] + wet[2] + wet[3] + wet[4]
 
         def spread(x):
@@ -343,69 +392,59 @@
         )
         change = spreading * spread(t) - carry_along
         if advance == 1:
-            halves = [got_ref[i, y, :, part] for i in range(2)]
-            absorb = jnp.where(
-                sc[0] == 0, linked_ref[0, y, :, part] + linked_ref[1, y, :, part], jnp.concatenate(halves, axis=0)
-            )
-            change = change + heat_gain * absorb
+            change = change + heat_gain * absorb_ref[o, :, part]
         zonal = 0.5 * (wet[1] * (p[1] - p[0]) + wet[2] * (p[0] - p[2]))
         merid = 0.5 * (wet[3] * (p[3] - p[0]) + wet[4] * (p[0] - p[4]))
-        turn = coriolis_ref[y]
+        turn = coriolis_ref[o + advance - 1]
         results = (
             wet[0] * (u[0] + advance_marine * (turn * v[0] - zonal + viscosity * spread(u) - damping * u[0])),
             wet[0] * (v[0] + advance_marine * (-turn * u[0] - merid + viscosity * spread(v) - damping * v[0])),
             wet[0] * (t[0] + advance_marine * change),
         )
-        for f, (ref, value) in enumerate(zip((un_ref, vn_ref, tn_ref), results)):
-            ref[y, :, part] = value
-
-    def row(y, at):
+        for ref, value in zip((next_ref.at[0], next_ref.at[1], tn_ref), results):
+            ref[o, :, part] = value[:out_width]
+
+    def row(o, carry):
         for lane in range(0, levels, lanes):
-            piece(y, at, lane)
-        if edge_refs:
-            for f, ref in enumerate((un_ref, vn_ref, tn_ref)):
-                edge_refs[2][f, pl.ds(y, 1)] = ref[y, :1]
-                edge_refs[3][f, pl.ds(y, 1)] = ref[y, cols - 1 :]
-
-    row(0, 0)
-
-    def inner(y, carry):
-        row(y, 1)
+            piece(o, lane)
         return carry
 
-    lax.fori_loop(1, rows - 1, inner, 0)
-    row(rows - 1, rows - 1)
-    if edge_refs:
-        for f, ref in enumerate((un_ref, vn_ref, tn_ref)):
-            edge_refs[0][f] = ref[0]
-            edge_refs[1][f] = ref[rows - 1]
-    sums = level_sums(div_ref[...].reshape(rows * cols, levels), level_matrix(levels, "below"))
-    rise_ref[...] = -sums.reshape(rows, cols, levels)
-
-
-def ocean(advance, comp, coriolis, speeds, heat, halos, depth, linked=None, got=None):
-    rows, cols, levels = heat.shape
-    grid = shape_of(rows, cols, levels)
-    outs = (shape_of(2, rows, cols, levels), grid, grid)
+    lax.fori_loop(0, tall - 2, row, 0)
+    rim = (tall - 2 - rows) // 2
+    div = div_ref[rim : rim + rows, :cols].reshape(rows * cols, levels)
+    rise_ref[...] = -level_sums(div, level_matrix(levels, "below")).reshape(rows, cols, levels)
     if advance == 1:
-        outs += (
-            shape_of(3, cols, levels), shape_of(3, cols, levels), shape_of(3, rows, levels), shape_of(3, rows, levels),
-        )
-    scratch = [
-        (rows, cols, levels), (cols, levels), (cols, levels), (rows, levels), (rows, levels), (rows, cols, levels),
+        inner_ref[...] = tn_ref[rim : rim + rows, :cols]
+
+
+def ocean(advance, comp, coriolis, args, depth, rows, cols):
+    width, levels = depth.shape[1], args[1].shape[-1]
+    patch = shape_of(rows, cols, levels)
+    if advance == 1:
+        tall = rows + 4
+        outs = (shape_of(2, rows + 2, width, levels), shape_of(rows + 2, width, levels), patch, patch)
+        scratch = [
+            pltpu.VMEM((3, tall, width, levels), jnp.float32),
+            pltpu.VMEM((rows + 2, width, levels), jnp.float32),
+            pltpu.VMEM(args[-1].shape, jnp.float32),
+            pltpu.VMEM(args[2].shape, jnp.float32),
+            pltpu.SemaphoreType.DMA((4,)),
+        ]
+    else:
+        tall = rows + 2
+        outs = (shape_of(2, rows, cols, levels), patch, patch)
+        scratch = []
+    scratch += [
+        pltpu.VMEM((tall, width, levels), jnp.float32), pltpu.VMEM((tall - 2, width, levels), jnp.float32)
     ]
-    scratch = [pltpu.VMEM(s, jnp.float32) for s in scratch]
-    if advance == 1:
-        scratch += [pltpu.VMEM(x.shape, jnp.float32) for x in (heat, speeds, linked)] + [pltpu.SemaphoreType.DMA((3,))]
-    args = [coriolis, speeds, heat, *halos, depth] + ([linked, got] if advance == 1 else [])
+    args = [coriolis, *args, depth]
+    own_copies = 3 if advance == 1 else 0
     return pl.pallas_call(
         functools.partial(ocean_kernel, advance),
         grid_spec=pltpu.PrefetchScalarGridSpec(
             num_scalar_prefetch=1,
             grid=(1,),
-            in_specs=[SMEM] + [
-                HBM if advance == 1 and any(x is y for y in (speeds, heat, linked)) else whole(x) for x in args[1:]
-            ],
+            in_specs=[SMEM] + [HBM] * own_copies + [whole(x) for x in args[1 + own_copies :]],
             out_specs=[whole(o) for o in outs],
             scratch_shapes=scratch,
         ),
@@ -739,9 +778,14 @@
     u0, v0 = current_speeds[0], current_speeds[1]
 
     column_depth = marine_indicator * floor_layer_index
-    wrapped = jnp.concatenate([column_depth[:, -1:], column_depth, column_depth[:, :1]], axis=1)
-    padded = jnp.pad(wrapped, ((1, 1), (0, 0)))
-    local = lax.dynamic_slice(padded, (row_index * CY, col_index * CX), (CY + 2, CX + 2))
+    wrapped = jnp.concatenate([column_depth[:, -2:], column_depth, column_depth[:, :2]], axis=1)
+    padded = jnp.pad(wrapped, ((2, 2), (0, 0)))
+    far = lax.dynamic_slice(padded, (row_index * CY, col_index * CX), (CY + 4, CX + 4))
+    local = far[1:-1, 1:-1]
+    gap = 4
+    wide_depth = jnp.concatenate(
+        [far[:, 2:], jnp.zeros((CY + 4, gap), jnp.int32), far[:, :2]], axis=1
+    )[..., None]
     depth = jnp.stack([local[1:-1, 1:-1], local[1:-1, 2:], local[1:-1, :-2], local[2:, 1:-1], local[:-2, 1:-1]])
     depth = depth[..., None]
     by_strip = (
@@ -753,12 +797,12 @@
     owner_row = lax.dynamic_index_in_dim(holder_rank, patch_index, 0, keepdims=False)
     side_index = comp_index.astype(jnp.int32)[None]
     comp = jnp.concatenate([side_index, owner_row])
-    ys = (row_index * CY + jnp.arange(CY, dtype=jnp.int32)).astype(jnp.float32)
+    ys = (row_index * CY - 1 + jnp.arange(CY + 2, dtype=jnp.int32)).astype(jnp.float32)
     coriolis = coriolis_scale * (2.0 * (ys + 0.5) / (CY * rows_mesh) - 1.0)
 
-    if half % 8:
+    if half % 8 or strip != CX:
         out = general(
-            linked, u0, v0, thermal_anomaly, tracers, depth, tracer_depth, holder_rank, patch_index, coriolis,
+            linked, u0, v0, thermal_anomaly, tracers, depth, tracer_depth, holder_rank, patch_index, coriolis[1:-1],
             biota_exchange_matrix, photic_absorb_share, chroma_loading,
         )
         return out.reshape(1, 2, 1, columns, levels)
@@ -777,17 +821,25 @@
     shares = times(weights, photic_absorb_share)
 
     projected, g = project(side_index, tracers, weights)
-    edges, projected, g = lax.optimization_barrier((edges, projected, g))
+    low, high, left, right = edges
+    north, south = exchange_rows(low, high)
+    left, right, projected, g = lax.optimization_barrier((left, right, projected, g))
     projected, g = in_vmem(projected), in_vmem(g)
-    halos0 = exchange_rows(edges[0], edges[1]) + exchange_cols(edges[2], edges[3])
+
+    outer = shape_of(4, 2, CY + 2, levels)
+    left, right = call(corner_kernel, side_index, (left, right, north, south), [None] * 4, (outer, outer), (), "corner")
+    east, west = exchange_cols(left, right)
     kept = first_tracer(side_index, projected, g, got, linked, tracer_depth, shares)
-    kept, halos0 = lax.optimization_barrier((kept, halos0))
+    kept, north, south, east, west = lax.optimization_barrier((kept, north, south, east, west))
     arrived = to_owners(kept)
 
-    speeds1, t1, r1, *edges = ocean(1, comp, coriolis, current_speeds, thermal_anomaly, halos0, depth, linked, got)
-    halos1 = exchange_rows(edges[0], edges[1]) + exchange_cols(edges[2], edges[3])
-    speeds1, t1, r1 = in_vmem(speeds1), in_vmem(t1), in_hbm(r1)
-    speeds2, t2, r2 = ocean(2, comp, coriolis, speeds1, t1, halos1, depth)
+    rim = shape_of(ring_places(CY, CX)[2], levels)
+    [own_ring] = call(ring_kernel, side_index, (north, south, east, west), [None] * 4, (rim,), (), "ring")
+    other_ring = swap(own_ring)
+    args = (current_speeds, thermal_anomaly, linked, got, north, south, east, west, own_ring, other_ring)
+    speeds1, wide_t1, t1, r1 = ocean(1, comp, coriolis, args, wide_depth, CY, CX)
+    r1 = in_hbm(r1)
+    speeds2, t2, r2 = ocean(2, comp, coriolis, (speeds1, wide_t1), wide_depth, CY, CX)
     arrived, speeds2, t2 = lax.optimization_barrier((arrived, speeds2, t2))
     speeds2, t2, r2 = in_hbm(speeds2), in_hbm(t2), in_hbm(r2)
 

time: 115 us -> 112 us (0.974)
  starting transfers between devices: 32.9 us -> 20.8 us
  local copies, waits for them, and re-layouts: 7.95 us -> 14.3 us
  Pallas kernels: 36.9 us -> 40.7 us
  waiting for transfers between devices: 35.3 us -> 33.3 us
    ppermute x2 -> x1, waiting for transfers between devices: 8.35 us -> 0.01 us  [exchange_cols(): east = lax.ppermute(low, 'px', [((i + 1) % count, i) for i in range(count)])]
    unnamed x48 -> x58, local copies, waits for them, and re-layouts: 6.7 us -> 11.9 us
    all_to_all x1, starting transfers between devices: 8.09 us -> 3.68 us  [shards(): lax.all_to_all(back.reshape(2 * patches, 2, half, levels), ('comp', 'py',...]
    ppermute x2 -> x3, waiting for transfers between devices: 18.7 us -> 22.4 us  [swap(): return lax.ppermute(block, 'comp', [(0, 1), (1, 0)])]
    all_to_all x1, waiting for transfers between devices: 0.01 us -> 3.33 us  [to_owners(): lax.all_to_all(blocks, ('py', 'px'), split_axis=0, concat_axis=0, tiled=T...]
    ppermute x2 -> x1, starting transfers between devices: 6.56 us -> 3.32 us  [exchange_cols(): east = lax.ppermute(low, 'px', [((i + 1) % count, i) for i in range(count)])]
    all_to_all x1, starting transfers between devices: 7.01 us -> 4.72 us  [to_owners(): lax.all_to_all(blocks, ('py', 'px'), split_axis=0, concat_axis=0, tiled=T...]
    pallas_call x2, Pallas kernels: 11.9 us -> 14 us  [ocean(): pl.pallas_call(functools.partial(ocean_kernel, advance), grid_spec=pltpu....]
  transfers between devices with their start and end apart: 16 -> 13, of which waited for: 5 -> 6; matrix products, arithmetic and copies ran while one was open for 2% -> 4% of each run, Pallas kernels for 24% -> 27%
where the time goes in v4:
time: 112 us; the launch traced here: 111 us
  Pallas kernels  40.7 us (36%)
  waiting for transfers between devices  33.3 us (30%)
  starting transfers between devices  20.8 us (19%)
  local copies, waits for them, and re-layouts  14.3 us (13%)
  other arithmetic  1.32 us (1%)
    ppermute x3, waiting for transfers between devices, swap(): return lax.ppermute(block, 'comp', [(0, 1), (1, 0)])  22.4 us
    pallas_call x7, Pallas kernels, call(): pl.pallas_call(kernel, grid_spec=pltpu.PrefetchScalarGridSpec(num_scalar_...  14.8 us
    pallas_call x2, Pallas kernels, ocean(): pl.pallas_call(functools.partial(ocean_kernel, advance), grid_spec=pltpu....  14 us
    unnamed x58, local copies, waits for them, and re-layouts  11.9 us
    pallas_call x1, Pallas kernels, project(): pl.pallas_call(project_kernel, grid_spec=pltpu.PrefetchScalarGridSpec(num...  4.95 us
    all_to_all x1, starting transfers between devices, to_owners(): lax.all_to_all(blocks, ('py', 'px'), split_axis=0, concat_axis=0, tiled=T...  4.72 us
    pallas_call x1, Pallas kernels, first_tracer(): pl.pallas_call(first_tracer_kernel, grid_spec=pltpu.PrefetchScalarGridSpe...  4.34 us
    ppermute x3, starting transfers between devices, swap(): return lax.ppermute(block, 'comp', [(0, 1), (1, 0)])  3.76 us
  transfers between devices with their start and end apart: 13, of which 6 were waited for; matrix products, arithmetic and copies ran while one was open for 4% of the time, Pallas kernels for 27%

profile of v4, /device:TPU:1, one launch (start us, length us, event | category | flops | bytes accessed | tf_op | source)
XLA Modules:
  0.0 111.3 jit_solution(3805365668514882639)
XLA Ops:
  0.0 2.7 %pack.1 = (f32[2,16,16,256]{3,2,1,0:T(8,128)}, f32[4,2,32,256]{3,2,1,0:T(8,128)}, f32[4,2,32,256]{3,2,1,0:T(8,128)}, f32[4,2,16,256]{3,2,1,0:T(8,128)}, f32[4,2,16,256]{3,2,1,0:T(8,128)}) custom-call(s32[1]{0:T(128)} %bitcast.sc, f32[2,16,32,256]{3,2,1,0:T(8,128)} %bitcast.53, f32[2,16,32,256]{3,2,1,0:T(8,128)} %refs_0_.1, f32[2,16,32,256]{3,2,1,0:T(8,128)} %refs_0_.1, ...), custom_call_target="tpu_custom_call" | custom-call | tf_op jit(solution)/shard_map/pack/pallas_call | solution.py:277
  2.7 2.0 %collective-permute-start = (f32[2,16,16,256]{3,2,1,0:T(8,128)}, f32[2,16,16,256]{3,2,1,0:T(8,128)S(1)}, u32[]{:S(2)}, u32[]{:S(2)}) collective-permute-start(f32[2,16,16,256]{3,2,1,0:T(8,128)} %get-tuple-element.49), channel_id=1, source_target_pairs={{0,16},{16,0},{1,17},{17,1},{2,18},{18,2},{3,19},{19,3},{4,20},{20... | collective-permute-start | bytes 1572872 | tf_op jit(solution)/shard_map/ppermute | solution.py:645
  4.7 1.0 collective-permute-start.1
  5.7 1.1 %collective-permute-start.2 = (f32[4,2,32,256]{3,2,1,0:T(8,128)}, f32[4,2,32,256]{3,2,1,0:T(8,128)S(1)}, u32[]{:S(2)}, u32[]{:S(2)}) collective-permute-start(f32[4,2,32,256]{3,2,1,0:T(8,128)} %get-tuple-element.51), channel_id=1, source_target_pairs={{0,4},{4,8},{8,12},{12,0},{1,5},{5,9},{9,13},{13,1},{2,6},{6,10},{... | collective-permute-start | bytes 786440 | tf_op jit(solution)/shard_map/ppermute | solution.py:612
  7.3 5.0 %project.1 = (f32[7,16,16,256]{3,2,1,0:T(8,128)S(1)}, f32[16,16,256]{2,1,0:T(8,128)S(1)}) custom-call(s32[1]{0:T(128)} %bitcast.sc, f32[16,16,32,256]{3,2,1,0:T(8,128)} %bitcast.56, f32[7,16]{1,0:T(8,128)S(1)} %stack.30.w_ref), custom_call_target="tpu_custom_call" | custom-call | tf_op jit(solution)/shard_map/project/pallas_call | solution.py:140
  13.2 1.0 fusion
  15.2 3.3 %collective-permute-start.3 = (f32[4,2,18,256]{3,2,1,0:T(8,128)}, f32[4,2,18,256]{3,2,1,0:T(8,128)S(1)}, u32[]{:S(2)}, u32[]{:S(2)}) collective-permute-start(f32[4,2,18,256]{3,2,1,0:T(8,128)} %get-tuple-element.54), channel_id=1, source_target_pairs={{1,0},{2,1},{3,2},{0,3},{5,4},{6,5},{7,6},{4,7},{9,8},{10,9},{11,1... | collective-permute-start | bytes 442376 | tf_op jit(solution)/shard_map/ppermute | solution.py:618
  18.9 1.0 copy-done.15
  19.9 4.3 %first_tracer.1 = f32[16,5,16,256]{3,2,1,0:T(8,128)} custom-call(s32[1]{0:T(128)} %bitcast.sc, f32[7,16,16,256]{3,2,1,0:T(8,128)S(1)} %get-tuple-element.47.y_ref, f32[16,16,256]{2,1,0:T(8,128)S(1)} %copy-done.15, f32[2,16,16,256]{3,2,1,0:T(8,128)S(1)} %collective-permute-done.got_ref.refs_3_, f32[2,16,32,256]{3,2,1,0:T(8,128)} %bitcast.54, ...), custom_call_target="tpu_custom_call" | custom-call | tf_op jit(solution)/shard_map/first_tracer/pallas_call | solution.py:187
  24.2 3.7 %collective-permute-done.4.west_ref.refs_7_ = f32[4,2,18,256]{3,2,1,0:T(8,128)S(1)} collective-permute-done((f32[4,2,18,256]{3,2,1,0:T(8,128)}, f32[4,2,18,256]{3,2,1,0:T(8,128)S(1)}, u32[]{:S(2)}, u32[]{:S(2)}) %collective-permute-start.4) | collective-permute-done | bytes 147488 | tf_op jit(solution)/shard_map/ppermute | solution.py:619
  28.6 4.7 %all-to-all-start = ((f32[16,5,16,256]{3,2,1,0:T(8,128)}), f32[16,5,16,256]{3,2,1,0:T(8,128)S(1)}, u32[]{:S(2)}, u32[]{:S(2)}) async-start(f32[16,5,16,256]{3,2,1,0:T(8,128)} %first_tracer.1), calls=%async_computation | async-start | bytes 2621440 | tf_op jit(solution)/shard_map/all_to_all | solution.py:641
  34.2 0.9 copy-done.7
  36.9 3.8 %collective-permute-done.5.refs_9_ = f32[112,256]{1,0:T(8,128)} collective-permute-done((f32[112,256]{1,0:T(8,128)}, f32[112,256]{1,0:T(8,128)}, u32[]{:S(2)}, u32[]{:S(2)}) %collective-permute-start.5) | collective-permute-done | bytes 114720 | tf_op jit(solution)/shard_map/ppermute | solution.py:645
  40.7 0.9 copy-done.3
  41.7 1.0 copy-done.5
  43.6 8.5 %ocean1.1 = (f32[2,18,40,256]{3,2,1,0:T(8,128)S(1)}, f32[18,40,256]{2,1,0:T(8,128)S(1)}, f32[16,32,256]{2,1,0:T(8,128)S(1)}, f32[16,32,256]{2,1,0:T(8,128)S(1)}) custom-call(s32[17]{0:T(128)S(1)} %pad_add_fusion.1.sc, f32[18]{0:T(128)S(1)} %multiply_add_fusion.coriolis_ref, f32[2,16,32,256]{3,2,1,0:T(8,128)} %refs_0_.1, f32[16,32,256]{2,1,0:T(8,128)} %refs_1_.1, ...), custom_call_target="tpu_custom_call" | custom-call | tf_op jit(solution)/shard_map/ocean1/pallas_call | solution.py:442
  53.7 5.5 %ocean2.1 = (f32[2,16,32,256]{3,2,1,0:T(8,128)S(1)}, f32[16,32,256]{2,1,0:T(8,128)S(1)}, f32[16,32,256]{2,1,0:T(8,128)S(1)}) custom-call(s32[17]{0:T(128)S(1)} %pad_add_fusion.1.sc, f32[18]{0:T(128)S(1)} %multiply_add_fusion.coriolis_ref, f32[2,18,40,256]{3,2,1,0:T(8,128)S(1)} %get-tuple-element.61.refs_0_, f32[18,40,256]{2,1,0:T(8,128)S(1)} %get-tuple-element.62.refs_1_, ...), custom_call_target="tpu_custom_call" | custom-call | tf_op jit(solution)/shard_map/ocean2/pallas_call | solution.py:442
  59.2 1.0 copy-done.1
  61.8 3.3 %all-to-all-done.y_hbm.y_ref = f32[16,5,16,256]{3,2,1,0:T(8,128)S(1)} async-done(((f32[16,5,16,256]{3,2,1,0:T(8,128)}), f32[16,5,16,256]{3,2,1,0:T(8,128)S(1)}, u32[]{:S(2)}, u32[]{:S(2)}) %all-to-all-start) | async-done | bytes 1310752 | tf_op jit(solution)/shard_map/all_to_all | solution.py:641
  65.1 2.4 %absorb.1 = (f32[16,16,256]{2,1,0:T(8,128)S(1)}, f32[16,16,256]{2,1,0:T(8,128)S(1)}, f32[3,16,256]{2,1,0:T(8,128)S(1)}, f32[3,16,256]{2,1,0:T(8,128)S(1)}, f32[3...) custom-call(s32[17]{0:T(128)S(1)} %pad_add_fusion.1.sc, f32[16,5,16,256]{3,2,1,0:T(8,128)S(1)} %all-to-all-done.y_hbm.y_ref, ...), custom_call_target="tpu_custom_call" | custom-call | tf_op jit(solution)/shard_map/absorb/pallas_call | solution.py:594
  69.4 1.0 collective-permute-start.8
  70.9 3.0 %second.1 = (f32[16,16,256]{2,1,0:T(8,128)S(1)}, f32[16,16,256]{2,1,0:T(8,128)S(1)}, f32[16,16,256]{2,1,0:T(8,128)S(1)}, f32[16,16,256]{2,1,0:T(8,128)S(1)}) custom-call(s32[17]{0:T(128)S(1)} %pad_add_fusion.1.sc, f32[16,5,16,256]{3,2,1,0:T(8,128)S(1)} %all-to-all-done.y_hbm.y_ref, f32[16,16,256]{2,1,0:T(8,128)S(1)} %get-tuple-element.68.irr_ref, ...), custom_call_target="tpu_custom_call" | custom-call | tf_op jit(solution)/shard_map/second/pallas_call | solution.py:594
  73.9 2.1 %collective-permute-done.9.west_ref = f32[3,16,256]{2,1,0:T(8,128)S(1)} collective-permute-done((f32[3,16,256]{2,1,0:T(8,128)S(1)}, f32[3,16,256]{2,1,0:T(8,128)S(1)}, u32[]{:S(2)}, u32[]{:S(2)}) %collective-permute-start.9) | collective-permute-done | bytes 49184 | tf_op jit(solution)/shard_map/ppermute | solution.py:628
  76.0 3.5 %last_ocean.1 = f32[2,16,2,16,256]{4,3,2,1,0:T(8,128)} custom-call(s32[17]{0:T(128)S(1)} %pad_add_fusion.1.sc, f32[2,16,32,256]{3,2,1,0:T(8,128)} %copy-done.1, f32[16,16,256]{2,1,0:T(8,128)S(1)} %get-tuple-element.74.t2_ref.t_ref, f32[3,16,256]{2,1,0:T(8,128)S(1)} %collective-permute-done.6.north_ref, f32[3,16,256]{2,1,0:T(8,128)S(1)} %collective-permute-done.7.south_ref, ...), custom_call_target="tpu_custom_call" | custom-call | tf_op jit(solution)/shard_map/last_ocean/pallas_call | solution.py:594
  79.5 3.7 %all-to-all-start.1 = ((f32[32,2,16,256]{3,2,1,0:T(8,128)}), f32[32,2,16,256]{3,2,1,0:T(8,128)S(1)}, u32[]{:S(2)}, u32[]{:S(2)}) async-start(f32[32,2,16,256]{3,2,1,0:T(8,128)} %bitcast.18), calls=%async_computation.1 | async-start | bytes 2097152 | tf_op jit(solution)/shard_map/all_to_all | solution.py:869
  83.2 0.9 copy-done.17
  84.1 0.9 copy-done.19
  85.1 2.7 %third.1.absorbed_ref = f32[16,2,16,256]{3,2,1,0:T(8,128)S(1)} custom-call(s32[17]{0:T(128)S(1)} %pad_add_fusion.1.sc, f32[16,16,256]{2,1,0:T(8,128)S(1)} %get-tuple-element.71.a_ref, f32[16,16,256]{2,1,0:T(8,128)S(1)} %copy-done.17, f32[16,16,256]{2,1,0:T(8,128)S(1)} %copy-done.19, f32[16,16,256]{2,1,0:T(8,128)S(1)} %get-tuple-element.74.t2_ref.t_ref, ...), custom_call_target="tpu_custom_call" | custom-call | tf_op jit(solution)/shard_map/third/pallas_call | solution.py:594
  87.8 1.5 %collective-permute-start.10 = (f32[16,2,16,256]{3,2,1,0:T(8,128)S(1)}, f32[16,2,16,256]{3,2,1,0:T(8,128)S(1)}, u32[]{:S(2)}, u32[]{:S(2)}) collective-permute-start(f32[16,2,16,256]{3,2,1,0:T(8,128)S(1)} %third.1.absorbed_ref), channel_id=1, source_target_pairs={{0,16},{16,0},{1,17},{17,1},{2,18},{18,2},{3,19},{19,3},{4,20},{20... | collective-permute-start | bytes 1572872 | tf_op jit(solution)/shard_map/ppermute | solution.py:645
  89.3 18.6 %collective-permute-done.10.other_ref = f32[16,2,16,256]{3,2,1,0:T(8,128)S(1)} collective-permute-done((f32[16,2,16,256]{3,2,1,0:T(8,128)S(1)}, f32[16,2,16,256]{3,2,1,0:T(8,128)S(1)}, u32[]{:S(2)}, u32[]{:S(2)}) %collective-permute-start.10) | collective-permute-done | bytes 524320 | tf_op jit(solution)/shard_map/ppermute | solution.py:645
  107.9 1.8 %all-to-all-done.1 = f32[32,2,16,256]{3,2,1,0:T(8,128)S(1)} async-done(((f32[32,2,16,256]{3,2,1,0:T(8,128)}), f32[32,2,16,256]{3,2,1,0:T(8,128)S(1)}, u32[]{:S(2)}, u32[]{:S(2)}) %all-to-all-start.1) | async-done | bytes 1048608 | tf_op jit(solution)/shard_map/all_to_all | solution.py:869
  109.7 1.6 %join.1 = f32[2,16,32,256]{3,2,1,0:T(8,128)} custom-call(s32[17]{0:T(128)S(1)} %pad_add_fusion.1.sc, f32[16,2,16,256]{3,2,1,0:T(8,128)S(1)} %third.1.absorbed_ref, f32[2,16,2,16,256]{4,3,2,1,0:T(8,128)S(1)} %bitcast.52, f32[16,2,16,256]{3,2,1,0:T(8,128)S(1)} %collective-permute-done.10.other_ref), custom_call_target="tpu_custom_call" | custom-call | tf_op jit(solution)/shard_map/join/pallas_call | solution.py:594
  (91 shorter events, 12.4 us)
Async XLA Ops:
  0.0 6.8 %copy-start = (f32[16,16]{1,0:T(8,128)S(1)}, f32[16,16]{1,0:T(8,128)}, u32[]{:S(2)}) copy-start(f32[16,16]{1,0:T(8,128)} %param.17) | copy-start | bytes 3076
  0.0 6.8 %copy-start.25 = (f32[16]{0:T(128)S(1)}, f32[16]{0:T(128)}, u32[]{:S(2)}) copy-start(f32[16]{0:T(128)} %param.19) | copy-start | bytes 196
  2.7 16.2 %collective-permute-start = (f32[2,16,16,256]{3,2,1,0:T(8,128)}, f32[2,16,16,256]{3,2,1,0:T(8,128)S(1)}, u32[]{:S(2)}, u32[]{:S(2)}) collective-permute-start(f32[2,16,16,256]{3,2,1,0:T(8,128)} %get-tuple-element.49), channel_id=1, source_target_pairs={{0,16},{16,0},{1,17},{17,1},{2,18},{18,2},{3,19},{19,3},{4,20},{20... | collective-permute-start | bytes 1572872 | tf_op jit(solution)/shard_map/ppermute | solution.py:645
  4.7 9.6 %collective-permute-start.1 = (f32[4,2,32,256]{3,2,1,0:T(8,128)}, f32[4,2,32,256]{3,2,1,0:T(8,128)S(1)}, u32[]{:S(2)}, u32[]{:S(2)}) collective-permute-start(f32[4,2,32,256]{3,2,1,0:T(8,128)} %get-tuple-element.50), channel_id=1, source_target_pairs={{4,0},{8,4},{12,8},{0,12},{5,1},{9,5},{13,9},{1,13},{6,2},{10,6},{... | collective-permute-start | bytes 786440 | tf_op jit(solution)/shard_map/ppermute | solution.py:611
  5.7 8.6 %collective-permute-start.2 = (f32[4,2,32,256]{3,2,1,0:T(8,128)}, f32[4,2,32,256]{3,2,1,0:T(8,128)S(1)}, u32[]{:S(2)}, u32[]{:S(2)}) collective-permute-start(f32[4,2,32,256]{3,2,1,0:T(8,128)} %get-tuple-element.51), channel_id=1, source_target_pairs={{0,4},{4,8},{8,12},{12,0},{1,5},{5,9},{9,13},{13,1},{2,6},{6,10},{... | collective-permute-start | bytes 786440 | tf_op jit(solution)/shard_map/ppermute | solution.py:612
  7.3 5.0 %copy-start.22 = (s32[64,128]{1,0:T(8,128)S(1)}, s32[64,128]{1,0:T(8,128)}, u32[]{:S(2)}) copy-start(s32[64,128]{1,0:T(8,128)} %param.14) | copy-start | bytes 98308
  7.3 5.0 %copy-start.23 = (s32[64,128]{1,0:T(8,128)S(1)}, s32[64,128]{1,0:T(8,128)}, u32[]{:S(2)}) copy-start(s32[64,128]{1,0:T(8,128)} %param.15) | copy-start | bytes 98308
  7.3 5.8 %copy-start.24 = (s32[16,16]{1,0:T(8,128)S(1)}, s32[16,16]{1,0:T(8,128)}, u32[]{:S(2)}) copy-start(s32[16,16]{1,0:T(8,128)} %param.16) | copy-start | bytes 3076
  7.3 7.0 %copy-start.20 = (f32[4,2,16,256]{3,2,1,0:T(8,128)S(1)}, f32[4,2,16,256]{3,2,1,0:T(8,128)}, u32[]{:S(2)}) copy-start(f32[4,2,16,256]{3,2,1,0:T(8,128)} %get-tuple-element.52.left_ref) | copy-start | bytes 393220
  7.3 7.0 %copy-start.21 = (f32[4,2,16,256]{3,2,1,0:T(8,128)S(1)}, f32[4,2,16,256]{3,2,1,0:T(8,128)}, u32[]{:S(2)}) copy-start(f32[4,2,16,256]{3,2,1,0:T(8,128)} %get-tuple-element.53.right_ref) | copy-start | bytes 393220
  7.3 11.4 %copy-start.26 = (f32[16]{0:T(128)S(1)}, f32[16]{0:T(128)}, u32[]{:S(2)}) copy-start(f32[16]{0:T(128)} %param.18) | copy-start | bytes 196
  12.3 6.2 %copy-start.14 = (f32[16,16,256]{2,1,0:T(8,128)}, f32[16,16,256]{2,1,0:T(8,128)S(1)}, u32[]{:S(2)}) copy-start(f32[16,16,256]{2,1,0:T(8,128)S(1)} %get-tuple-element.48.g_ref) | copy-start | bytes 786436
  14.3 19.9 %copy-start.2 = (f32[4,2,32,256]{3,2,1,0:T(8,128)}, f32[4,2,32,256]{3,2,1,0:T(8,128)S(1)}, u32[]{:S(2)}) copy-start(f32[4,2,32,256]{3,2,1,0:T(8,128)S(1)} %collective-permute-done.2.south_ref.refs_5_) | copy-start | bytes 786436
  15.2 9.0 %collective-permute-start.3 = (f32[4,2,18,256]{3,2,1,0:T(8,128)}, f32[4,2,18,256]{3,2,1,0:T(8,128)S(1)}, u32[]{:S(2)}, u32[]{:S(2)}) collective-permute-start(f32[4,2,18,256]{3,2,1,0:T(8,128)} %get-tuple-element.54), channel_id=1, source_target_pairs={{1,0},{2,1},{3,2},{0,3},{5,4},{6,5},{7,6},{4,7},{9,8},{10,9},{11,1... | collective-permute-start | bytes 442376 | tf_op jit(solution)/shard_map/ppermute | solution.py:618
  18.5 9.4 %collective-permute-start.4 = (f32[4,2,18,256]{3,2,1,0:T(8,128)}, f32[4,2,18,256]{3,2,1,0:T(8,128)S(1)}, u32[]{:S(2)}, u32[]{:S(2)}) collective-permute-start(f32[4,2,18,256]{3,2,1,0:T(8,128)} %get-tuple-element.55), channel_id=1, source_target_pairs={{0,1},{1,2},{2,3},{3,0},{4,5},{5,6},{6,7},{7,4},{8,9},{9,10},{10,1... | collective-permute-start | bytes 442376 | tf_op jit(solution)/shard_map/ppermute | solution.py:619
  18.9 1.0 copy-start.15
  19.9 4.3 %copy-start.4 = (f32[2,16,16,256]{3,2,1,0:T(8,128)}, f32[2,16,16,256]{3,2,1,0:T(8,128)S(1)}, u32[]{:S(2)}) copy-start(f32[2,16,16,256]{3,2,1,0:T(8,128)S(1)} %collective-permute-done.got_ref.refs_3_) | copy-start | bytes 1572868
  28.6 36.6 %all-to-all-start = ((f32[16,5,16,256]{3,2,1,0:T(8,128)}), f32[16,5,16,256]{3,2,1,0:T(8,128)S(1)}, u32[]{:S(2)}, u32[]{:S(2)}) async-start(f32[16,5,16,256]{3,2,1,0:T(8,128)} %first_tracer.1), calls=%async_computation | async-start | bytes 2621440 | tf_op jit(solution)/shard_map/all_to_all | solution.py:641
  35.8 4.9 %collective-permute-start.5 = (f32[112,256]{1,0:T(8,128)}, f32[112,256]{1,0:T(8,128)}, u32[]{:S(2)}, u32[]{:S(2)}) collective-permute-start(f32[112,256]{1,0:T(8,128)} %ring.1.refs_8_), channel_id=1, source_target_pairs={{0,16},{16,0},{1,17},{17,1},{2,18},{18,2},{3,19},{19,3},{4,20},{20... | collective-permute-start | bytes 344072 | tf_op jit(solution)/shard_map/ppermute | solution.py:645
  40.7 1.0 copy-start.3
  41.7 1.0 copy-start.5
  59.2 1.0 copy-start.1
  65.1 5.7 %copy-start.11 = (f32[16,32,256]{2,1,0:T(8,128)S(1)}, f32[16,32,256]{2,1,0:T(8,128)}, u32[]{:S(2)}) copy-start(f32[16,32,256]{2,1,0:T(8,128)} %copy-done.10) | copy-start | bytes 1572868
  67.6 6.3 %collective-permute-start.6 = (f32[3,16,256]{2,1,0:T(8,128)S(1)}, f32[3,16,256]{2,1,0:T(8,128)S(1)}, u32[]{:S(2)}, u32[]{:S(2)}) collective-permute-start(f32[3,16,256]{2,1,0:T(8,128)S(1)} %get-tuple-element.76), channel_id=1, source_target_pairs={{4,0},{8,4},{12,8},{0,12},{5,1},{9,5},{13,9},{1,13},{6,2},{10,6},{... | collective-permute-start | bytes 147464 | tf_op jit(solution)/shard_map/ppermute | solution.py:611
  68.5 5.4 %collective-permute-start.7 = (f32[3,16,256]{2,1,0:T(8,128)S(1)}, f32[3,16,256]{2,1,0:T(8,128)S(1)}, u32[]{:S(2)}, u32[]{:S(2)}) collective-permute-start(f32[3,16,256]{2,1,0:T(8,128)S(1)} %get-tuple-element.77), channel_id=1, source_target_pairs={{0,4},{4,8},{8,12},{12,0},{1,5},{5,9},{9,13},{13,1},{2,6},{6,10},{... | collective-permute-start | bytes 147464 | tf_op jit(solution)/shard_map/ppermute | solution.py:612
  69.4 4.5 %collective-permute-start.8 = (f32[3,16,256]{2,1,0:T(8,128)S(1)}, f32[3,16,256]{2,1,0:T(8,128)S(1)}, u32[]{:S(2)}, u32[]{:S(2)}) collective-permute-start(f32[3,16,256]{2,1,0:T(8,128)S(1)} %get-tuple-element.78), channel_id=1, source_target_pairs={{16,0},{1,16},{17,1},{2,17},{18,2},{3,18},{19,3},{0,19},{20,4},{5,... | collective-permute-start | bytes 147464 | tf_op jit(solution)/shard_map/ppermute | solution.py:627
  70.4 5.6 %collective-permute-start.9 = (f32[3,16,256]{2,1,0:T(8,128)S(1)}, f32[3,16,256]{2,1,0:T(8,128)S(1)}, u32[]{:S(2)}, u32[]{:S(2)}) collective-permute-start(f32[3,16,256]{2,1,0:T(8,128)S(1)} %get-tuple-element.79), channel_id=1, source_target_pairs={{0,16},{16,1},{1,17},{17,2},{2,18},{18,3},{3,19},{19,0},{4,20},{20... | collective-permute-start | bytes 147464 | tf_op jit(solution)/shard_map/ppermute | solution.py:628
  73.9 5.6 %copy-start.16 = (f32[16,16,256]{2,1,0:T(8,128)}, f32[16,16,256]{2,1,0:T(8,128)S(1)}, u32[]{:S(2)}) copy-start(f32[16,16,256]{2,1,0:T(8,128)S(1)} %get-tuple-element.72.b_ref) | copy-start | bytes 786436
  73.9 5.6 %copy-start.18 = (f32[16,16,256]{2,1,0:T(8,128)}, f32[16,16,256]{2,1,0:T(8,128)S(1)}, u32[]{:S(2)}) copy-start(f32[16,16,256]{2,1,0:T(8,128)S(1)} %get-tuple-element.73.g_ref) | copy-start | bytes 786436
  79.5 30.2 %all-to-all-start.1 = ((f32[32,2,16,256]{3,2,1,0:T(8,128)}), f32[32,2,16,256]{3,2,1,0:T(8,128)S(1)}, u32[]{:S(2)}, u32[]{:S(2)}) async-start(f32[32,2,16,256]{3,2,1,0:T(8,128)} %bitcast.18), calls=%async_computation.1 | async-start | bytes 2097152 | tf_op jit(solution)/shard_map/all_to_all | solution.py:869
  83.2 1.0 copy-start.17
  87.8 20.0 %collective-permute-start.10 = (f32[16,2,16,256]{3,2,1,0:T(8,128)S(1)}, f32[16,2,16,256]{3,2,1,0:T(8,128)S(1)}, u32[]{:S(2)}, u32[]{:S(2)}) collective-permute-start(f32[16,2,16,256]{3,2,1,0:T(8,128)S(1)} %third.1.absorbed_ref), channel_id=1, source_target_pairs={{0,16},{16,0},{1,17},{17,1},{2,18},{18,2},{3,19},{19,3},{4,20},{20... | collective-permute-start | bytes 1572872 | tf_op jit(solution)/shard_map/ppermute | solution.py:645
  (8 other events, 6.7 us)

commit v5 on v4

--- a/solution.py
+++ b/solution.py
@@ -206,7 +206,7 @@
 
 
 def pack_kernel(sc, linked_ref, row0_ref, row1_ref, col0_ref, col1_ref, t0_ref, t1_ref, tc0_ref, tc1_ref,
-                sent_ref, low_ref, high_ref, left_ref, right_ref):
+                sent_ref, low_ref, high_ref, left_ref, right_ref, first_ref):
     _, strips, strip, levels = linked_ref.shape
     half = strip // 2
 
@@ -230,6 +230,7 @@
         right_ref[2, i] = tc1_ref[:, last - 2 + i]
         left_ref[3, i] = linked_ref[0, :, i] + linked_ref[1, :, i]
         right_ref[3, i] = linked_ref[0, :, strip - 2 + i] + linked_ref[1, :, strip - 2 + i]
+    first_ref[...] = left_ref[3, 0]
     for f in range(2):
         low_ref[f] = row0_ref[f]
         high_ref[f] = row1_ref[f]
@@ -239,31 +240,29 @@
     high_ref[3] = linked_ref[0, tall:] + linked_ref[1, tall:]
 
 
-def corner_kernel(sc, left_ref, right_ref, north_ref, south_ref, low_ref, high_ref):
+def corner_kernel(sc, left_ref, right_ref, north_ref, south_ref, out_ref):
     rows = left_ref.shape[2]
     cols = north_ref.shape[2]
-    for source, target, at in ((left_ref, low_ref, 0), (right_ref, high_ref, cols - 2)):
+
+    def fill(source, at):
         for f in range(source.shape[0]):
             for i in range(2):
-                target[f, i, :rows] = source[f, i]
-                target[f, i, rows : rows + 1] = south_ref[f, 1, at + i : at + i + 1]
-                target[f, i, rows + 1 :] = north_ref[f, 0, at + i : at + i + 1]
-
-
-def ring_places(rows, cols):
-    tall = -(-(rows + 2) // 8) * 8
-    return 2 * cols, 2 * cols + tall, 2 * cols + 2 * tall
-
-
-def ring_kernel(sc, north_ref, south_ref, east_ref, west_ref, ring_ref):
-    cols = north_ref.shape[2]
-    tall = east_ref.shape[2]
-    at_east, at_west, _ = ring_places(tall - 2, cols)
-    ring_ref[...] = jnp.zeros(ring_ref.shape, jnp.float32)
-    ring_ref[:cols] = south_ref[3, 1]
-    ring_ref[cols : 2 * cols] = north_ref[3, 0]
-    ring_ref[at_east : at_east + tall] = east_ref[3, 0]
-    ring_ref[at_west : at_west + tall] = west_ref[3, 1]
+                out_ref[f, i, :rows] = source[f, i]
+                out_ref[f, i, rows : rows + 1] = south_ref[f, 1, at + i : at + i + 1]
+                out_ref[f, i, rows + 1 :] = north_ref[f, 0, at + i : at + i + 1]
+
+    @pl.when(sc[0] == 0)
+    def _():
+        fill(right_ref, cols - 2)
+
+    @pl.when(sc[0] != 0)
+    def _():
+        fill(left_ref, 0)
+
+
+def ring_kernel(sc, north_ref, south_ref, ring_ref):
+    ring_ref[0] = south_ref[3, 1]
+    ring_ref[1] = north_ref[3, 0]
 
 
 def pack(comp, linked, speeds, heat):
@@ -271,7 +270,7 @@
     rows, cols, _ = heat.shape
     outs = (
         shape_of(2, strips, strip // 2, levels), shape_of(4, 2, cols, levels), shape_of(4, 2, cols, levels),
-        shape_of(4, 2, rows, levels), shape_of(4, 2, rows, levels),
+        shape_of(4, 2, rows, levels), shape_of(4, 2, rows, levels), shape_of(rows, levels),
     )
     edge = min(8, cols)
     return pl.pallas_call(
@@ -298,55 +297,61 @@
     )(comp, linked, speeds, speeds, speeds, speeds, heat, heat, heat, heat)
 
 
-def wide_rows(speed_hbm, heat_hbm, linked_hbm, got_ref, north_ref, south_ref, east_ref, west_ref, own_ref, other_ref,
-              first, x_ref, absorb_ref, ring_absorb_ref, linked_ref, sems):
+def wide_rows(sc, speed_hbm, heat_hbm, linked_hbm, got_ref, north_ref, south_ref, side_ref, edge_ref, ring_ref,
+              x_ref, near_ref, absorb_ref, linked_ref, sems):
     rows, cols, levels = heat_hbm.shape
+    half = cols // 2
+    comp = sc[0]
+    first = comp == 0
     width = x_ref.shape[2]
-    inner = (pl.ds(2, rows), pl.ds(0, cols))
-    copies = [
-        pltpu.make_async_copy(linked_hbm, linked_ref, sems.at[0]),
-        pltpu.make_async_copy(heat_hbm, x_ref.at[2, *inner], sems.at[1]),
-        pltpu.make_async_copy(speed_hbm.at[0], x_ref.at[0, *inner], sems.at[2]),
-        pltpu.make_async_copy(speed_hbm.at[1], x_ref.at[1, *inner], sems.at[3]),
-    ]
+    rim = width - half
+    own = pl.ds(pl.multiple_of(comp * half, half), half)
+    near = pl.ds(pl.multiple_of(half - rim * comp, 8), rim)
+    copies = [pltpu.make_async_copy(linked_hbm, linked_ref, sems.at[0])]
+    for f, source in enumerate((speed_hbm.at[0], speed_hbm.at[1], heat_hbm)):
+        copies.append(
+            pltpu.make_async_copy(source.at[:, own], x_ref.at[f, pl.ds(2, rows), pl.ds(0, half)], sems.at[1 + f])
+        )
+        copies.append(pltpu.make_async_copy(source.at[:, near], near_ref.at[f], sems.at[4 + f]))
     for copy in copies:
         copy.start()
-    place = lax.broadcasted_iota(jnp.int32, (width - cols, levels), 0)
-    none = jnp.zeros((width - cols, levels), jnp.float32)
-    line = [rows, *range(rows), rows + 1]
+    place = lax.broadcasted_iota(jnp.int32, (rim, levels), 0)
+    none = jnp.zeros((rim, levels), jnp.float32)
+    far_place = (1 - comp) * (rim - 2)
+    for copy in copies:
+        copy.wait()
     for f in range(3):
-        x_ref[f, :2, :cols] = south_ref[f]
-        x_ref[f, rows + 2 :, :cols] = north_ref[f]
-        x_ref[f, 0, cols:] = none
-        x_ref[f, rows + 3, cols:] = none
-        for o, r in enumerate(line):
-            cells = none
+        x_ref[f, :2, :half] = south_ref[f, :, own]
+        x_ref[f, rows + 2 :, :half] = north_ref[f, :, own]
+        x_ref[f, 0, half:] = none
+        x_ref[f, rows + 3, half:] = none
+        for o in range(rows + 2):
+            if o == 0:
+                r, cells = rows, south_ref[f, 1, near]
+            elif o == rows + 1:
+                r, cells = rows + 1, north_ref[f, 0, near]
+            else:
+                r, cells = o - 1, near_ref[f, o - 1]
             for i in range(2):
-                cells = jnp.where(place == i, east_ref[f, i, r : r + 1], cells)
-                cells = jnp.where(place == width - cols - 2 + i, west_ref[f, i, r : r + 1], cells)
-            x_ref[f, o + 1, cols:] = cells
-    ring_absorb_ref[...] = jnp.where(first, own_ref[...], other_ref[...])
-    absorb_ref[0, :cols] = ring_absorb_ref[:cols]
-    absorb_ref[rows + 1, :cols] = ring_absorb_ref[cols : 2 * cols]
-    at_east, at_west, _ = ring_places(rows, cols)
-    for o, r in enumerate(line):
-        e = ring_absorb_ref[at_east + r : at_east + r + 1]
-        w = ring_absorb_ref[at_west + r : at_west + r + 1]
-        absorb_ref[o, cols:] = jnp.where(place == 0, e, jnp.where(place == width - cols - 1, w, 0.0))
-    copies[0].wait()
+                cells = jnp.where(place == far_place + i, side_ref[f, i, r : r + 1], cells)
+            x_ref[f, o + 1, half:] = cells
+    for o, side in ((0, 0), (rows + 1, 1)):
+        here = (south_ref[3, 1] if side == 0 else north_ref[3, 0])[:half]
+        absorb_ref[o, :half] = jnp.where(first, here, ring_ref[side, half:])
+        absorb_ref[o, half:] = none
     for y in range(rows):
-        absorb_ref[y + 1, :cols] = jnp.where(
-            first, linked_ref[0, y] + linked_ref[1, y], jnp.concatenate([got_ref[0, y], got_ref[1, y]], axis=0)
-        )
-    for copy in copies[1:]:
-        copy.wait()
+        both = linked_ref[0, y] + linked_ref[1, y]
+        absorb_ref[y + 1, :half] = jnp.where(first, both[:half], got_ref[1, y])
+        cells = jnp.where(first, both[half : half + rim], got_ref[0, y, half - rim :])
+        far = jnp.where(first, side_ref[3, 1, y : y + 1], edge_ref[y : y + 1])
+        absorb_ref[y + 1, half:] = jnp.where(place == (1 - comp) * (rim - 1), far, cells)
 
 
 def ocean_kernel(advance, sc, coriolis_ref, *refs):
     if advance == 1:
-        *sources, depth_ref, next_ref, tn_ref, inner_ref, rise_ref, x_ref, absorb_ref = refs[: -5]
-        ring_absorb_ref, linked_ref, sems, p_ref, div_ref = refs[-5:]
-        wide_rows(*sources, sc[0] == 0, x_ref, absorb_ref, ring_absorb_ref, linked_ref, sems)
+        *sources, depth_ref, next_ref, tn_ref, inner_ref, rise_ref, x_ref, near_ref, absorb_ref = refs[:-4]
+        linked_ref, sems, p_ref, div_ref = refs[-4:]
+        wide_rows(sc, *sources, x_ref, near_ref, absorb_ref, linked_ref, sems)
         fields = [x_ref.at[f] for f in range(3)]
     else:
         speed_ref, t_ref, depth_ref, next_ref, tn_ref, rise_ref, p_ref, div_ref = refs
@@ -425,10 +430,10 @@
         outs = (shape_of(2, rows + 2, width, levels), shape_of(rows + 2, width, levels), patch, patch)
         scratch = [
             pltpu.VMEM((3, tall, width, levels), jnp.float32),
+            pltpu.VMEM((3, rows, width - cols, levels), jnp.float32),
             pltpu.VMEM((rows + 2, width, levels), jnp.float32),
-            pltpu.VMEM(args[-1].shape, jnp.float32),
             pltpu.VMEM(args[2].shape, jnp.float32),
-            pltpu.SemaphoreType.DMA((4,)),
+            pltpu.SemaphoreType.DMA((7,)),
         ]
     else:
         tall = rows + 2
@@ -620,6 +625,18 @@
     return east, west
 
 
+def far_columns(block):
+    count = lax.axis_size("px")
+    east = [(i, (i + 1) % count) for i in range(count)]
+    west = [(count + (i + 1) % count, count + i) for i in range(count)]
+    return lax.ppermute(block, ("comp", "px"), east + west)
+
+
+def east_column(block):
+    count = lax.axis_size("px")
+    return lax.ppermute(block, ("comp", "px"), [((i + 1) % count, count + i) for i in range(count)])
+
+
 def exchange_half_cols(low, high):
     count = lax.axis_size("px")
     line = [(h % 2) * count + h // 2 for h in range(2 * count)]
@@ -783,8 +800,9 @@
     far = lax.dynamic_slice(padded, (row_index * CY, col_index * CX), (CY + 4, CX + 4))
     local = far[1:-1, 1:-1]
     gap = 4
+    near = lax.dynamic_slice_in_dim(far, comp_index * half, half + 4, 1)
     wide_depth = jnp.concatenate(
-        [far[:, 2:], jnp.zeros((CY + 4, gap), jnp.int32), far[:, :2]], axis=1
+        [near[:, 2:], jnp.zeros((CY + 4, gap), jnp.int32), near[:, :2]], axis=1
     )[..., None]
     depth = jnp.stack([local[1:-1, 1:-1], local[1:-1, 2:], local[1:-1, :-2], local[2:, 1:-1], local[:-2, 1:-1]])
     depth = depth[..., None]
@@ -821,30 +839,26 @@
     shares = times(weights, photic_absorb_share)
 
     projected, g = project(side_index, tracers, weights)
-    low, high, left, right = edges
+    low, high, left, right, first_column = edges
     north, south = exchange_rows(low, high)
+    edge = east_column(first_column)
     left, right, projected, g = lax.optimization_barrier((left, right, projected, g))
     projected, g = in_vmem(projected), in_vmem(g)
-
     outer = shape_of(4, 2, CY + 2, levels)
-    left, right = call(corner_kernel, side_index, (left, right, north, south), [None] * 4, (outer, outer), (), "corner")
-    east, west = exchange_cols(left, right)
+    [sides] = call(corner_kernel, side_index, (left, right, north, south), [None] * 4, (outer,), (), "corner")
+    sides = far_columns(sides)
     kept = first_tracer(side_index, projected, g, got, linked, tracer_depth, shares)
-    kept, north, south, east, west = lax.optimization_barrier((kept, north, south, east, west))
+    kept, north, south, sides, edge = lax.optimization_barrier((kept, north, south, sides, edge))
     arrived = to_owners(kept)
 
-    rim = shape_of(ring_places(CY, CX)[2], levels)
-    [own_ring] = call(ring_kernel, side_index, (north, south, east, west), [None] * 4, (rim,), (), "ring")
-    other_ring = swap(own_ring)
-    args = (current_speeds, thermal_anomaly, linked, got, north, south, east, west, own_ring, other_ring)
-    speeds1, wide_t1, t1, r1 = ocean(1, comp, coriolis, args, wide_depth, CY, CX)
+    [ring] = call(ring_kernel, side_index, (north, south), [None] * 2, (shape_of(2, CX, levels),), (), "ring")
+    args = (current_speeds, thermal_anomaly, linked, got, north, south, sides, edge, swap(ring))
+    speeds1, wide_t1, t1, r1 = ocean(1, comp, coriolis, args, wide_depth, CY, half)
     r1 = in_hbm(r1)
-    speeds2, t2, r2 = ocean(2, comp, coriolis, (speeds1, wide_t1), wide_depth, CY, CX)
+    speeds2, t2, r2 = ocean(2, comp, coriolis, (speeds1, wide_t1), wide_depth, CY, half)
     arrived, speeds2, t2 = lax.optimization_barrier((arrived, speeds2, t2))
-    speeds2, t2, r2 = in_hbm(speeds2), in_hbm(t2), in_hbm(r2)
-
-    patch_half = half_spec((CY,), half, levels)
-    speeds_half = half_spec((2, CY), half, levels)
+    speeds2, t2, r2 = in_vmem(speeds2), in_vmem(t2), in_hbm(r2)
+
     depth_half = pl.BlockSpec((5, CY, half, 1), lambda i, c: (0, 0, c[0], 0))
     piece = shape_of(CY, half, levels)
     scratch = (CY, half, levels)
@@ -852,18 +866,18 @@
     side = shape_of(3, CY, levels)
 
     t2, irr1, *edges = call(
-        absorb_kernel, comp, (arrived, t2, speeds2, depth), [HBM, patch_half, speeds_half, depth_half],
+        absorb_kernel, comp, (arrived, t2, speeds2, depth), [HBM, None, None, depth_half],
         (piece, piece, line, line, side, side), [scratch] * 2, "absorb", [pltpu.SemaphoreType.DMA],
     )
     halos2 = exchange_rows(edges[0], edges[1]) + exchange_half_cols(edges[2], edges[3])
     heat, a, b, g = call(
         second_kernel, comp, (arrived, irr1, t1, r1, depth, shares),
-        [None, None, patch_half, patch_half, depth_half, SMEM],
+        [None] * 4 + [depth_half, SMEM],
         (piece,) * 4, [scratch] * 2, "second",
     )
     [back] = call(
         last_ocean_kernel, comp, (speeds2, t2, *halos2, depth, heat),
-        [speeds_half] + [None] * 5 + [depth_half, None],
+        [None] * 6 + [depth_half, None],
         (shape_of(2, patches, 2, half, levels),), [scratch], "last_ocean",
     )
     flux = lax.all_to_all(
@@ -871,7 +885,7 @@
     ).reshape(2, patches, 2, half, levels)
     [absorbed] = call(
         third_kernel, comp, (a, b, g, t2, r2, depth, shares),
-        [None] * 4 + [patch_half, depth_half, SMEM], (shape_of(CY, 2, half, levels),), [scratch], "third",
+        [None] * 5 + [depth_half, SMEM], (shape_of(CY, 2, half, levels),), [scratch], "third",
     )
     other = swap(absorbed)
     [out] = call(

time: 112 us -> 109 us (0.973)
  waiting for transfers between devices: 33.3 us -> 39.8 us
  Pallas kernels: 40.7 us -> 34.6 us
  local copies, waits for them, and re-layouts: 14.3 us -> 10.1 us
    all_to_all x1, waiting for transfers between devices: 3.33 us -> 11.9 us  [to_owners(): lax.all_to_all(blocks, ('py', 'px'), split_axis=0, concat_axis=0, tiled=T...]
    unnamed x58 -> x46, local copies, waits for them, and re-layouts: 11.9 us -> 7.77 us
    pallas_call x2, Pallas kernels: 14 us -> 10.8 us  [ocean(): pl.pallas_call(functools.partial(ocean_kernel, advance), grid_spec=pltpu....]
    pallas_call x7, Pallas kernels: 14.8 us -> 11.8 us  [call(): pl.pallas_call(kernel, grid_spec=pltpu.PrefetchScalarGridSpec(num_scalar_...]
    ppermute x2, starting transfers between devices: 3.32 us -> 5.21 us  [the longest x1 5.21 us: east_column(): lax.ppermute(block, ('comp', 'px'), [((i + 1) % count, count + i) for i i...]
    ppermute x2, starting transfers between devices: 2.05 us -> 3.5 us  [exchange_rows(): lax.ppermute(high, 'py', [(i, (i + 1) % count) for i in range(count)])]
  transfers between devices with their start and end apart: 13 -> 13, of which waited for: 6 -> 6; matrix products, arithmetic and copies ran while one was open for 4% -> 5% of each run, Pallas kernels for 27% -> 24%
where the time goes in v5:
time: 109 us
  waiting for transfers between devices  39.8 us (37%)
  Pallas kernels  34.6 us (32%)
  starting transfers between devices  21.4 us (20%)
  local copies, waits for them, and re-layouts  10.1 us (9%)
  other arithmetic  1.32 us (1%)
  matrix products  1.18 us (1%)
    ppermute x3, waiting for transfers between devices, swap(): return lax.ppermute(block, 'comp', [(0, 1), (1, 0)])  22 us
    all_to_all x1, waiting for transfers between devices, to_owners(): lax.all_to_all(blocks, ('py', 'px'), split_axis=0, concat_axis=0, tiled=T...  11.9 us
    pallas_call x7, Pallas kernels, call(): pl.pallas_call(kernel, grid_spec=pltpu.PrefetchScalarGridSpec(num_scalar_...  11.8 us
    pallas_call x2, Pallas kernels, ocean(): pl.pallas_call(functools.partial(ocean_kernel, advance), grid_spec=pltpu....  10.8 us
    unnamed x46, local copies, waits for them, and re-layouts  7.77 us
    ppermute x1, starting transfers between devices, east_column(): lax.ppermute(block, ('comp', 'px'), [((i + 1) % count, count + i) for i i...  5.21 us
    pallas_call x1, Pallas kernels, project(): pl.pallas_call(project_kernel, grid_spec=pltpu.PrefetchScalarGridSpec(num...  4.95 us
    all_to_all x1, starting transfers between devices, to_owners(): lax.all_to_all(blocks, ('py', 'px'), split_axis=0, concat_axis=0, tiled=T...  4.67 us
  transfers between devices with their start and end apart: 13, of which 6 were waited for; matrix products, arithmetic and copies ran while one was open for 5% of the time, Pallas kernels for 24%

profile of v5, /device:TPU:1, one launch (start us, length us, event | category | flops | bytes accessed | tf_op | source)
XLA Modules:
  0.0 108.7 jit_solution(3333935509776917815)
XLA Ops:
  0.0 2.7 %pack.1 = (f32[2,16,16,256]{3,2,1,0:T(8,128)}, f32[4,2,32,256]{3,2,1,0:T(8,128)}, f32[4,2,32,256]{3,2,1,0:T(8,128)}, f32[4,2,16,256]{3,2,1,0:T(8,128)}, f32[4,2,16,256]{3,2,1,0:T(8,128)}, /*index=5*/f32[16,256]{1,0:T(8,128)}) custom-call(s32[1]{0:T(128)} %bitcast.sc, f32[2,16,32,256]{3,2,1,0:T(8,128)} %bitcast.53, f32[2,16,32,256]{3,2,1,0:T(8,128)} %refs_0_.1, ...), custom_call_target="tpu_custom_call" | custom-call | tf_op jit(solution)/shard_map/pack/pallas_call | solution.py:276
  2.8 2.6 %collective-permute-start.2 = (f32[4,2,32,256]{3,2,1,0:T(8,128)}, f32[4,2,32,256]{3,2,1,0:T(8,128)S(1)}, u32[]{:S(2)}, u32[]{:S(2)}) collective-permute-start(f32[4,2,32,256]{3,2,1,0:T(8,128)} %get-tuple-element.50), channel_id=1, source_target_pairs={{0,4},{4,8},{8,12},{12,0},{1,5},{5,9},{9,13},{13,1},{2,6},{6,10},{... | collective-permute-start | bytes 786440 | tf_op jit(solution)/shard_map/ppermute | solution.py:617
  5.4 1.2 %collective-permute-start = (f32[2,16,16,256]{3,2,1,0:T(8,128)}, f32[2,16,16,256]{3,2,1,0:T(8,128)S(1)}, u32[]{:S(2)}, u32[]{:S(2)}) collective-permute-start(f32[2,16,16,256]{3,2,1,0:T(8,128)} %get-tuple-element.48), channel_id=1, source_target_pairs={{0,16},{16,0},{1,17},{17,1},{2,18},{18,2},{3,19},{19,3},{4,20},{20... | collective-permute-start | bytes 1572872 | tf_op jit(solution)/shard_map/ppermute | solution.py:662
  6.6 5.2 %collective-permute-start.4 = (f32[16,256]{1,0:T(8,128)}, f32[16,256]{1,0:T(8,128)S(1)}, u32[]{:S(2)}, u32[]{:S(2)}) collective-permute-start(f32[16,256]{1,0:T(8,128)} %get-tuple-element.53), channel_id=1, source_target_pairs={{1,16},{2,17},{3,18},{0,19},{5,20},{6,21},{7,22},{4,23},{9,24},{10... | collective-permute-start | bytes 49160 | tf_op jit(solution)/shard_map/ppermute | solution.py:637
  12.3 5.0 %project.1 = (f32[7,16,16,256]{3,2,1,0:T(8,128)S(1)}, f32[16,16,256]{2,1,0:T(8,128)S(1)}) custom-call(s32[1]{0:T(128)} %bitcast.sc, f32[16,16,32,256]{3,2,1,0:T(8,128)} %bitcast.56, f32[7,16]{1,0:T(8,128)S(1)} %stack.30.w_ref), custom_call_target="tpu_custom_call" | custom-call | tf_op jit(solution)/shard_map/project/pallas_call | solution.py:140
  17.5 0.8 reshape.35
  18.2 1.0 fusion
  20.0 0.8 convolution_bitcast_fusion.share_ref
  21.1 4.3 %first_tracer.1 = f32[16,5,16,256]{3,2,1,0:T(8,128)} custom-call(s32[1]{0:T(128)} %bitcast.sc, f32[7,16,16,256]{3,2,1,0:T(8,128)S(1)} %get-tuple-element.46.y_ref, f32[16,16,256]{2,1,0:T(8,128)S(1)} %get-tuple-element.47.g_ref, f32[2,16,16,256]{3,2,1,0:T(8,128)S(1)} %collective-permute-done.got_ref.refs_3_, f32[2,16,32,256]{3,2,1,0:T(8,128)} %bitcast.54, ...), custom_call_target="tpu_custom_call" | custom-call | tf_op jit(solution)/shard_map/first_tracer/pallas_call | solution.py:187
  25.4 2.9 %collective-permute-done.3.refs_6_ = f32[4,2,18,256]{3,2,1,0:T(8,128)} collective-permute-done((f32[4,2,18,256]{3,2,1,0:T(8,128)}, f32[4,2,18,256]{3,2,1,0:T(8,128)}, u32[]{:S(2)}, u32[]{:S(2)}) %collective-permute-start.3) | collective-permute-done | bytes 147488 | tf_op jit(solution)/shard_map/ppermute | solution.py:632
  28.3 4.7 %all-to-all-start = ((f32[16,5,16,256]{3,2,1,0:T(8,128)}), f32[16,5,16,256]{3,2,1,0:T(8,128)S(1)}, u32[]{:S(2)}, u32[]{:S(2)}) async-start(f32[16,5,16,256]{3,2,1,0:T(8,128)} %first_tracer.1), calls=%async_computation | async-start | bytes 2621440 | tf_op jit(solution)/shard_map/all_to_all | solution.py:658
  34.8 3.4 %collective-permute-done.5.refs_8_ = f32[2,32,256]{2,1,0:T(8,128)S(1)} collective-permute-done((f32[2,32,256]{2,1,0:T(8,128)S(1)}, f32[2,32,256]{2,1,0:T(8,128)S(1)}, u32[]{:S(2)}, u32[]{:S(2)}) %collective-permute-start.5) | collective-permute-done | bytes 65568 | tf_op jit(solution)/shard_map/ppermute | solution.py:662
  38.3 1.0 copy-done.2
  39.3 6.8 %ocean1.1 = (f32[2,18,24,256]{3,2,1,0:T(8,128)S(1)}, f32[18,24,256]{2,1,0:T(8,128)S(1)}, f32[16,16,256]{2,1,0:T(8,128)S(1)}, f32[16,16,256]{2,1,0:T(8,128)S(1)}) custom-call(s32[17]{0:T(128)S(1)} %pad_add_fusion.1.sc, f32[18]{0:T(128)S(1)} %multiply_add_fusion.coriolis_ref, f32[2,16,32,256]{3,2,1,0:T(8,128)} %refs_0_.1, f32[16,32,256]{2,1,0:T(8,128)} %refs_1_.1, ...), custom_call_target="tpu_custom_call" | custom-call | tf_op jit(solution)/shard_map/ocean1/pallas_call | solution.py:447
  47.5 4.0 %ocean2.1 = (f32[2,16,16,256]{3,2,1,0:T(8,128)S(1)}, f32[16,16,256]{2,1,0:T(8,128)S(1)}, f32[16,16,256]{2,1,0:T(8,128)S(1)}) custom-call(s32[17]{0:T(128)S(1)} %pad_add_fusion.1.sc, f32[18]{0:T(128)S(1)} %multiply_add_fusion.coriolis_ref, f32[2,18,24,256]{3,2,1,0:T(8,128)S(1)} %get-tuple-element.59.refs_0_, f32[18,24,256]{2,1,0:T(8,128)S(1)} %get-tuple-element.60.refs_1_, ...), custom_call_target="tpu_custom_call" | custom-call | tf_op jit(solution)/shard_map/ocean2/pallas_call | solution.py:447
  52.9 11.9 %all-to-all-done.y_hbm.y_ref = f32[16,5,16,256]{3,2,1,0:T(8,128)S(1)} async-done(((f32[16,5,16,256]{3,2,1,0:T(8,128)}), f32[16,5,16,256]{3,2,1,0:T(8,128)S(1)}, u32[]{:S(2)}, u32[]{:S(2)}) %all-to-all-start) | async-done | bytes 1310752 | tf_op jit(solution)/shard_map/all_to_all | solution.py:658
  64.8 0.9 copy-done.14
  65.8 1.3 %absorb.1 = (f32[16,16,256]{2,1,0:T(8,128)S(1)}, f32[16,16,256]{2,1,0:T(8,128)S(1)}, f32[3,16,256]{2,1,0:T(8,128)S(1)}, f32[3,16,256]{2,1,0:T(8,128)S(1)}, f32[3...) custom-call(s32[17]{0:T(128)S(1)} %pad_add_fusion.1.sc, f32[16,5,16,256]{3,2,1,0:T(8,128)S(1)} %all-to-all-done.y_hbm.y_ref, ...), custom_call_target="tpu_custom_call" | custom-call | tf_op jit(solution)/shard_map/absorb/pallas_call | solution.py:599
  67.1 0.9 collective-permute-start.6
  68.1 0.9 collective-permute-start.7
  68.9 1.5 %collective-permute-start.9 = (f32[3,16,256]{2,1,0:T(8,128)S(1)}, f32[3,16,256]{2,1,0:T(8,128)S(1)}, u32[]{:S(2)}, u32[]{:S(2)}) collective-permute-start(f32[3,16,256]{2,1,0:T(8,128)S(1)} %get-tuple-element.77), channel_id=1, source_target_pairs={{0,16},{16,1},{1,17},{17,2},{2,18},{18,3},{3,19},{19,0},{4,20},{20... | collective-permute-start | bytes 147464 | tf_op jit(solution)/shard_map/ppermute | solution.py:645
  70.4 3.0 %second.1 = (f32[16,16,256]{2,1,0:T(8,128)S(1)}, f32[16,16,256]{2,1,0:T(8,128)S(1)}, f32[16,16,256]{2,1,0:T(8,128)S(1)}, f32[16,16,256]{2,1,0:T(8,128)S(1)}) custom-call(s32[17]{0:T(128)S(1)} %pad_add_fusion.1.sc, f32[16,5,16,256]{3,2,1,0:T(8,128)S(1)} %all-to-all-done.y_hbm.y_ref, f32[16,16,256]{2,1,0:T(8,128)S(1)} %get-tuple-element.66.irr_ref, ...), custom_call_target="tpu_custom_call" | custom-call | tf_op jit(solution)/shard_map/second/pallas_call | solution.py:599
  74.1 1.2 %collective-permute-done.9.west_ref = f32[3,16,256]{2,1,0:T(8,128)S(1)} collective-permute-done((f32[3,16,256]{2,1,0:T(8,128)S(1)}, f32[3,16,256]{2,1,0:T(8,128)S(1)}, u32[]{:S(2)}, u32[]{:S(2)}) %collective-permute-start.9) | collective-permute-done | bytes 49184 | tf_op jit(solution)/shard_map/ppermute | solution.py:645
  75.3 2.4 %last_ocean.1 = f32[2,16,2,16,256]{4,3,2,1,0:T(8,128)} custom-call(s32[17]{0:T(128)S(1)} %pad_add_fusion.1.sc, f32[2,16,16,256]{3,2,1,0:T(8,128)S(1)} %get-tuple-element.65.speed_ref, f32[16,16,256]{2,1,0:T(8,128)S(1)} %get-tuple-element.72.t2_ref.t_ref, f32[3,16,256]{2,1,0:T(8,128)S(1)} %collective-permute-done.6.north_ref, ...), custom_call_target="tpu_custom_call" | custom-call | tf_op jit(solution)/shard_map/last_ocean/pallas_call | solution.py:599
  77.7 2.9 %all-to-all-start.1 = ((f32[32,2,16,256]{3,2,1,0:T(8,128)}), f32[32,2,16,256]{3,2,1,0:T(8,128)S(1)}, u32[]{:S(2)}, u32[]{:S(2)}) async-start(f32[32,2,16,256]{3,2,1,0:T(8,128)} %bitcast.18), calls=%async_computation.1 | async-start | bytes 2097152 | tf_op jit(solution)/shard_map/all_to_all | solution.py:883
  80.6 0.9 copy-done.10
  81.6 0.9 copy-done.12
  82.5 2.7 %third.1.absorbed_ref = f32[16,2,16,256]{3,2,1,0:T(8,128)S(1)} custom-call(s32[17]{0:T(128)S(1)} %pad_add_fusion.1.sc, f32[16,16,256]{2,1,0:T(8,128)S(1)} %copy-done.8, f32[16,16,256]{2,1,0:T(8,128)S(1)} %copy-done.10, f32[16,16,256]{2,1,0:T(8,128)S(1)} %copy-done.12, f32[16,16,256]{2,1,0:T(8,128)S(1)} %get-tuple-element.72.t2_ref.t_ref, ...), custom_call_target="tpu_custom_call" | custom-call | tf_op jit(solution)/shard_map/third/pallas_call | solution.py:599
  85.3 1.5 %collective-permute-start.10 = (f32[16,2,16,256]{3,2,1,0:T(8,128)S(1)}, f32[16,2,16,256]{3,2,1,0:T(8,128)S(1)}, u32[]{:S(2)}, u32[]{:S(2)}) collective-permute-start(f32[16,2,16,256]{3,2,1,0:T(8,128)S(1)} %third.1.absorbed_ref), channel_id=1, source_target_pairs={{0,16},{16,0},{1,17},{17,1},{2,18},{18,2},{3,19},{19,3},{4,20},{20... | collective-permute-start | bytes 1572872 | tf_op jit(solution)/shard_map/ppermute | solution.py:662
  86.7 18.6 %collective-permute-done.10.other_ref = f32[16,2,16,256]{3,2,1,0:T(8,128)S(1)} collective-permute-done((f32[16,2,16,256]{3,2,1,0:T(8,128)S(1)}, f32[16,2,16,256]{3,2,1,0:T(8,128)S(1)}, u32[]{:S(2)}, u32[]{:S(2)}) %collective-permute-start.10) | collective-permute-done | bytes 524320 | tf_op jit(solution)/shard_map/ppermute | solution.py:662
  105.3 1.8 %all-to-all-done.1 = f32[32,2,16,256]{3,2,1,0:T(8,128)S(1)} async-done(((f32[32,2,16,256]{3,2,1,0:T(8,128)}), f32[32,2,16,256]{3,2,1,0:T(8,128)S(1)}, u32[]{:S(2)}, u32[]{:S(2)}) %all-to-all-start.1) | async-done | bytes 1048608 | tf_op jit(solution)/shard_map/all_to_all | solution.py:883
  107.1 1.6 %join.1 = f32[2,16,32,256]{3,2,1,0:T(8,128)} custom-call(s32[17]{0:T(128)S(1)} %pad_add_fusion.1.sc, f32[16,2,16,256]{3,2,1,0:T(8,128)S(1)} %third.1.absorbed_ref, f32[2,16,2,16,256]{4,3,2,1,0:T(8,128)S(1)} %bitcast.52, f32[16,2,16,256]{3,2,1,0:T(8,128)S(1)} %collective-permute-done.10.other_ref), custom_call_target="tpu_custom_call" | custom-call | tf_op jit(solution)/shard_map/join/pallas_call | solution.py:599
  (79 shorter events, 7.0 us)
Async XLA Ops:
  0.0 11.8 %copy-start = (f32[16,16]{1,0:T(8,128)S(1)}, f32[16,16]{1,0:T(8,128)}, u32[]{:S(2)}) copy-start(f32[16,16]{1,0:T(8,128)} %param.17) | copy-start | bytes 3076
  0.0 11.8 %copy-start.20 = (f32[16]{0:T(128)S(1)}, f32[16]{0:T(128)}, u32[]{:S(2)}) copy-start(f32[16]{0:T(128)} %param.19) | copy-start | bytes 196
  2.7 16.6 %collective-permute-start.1 = (f32[4,2,32,256]{3,2,1,0:T(8,128)}, f32[4,2,32,256]{3,2,1,0:T(8,128)S(1)}, u32[]{:S(2)}, u32[]{:S(2)}) collective-permute-start(f32[4,2,32,256]{3,2,1,0:T(8,128)} %get-tuple-element.49), channel_id=1, source_target_pairs={{4,0},{8,4},{12,8},{0,12},{5,1},{9,5},{13,9},{1,13},{6,2},{10,6},{... | collective-permute-start | bytes 786440 | tf_op jit(solution)/shard_map/ppermute | solution.py:616
  2.8 16.5 %collective-permute-start.2 = (f32[4,2,32,256]{3,2,1,0:T(8,128)}, f32[4,2,32,256]{3,2,1,0:T(8,128)S(1)}, u32[]{:S(2)}, u32[]{:S(2)}) collective-permute-start(f32[4,2,32,256]{3,2,1,0:T(8,128)} %get-tuple-element.50), channel_id=1, source_target_pairs={{0,4},{4,8},{8,12},{12,0},{1,5},{5,9},{9,13},{13,1},{2,6},{6,10},{... | collective-permute-start | bytes 786440 | tf_op jit(solution)/shard_map/ppermute | solution.py:617
  5.4 15.7 %collective-permute-start = (f32[2,16,16,256]{3,2,1,0:T(8,128)}, f32[2,16,16,256]{3,2,1,0:T(8,128)S(1)}, u32[]{:S(2)}, u32[]{:S(2)}) collective-permute-start(f32[2,16,16,256]{3,2,1,0:T(8,128)} %get-tuple-element.48), channel_id=1, source_target_pairs={{0,16},{16,0},{1,17},{17,1},{2,18},{18,2},{3,19},{19,3},{4,20},{20... | collective-permute-start | bytes 1572872 | tf_op jit(solution)/shard_map/ppermute | solution.py:662
  6.6 18.8 %collective-permute-start.4 = (f32[16,256]{1,0:T(8,128)}, f32[16,256]{1,0:T(8,128)S(1)}, u32[]{:S(2)}, u32[]{:S(2)}) collective-permute-start(f32[16,256]{1,0:T(8,128)} %get-tuple-element.53), channel_id=1, source_target_pairs={{1,16},{2,17},{3,18},{0,19},{5,20},{6,21},{7,22},{4,23},{9,24},{10... | collective-permute-start | bytes 49160 | tf_op jit(solution)/shard_map/ppermute | solution.py:637
  12.3 5.0 %copy-start.19 = (s32[16,16]{1,0:T(8,128)S(1)}, s32[16,16]{1,0:T(8,128)}, u32[]{:S(2)}) copy-start(s32[16,16]{1,0:T(8,128)} %param.16) | copy-start | bytes 3076
  12.3 5.2 %copy-start.17 = (s32[64,128]{1,0:T(8,128)S(1)}, s32[64,128]{1,0:T(8,128)}, u32[]{:S(2)}) copy-start(s32[64,128]{1,0:T(8,128)} %param.14) | copy-start | bytes 98308
  12.3 5.1 %copy-start.18 = (s32[64,128]{1,0:T(8,128)S(1)}, s32[64,128]{1,0:T(8,128)}, u32[]{:S(2)}) copy-start(s32[64,128]{1,0:T(8,128)} %param.15) | copy-start | bytes 98308
  12.3 7.0 %copy-start.15 = (f32[4,2,16,256]{3,2,1,0:T(8,128)S(1)}, f32[4,2,16,256]{3,2,1,0:T(8,128)}, u32[]{:S(2)}) copy-start(f32[4,2,16,256]{3,2,1,0:T(8,128)} %get-tuple-element.51.left_ref) | copy-start | bytes 393220
  12.3 7.0 %copy-start.16 = (f32[4,2,16,256]{3,2,1,0:T(8,128)S(1)}, f32[4,2,16,256]{3,2,1,0:T(8,128)}, u32[]{:S(2)}) copy-start(f32[4,2,16,256]{3,2,1,0:T(8,128)} %get-tuple-element.52.right_ref) | copy-start | bytes 393220
  20.0 8.3 %collective-permute-start.3 = (f32[4,2,18,256]{3,2,1,0:T(8,128)}, f32[4,2,18,256]{3,2,1,0:T(8,128)}, u32[]{:S(2)}, u32[]{:S(2)}) collective-permute-start(f32[4,2,18,256]{3,2,1,0:T(8,128)} %corner.1), channel_id=1, source_target_pairs={{0,1},{1,2},{2,3},{3,0},{17,16},{18,17},{19,18},{16,19},{4,5},{5,6... | collective-permute-start | bytes 442376 | tf_op jit(solution)/shard_map/ppermute | solution.py:632
  21.1 4.3 %copy-start.1 = (f32[2,16,16,256]{3,2,1,0:T(8,128)}, f32[2,16,16,256]{3,2,1,0:T(8,128)S(1)}, u32[]{:S(2)}) copy-start(f32[2,16,16,256]{3,2,1,0:T(8,128)S(1)} %collective-permute-done.got_ref.refs_3_) | copy-start | bytes 1572868
  28.3 36.5 %all-to-all-start = ((f32[16,5,16,256]{3,2,1,0:T(8,128)}), f32[16,5,16,256]{3,2,1,0:T(8,128)S(1)}, u32[]{:S(2)}, u32[]{:S(2)}) async-start(f32[16,5,16,256]{3,2,1,0:T(8,128)} %first_tracer.1), calls=%async_computation | async-start | bytes 2621440 | tf_op jit(solution)/shard_map/all_to_all | solution.py:658
  34.8 3.5 %collective-permute-start.5 = (f32[2,32,256]{2,1,0:T(8,128)S(1)}, f32[2,32,256]{2,1,0:T(8,128)S(1)}, u32[]{:S(2)}, u32[]{:S(2)}) collective-permute-start(f32[2,32,256]{2,1,0:T(8,128)S(1)} %ring.1), channel_id=1, source_target_pairs={{0,16},{16,0},{1,17},{17,1},{2,18},{18,2},{3,19},{19,3},{4,20},{20... | collective-permute-start | bytes 196616 | tf_op jit(solution)/shard_map/ppermute | solution.py:662
  38.3 1.0 copy-start.2
  51.5 0.7 copy-start.3
  52.2 0.7 copy-start.13
  64.8 1.0 copy-start.14
  65.8 4.6 %copy-start.5 = (f32[16,16,256]{2,1,0:T(8,128)S(1)}, f32[16,16,256]{2,1,0:T(8,128)}, u32[]{:S(2)}) copy-start(f32[16,16,256]{2,1,0:T(8,128)} %copy-done.4) | copy-start | bytes 786436
  67.1 7.0 %collective-permute-start.6 = (f32[3,16,256]{2,1,0:T(8,128)S(1)}, f32[3,16,256]{2,1,0:T(8,128)S(1)}, u32[]{:S(2)}, u32[]{:S(2)}) collective-permute-start(f32[3,16,256]{2,1,0:T(8,128)S(1)} %get-tuple-element.74), channel_id=1, source_target_pairs={{4,0},{8,4},{12,8},{0,12},{5,1},{9,5},{13,9},{1,13},{6,2},{10,6},{... | collective-permute-start | bytes 147464 | tf_op jit(solution)/shard_map/ppermute | solution.py:616
  68.1 6.0 %collective-permute-start.7 = (f32[3,16,256]{2,1,0:T(8,128)S(1)}, f32[3,16,256]{2,1,0:T(8,128)S(1)}, u32[]{:S(2)}, u32[]{:S(2)}) collective-permute-start(f32[3,16,256]{2,1,0:T(8,128)S(1)} %get-tuple-element.75), channel_id=1, source_target_pairs={{0,4},{4,8},{8,12},{12,0},{1,5},{5,9},{9,13},{13,1},{2,6},{6,10},{... | collective-permute-start | bytes 147464 | tf_op jit(solution)/shard_map/ppermute | solution.py:617
  68.9 5.2 %collective-permute-start.8 = (f32[3,16,256]{2,1,0:T(8,128)S(1)}, f32[3,16,256]{2,1,0:T(8,128)S(1)}, u32[]{:S(2)}, u32[]{:S(2)}) collective-permute-start(f32[3,16,256]{2,1,0:T(8,128)S(1)} %get-tuple-element.76), channel_id=1, source_target_pairs={{16,0},{1,16},{17,1},{2,17},{18,2},{3,18},{19,3},{0,19},{20,4},{5,... | collective-permute-start | bytes 147464 | tf_op jit(solution)/shard_map/ppermute | solution.py:644
  68.9 6.4 %collective-permute-start.9 = (f32[3,16,256]{2,1,0:T(8,128)S(1)}, f32[3,16,256]{2,1,0:T(8,128)S(1)}, u32[]{:S(2)}, u32[]{:S(2)}) collective-permute-start(f32[3,16,256]{2,1,0:T(8,128)S(1)} %get-tuple-element.77), channel_id=1, source_target_pairs={{0,16},{16,1},{1,17},{17,2},{2,18},{18,3},{3,19},{19,0},{4,20},{20... | collective-permute-start | bytes 147464 | tf_op jit(solution)/shard_map/ppermute | solution.py:645
  73.4 0.7 copy-start.7
  74.1 3.6 %copy-start.9 = (f32[16,16,256]{2,1,0:T(8,128)}, f32[16,16,256]{2,1,0:T(8,128)S(1)}, u32[]{:S(2)}) copy-start(f32[16,16,256]{2,1,0:T(8,128)S(1)} %get-tuple-element.70.b_ref) | copy-start | bytes 786436
  74.1 3.6 %copy-start.11 = (f32[16,16,256]{2,1,0:T(8,128)}, f32[16,16,256]{2,1,0:T(8,128)S(1)}, u32[]{:S(2)}) copy-start(f32[16,16,256]{2,1,0:T(8,128)S(1)} %get-tuple-element.71.g_ref) | copy-start | bytes 786436
  77.7 2.9 %copy-start.8 = (f32[16,16,256]{2,1,0:T(8,128)S(1)}, f32[16,16,256]{2,1,0:T(8,128)}, u32[]{:S(2)}) copy-start(f32[16,16,256]{2,1,0:T(8,128)} %copy-done.7) | copy-start | bytes 786436
  77.7 29.4 %all-to-all-start.1 = ((f32[32,2,16,256]{3,2,1,0:T(8,128)}), f32[32,2,16,256]{3,2,1,0:T(8,128)S(1)}, u32[]{:S(2)}, u32[]{:S(2)}) async-start(f32[32,2,16,256]{3,2,1,0:T(8,128)} %bitcast.18), calls=%async_computation.1 | async-start | bytes 2097152 | tf_op jit(solution)/shard_map/all_to_all | solution.py:883
  80.6 1.0 copy-start.10
  81.6 0.9 copy-start.12
  85.3 20.0 %collective-permute-start.10 = (f32[16,2,16,256]{3,2,1,0:T(8,128)S(1)}, f32[16,2,16,256]{3,2,1,0:T(8,128)S(1)}, u32[]{:S(2)}, u32[]{:S(2)}) collective-permute-start(f32[16,2,16,256]{3,2,1,0:T(8,128)S(1)} %third.1.absorbed_ref), channel_id=1, source_target_pairs={{0,16},{16,0},{1,17},{17,1},{2,18},{18,2},{3,19},{19,3},{4,20},{20... | collective-permute-start | bytes 1572872 | tf_op jit(solution)/shard_map/ppermute | solution.py:662
  (2 other events, 1.4 us)

commit v6 on v5

--- a/solution.py
+++ b/solution.py
@@ -806,12 +806,14 @@
     )[..., None]
     depth = jnp.stack([local[1:-1, 1:-1], local[1:-1, 2:], local[1:-1, :-2], local[2:, 1:-1], local[:-2, 1:-1]])
     depth = depth[..., None]
-    by_strip = (
-        column_depth.reshape(rows_mesh, CY, cols_mesh, CX).transpose(0, 2, 1, 3).reshape(patches, patches, strip)
-    )
-    here = (holder_rank == patch_index)[:, :, None]
-    tracer_depth = jnp.sum(jnp.where(here, by_strip, 0), axis=1)
-    tracer_depth = lax.dynamic_slice_in_dim(tracer_depth, comp_index * half, half, 1)[..., None]
+    def depth_of_tracers(column_depth):
+        by_strip = (
+            column_depth.reshape(rows_mesh, CY, cols_mesh, CX).transpose(0, 2, 1, 3).reshape(patches, patches, strip)
+        )
+        here = (holder_rank == patch_index)[:, :, None]
+        tracer_depth = jnp.sum(jnp.where(here, by_strip, 0), axis=1)
+        return lax.dynamic_slice_in_dim(tracer_depth, comp_index * half, half, 1)[..., None]
+
     owner_row = lax.dynamic_index_in_dim(holder_rank, patch_index, 0, keepdims=False)
     side_index = comp_index.astype(jnp.int32)[None]
     comp = jnp.concatenate([side_index, owner_row])
@@ -820,7 +822,7 @@
 
     if half % 8 or strip != CX:
         out = general(
-            linked, u0, v0, thermal_anomaly, tracers, depth, tracer_depth, holder_rank, patch_index, coriolis[1:-1],
+            linked, u0, v0, thermal_anomaly, tracers, depth, depth_of_tracers(column_depth), holder_rank, patch_index, coriolis[1:-1],
             biota_exchange_matrix, photic_absorb_share, chroma_loading,
         )
         return out.reshape(1, 2, 1, columns, levels)
@@ -836,7 +838,6 @@
     for _ in range(3):
         chain.append(times(chain[-1], biota_exchange_matrix))
     weights = jnp.stack([c[0] for c in chain] + [c[1] for c in chain[:3]])
-    shares = times(weights, photic_absorb_share)
 
     projected, g = project(side_index, tracers, weights)
     low, high, left, right, first_column = edges
@@ -846,7 +847,10 @@
     projected, g = in_vmem(projected), in_vmem(g)
     outer = shape_of(4, 2, CY + 2, levels)
     [sides] = call(corner_kernel, side_index, (left, right, north, south), [None] * 4, (outer,), (), "corner")
+    column_depth, photic_absorb_share, sides = lax.optimization_barrier((column_depth, photic_absorb_share, sides))
     sides = far_columns(sides)
+    tracer_depth = depth_of_tracers(column_depth)
+    shares = times(weights, photic_absorb_share)
     kept = first_tracer(side_index, projected, g, got, linked, tracer_depth, shares)
     kept, north, south, sides, edge = lax.optimization_barrier((kept, north, south, sides, edge))
     arrived = to_owners(kept)

time: 109 us -> 109 us (level)
  transfers between devices with their start and end apart: 13 -> 13, of which waited for: 6 -> 6; matrix products, arithmetic and copies ran while one was open for 5% -> 3% of each run, Pallas kernels for 24% -> 25%
where the time goes in v6:
time: 109 us; the launch traced here: 108 us
  waiting for transfers between devices  39.6 us (36%)
  Pallas kernels  34.6 us (32%)
  starting transfers between devices  22.4 us (21%)
  local copies, waits for them, and re-layouts  9.45 us (9%)
  matrix products  1.19 us (1%)
    ppermute x3, waiting for transfers between devices, swap(): return lax.ppermute(block, 'comp', [(0, 1), (1, 0)])  22 us
    all_to_all x1, waiting for transfers between devices, to_owners(): lax.all_to_all(blocks, ('py', 'px'), split_axis=0, concat_axis=0, tiled=T...  11.9 us
    pallas_call x7, Pallas kernels, call(): pl.pallas_call(kernel, grid_spec=pltpu.PrefetchScalarGridSpec(num_scalar_...  11.8 us
    pallas_call x2, Pallas kernels, ocean(): pl.pallas_call(functools.partial(ocean_kernel, advance), grid_spec=pltpu....  10.8 us
    unnamed x46, local copies, waits for them, and re-layouts  7.77 us
    ppermute x1, starting transfers between devices, east_column(): lax.ppermute(block, ('comp', 'px'), [((i + 1) % count, count + i) for i i...  5.21 us
    pallas_call x1, Pallas kernels, project(): pl.pallas_call(project_kernel, grid_spec=pltpu.PrefetchScalarGridSpec(num...  4.95 us
    all_to_all x1, starting transfers between devices, to_owners(): lax.all_to_all(blocks, ('py', 'px'), split_axis=0, concat_axis=0, tiled=T...  4.67 us
  transfers between devices with their start and end apart: 13, of which 6 were waited for; matrix products, arithmetic and copies ran while one was open for 3% of the time, Pallas kernels for 25%

profile of v6, /device:TPU:1, one launch (start us, length us, event | category | flops | bytes accessed | tf_op | source)
XLA Modules:
  0.0 108.0 jit_solution(3133654295854192270)
XLA Ops:
  0.0 2.7 %pack.1 = (f32[2,16,16,256]{3,2,1,0:T(8,128)}, f32[4,2,32,256]{3,2,1,0:T(8,128)}, f32[4,2,32,256]{3,2,1,0:T(8,128)}, f32[4,2,16,256]{3,2,1,0:T(8,128)}, f32[4,2,16,256]{3,2,1,0:T(8,128)}, /*index=5*/f32[16,256]{1,0:T(8,128)}) custom-call(s32[1]{0:T(128)} %bitcast.sc, f32[2,16,32,256]{3,2,1,0:T(8,128)} %bitcast.53, f32[2,16,32,256]{3,2,1,0:T(8,128)} %refs_0_.1, ...), custom_call_target="tpu_custom_call" | custom-call | tf_op jit(solution)/shard_map/pack/pallas_call | solution.py:276
  2.8 2.6 %collective-permute-start.2 = (f32[4,2,32,256]{3,2,1,0:T(8,128)}, f32[4,2,32,256]{3,2,1,0:T(8,128)S(1)}, u32[]{:S(2)}, u32[]{:S(2)}) collective-permute-start(f32[4,2,32,256]{3,2,1,0:T(8,128)} %get-tuple-element.55), channel_id=1, source_target_pairs={{0,4},{4,8},{8,12},{12,0},{1,5},{5,9},{9,13},{13,1},{2,6},{6,10},{... | collective-permute-start | bytes 786440 | tf_op jit(solution)/shard_map/ppermute | solution.py:617
  5.4 1.2 %collective-permute-start = (f32[2,16,16,256]{3,2,1,0:T(8,128)}, f32[2,16,16,256]{3,2,1,0:T(8,128)S(1)}, u32[]{:S(2)}, u32[]{:S(2)}) collective-permute-start(f32[2,16,16,256]{3,2,1,0:T(8,128)} %get-tuple-element.51), channel_id=1, source_target_pairs={{0,16},{16,0},{1,17},{17,1},{2,18},{18,2},{3,19},{19,3},{4,20},{20... | collective-permute-start | bytes 1572872 | tf_op jit(solution)/shard_map/ppermute | solution.py:662
  6.6 5.2 %collective-permute-start.4 = (f32[16,256]{1,0:T(8,128)}, f32[16,256]{1,0:T(8,128)S(1)}, u32[]{:S(2)}, u32[]{:S(2)}) collective-permute-start(f32[16,256]{1,0:T(8,128)} %get-tuple-element.59), channel_id=1, source_target_pairs={{1,16},{2,17},{3,18},{0,19},{5,20},{6,21},{7,22},{4,23},{9,24},{10... | collective-permute-start | bytes 49160 | tf_op jit(solution)/shard_map/ppermute | solution.py:637
  12.3 5.0 %project.1 = (f32[7,16,16,256]{3,2,1,0:T(8,128)S(1)}, f32[16,16,256]{2,1,0:T(8,128)S(1)}) custom-call(s32[1]{0:T(128)} %bitcast.sc, f32[16,16,32,256]{3,2,1,0:T(8,128)} %bitcast.56, f32[7,16]{1,0:T(8,128)S(1)} %stack.30.w_ref), custom_call_target="tpu_custom_call" | custom-call | tf_op jit(solution)/shard_map/project/pallas_call | solution.py:140
  17.5 0.7 corner.1
  18.6 0.8 convolution_bitcast_fusion.share_ref
  19.6 4.3 %first_tracer.1 = f32[16,5,16,256]{3,2,1,0:T(8,128)} custom-call(s32[1]{0:T(128)} %bitcast.sc, f32[7,16,16,256]{3,2,1,0:T(8,128)S(1)} %get-tuple-element.49.y_ref, f32[16,16,256]{2,1,0:T(8,128)S(1)} %get-tuple-element.50.g_ref, f32[2,16,16,256]{3,2,1,0:T(8,128)S(1)} %collective-permute-done.got_ref.refs_3_, f32[2,16,32,256]{3,2,1,0:T(8,128)} %bitcast.54, ...), custom_call_target="tpu_custom_call" | custom-call | tf_op jit(solution)/shard_map/first_tracer/pallas_call | solution.py:187
  23.9 2.7 %collective-permute-done.3.refs_6_ = f32[4,2,18,256]{3,2,1,0:T(8,128)} collective-permute-done((f32[4,2,18,256]{3,2,1,0:T(8,128)}, f32[4,2,18,256]{3,2,1,0:T(8,128)}, u32[]{:S(2)}, u32[]{:S(2)}) %collective-permute-start.3) | collective-permute-done | bytes 147488 | tf_op jit(solution)/shard_map/ppermute | solution.py:632
  26.7 4.7 %all-to-all-start = ((f32[16,5,16,256]{3,2,1,0:T(8,128)}), f32[16,5,16,256]{3,2,1,0:T(8,128)S(1)}, u32[]{:S(2)}, u32[]{:S(2)}) async-start(f32[16,5,16,256]{3,2,1,0:T(8,128)} %first_tracer.1), calls=%async_computation | async-start | bytes 2621440 | tf_op jit(solution)/shard_map/all_to_all | solution.py:658
  33.2 3.4 %collective-permute-done.5.refs_8_ = f32[2,32,256]{2,1,0:T(8,128)S(1)} collective-permute-done((f32[2,32,256]{2,1,0:T(8,128)S(1)}, f32[2,32,256]{2,1,0:T(8,128)S(1)}, u32[]{:S(2)}, u32[]{:S(2)}) %collective-permute-start.5) | collective-permute-done | bytes 65568 | tf_op jit(solution)/shard_map/ppermute | solution.py:662
  36.6 1.0 copy-done.2
  37.7 6.8 %ocean1.1 = (f32[2,18,24,256]{3,2,1,0:T(8,128)S(1)}, f32[18,24,256]{2,1,0:T(8,128)S(1)}, f32[16,16,256]{2,1,0:T(8,128)S(1)}, f32[16,16,256]{2,1,0:T(8,128)S(1)}) custom-call(s32[17]{0:T(128)S(1)} %pad_add_fusion.1.sc, f32[18]{0:T(128)S(1)} %multiply_add_fusion.coriolis_ref, f32[2,16,32,256]{3,2,1,0:T(8,128)} %refs_0_.1, f32[16,32,256]{2,1,0:T(8,128)} %refs_1_.1, ...), custom_call_target="tpu_custom_call" | custom-call | tf_op jit(solution)/shard_map/ocean1/pallas_call | solution.py:447
  45.9 4.0 %ocean2.1 = (f32[2,16,16,256]{3,2,1,0:T(8,128)S(1)}, f32[16,16,256]{2,1,0:T(8,128)S(1)}, f32[16,16,256]{2,1,0:T(8,128)S(1)}) custom-call(s32[17]{0:T(128)S(1)} %pad_add_fusion.1.sc, f32[18]{0:T(128)S(1)} %multiply_add_fusion.coriolis_ref, f32[2,18,24,256]{3,2,1,0:T(8,128)S(1)} %get-tuple-element.65.refs_0_, f32[18,24,256]{2,1,0:T(8,128)S(1)} %get-tuple-element.66.refs_1_, ...), custom_call_target="tpu_custom_call" | custom-call | tf_op jit(solution)/shard_map/ocean2/pallas_call | solution.py:447
  51.3 11.9 %all-to-all-done.y_hbm.y_ref = f32[16,5,16,256]{3,2,1,0:T(8,128)S(1)} async-done(((f32[16,5,16,256]{3,2,1,0:T(8,128)}), f32[16,5,16,256]{3,2,1,0:T(8,128)S(1)}, u32[]{:S(2)}, u32[]{:S(2)}) %all-to-all-start) | async-done | bytes 1310752 | tf_op jit(solution)/shard_map/all_to_all | solution.py:658
  63.2 0.9 copy-done.14
  64.2 1.3 %absorb.1 = (f32[16,16,256]{2,1,0:T(8,128)S(1)}, f32[16,16,256]{2,1,0:T(8,128)S(1)}, f32[3,16,256]{2,1,0:T(8,128)S(1)}, f32[3,16,256]{2,1,0:T(8,128)S(1)}, f32[3...) custom-call(s32[17]{0:T(128)S(1)} %pad_add_fusion.1.sc, f32[16,5,16,256]{3,2,1,0:T(8,128)S(1)} %all-to-all-done.y_hbm.y_ref, ...), custom_call_target="tpu_custom_call" | custom-call | tf_op jit(solution)/shard_map/absorb/pallas_call | solution.py:599
  65.5 0.9 collective-permute-start.6
  66.4 0.9 collective-permute-start.7
  67.3 0.7 collective-permute-start.8
  68.0 0.8 collective-permute-start.9
  68.8 3.0 %second.1 = (f32[16,16,256]{2,1,0:T(8,128)S(1)}, f32[16,16,256]{2,1,0:T(8,128)S(1)}, f32[16,16,256]{2,1,0:T(8,128)S(1)}, f32[16,16,256]{2,1,0:T(8,128)S(1)}) custom-call(s32[17]{0:T(128)S(1)} %pad_add_fusion.1.sc, f32[16,5,16,256]{3,2,1,0:T(8,128)S(1)} %all-to-all-done.y_hbm.y_ref, f32[16,16,256]{2,1,0:T(8,128)S(1)} %get-tuple-element.72.irr_ref, ...), custom_call_target="tpu_custom_call" | custom-call | tf_op jit(solution)/shard_map/second/pallas_call | solution.py:599
  72.5 1.2 %collective-permute-done.9.west_ref = f32[3,16,256]{2,1,0:T(8,128)S(1)} collective-permute-done((f32[3,16,256]{2,1,0:T(8,128)S(1)}, f32[3,16,256]{2,1,0:T(8,128)S(1)}, u32[]{:S(2)}, u32[]{:S(2)}) %collective-permute-start.9) | collective-permute-done | bytes 49184 | tf_op jit(solution)/shard_map/ppermute | solution.py:645
  73.6 2.4 %last_ocean.1 = f32[2,16,2,16,256]{4,3,2,1,0:T(8,128)} custom-call(s32[17]{0:T(128)S(1)} %pad_add_fusion.1.sc, f32[2,16,16,256]{3,2,1,0:T(8,128)S(1)} %get-tuple-element.71.speed_ref, f32[16,16,256]{2,1,0:T(8,128)S(1)} %get-tuple-element.78.t2_ref.t_ref, f32[3,16,256]{2,1,0:T(8,128)S(1)} %collective-permute-done.6.north_ref, ...), custom_call_target="tpu_custom_call" | custom-call | tf_op jit(solution)/shard_map/last_ocean/pallas_call | solution.py:599
  76.1 3.8 %all-to-all-start.1 = ((f32[32,2,16,256]{3,2,1,0:T(8,128)}), f32[32,2,16,256]{3,2,1,0:T(8,128)S(1)}, u32[]{:S(2)}, u32[]{:S(2)}) async-start(f32[32,2,16,256]{3,2,1,0:T(8,128)} %bitcast.18), calls=%async_computation.1 | async-start | bytes 2097152 | tf_op jit(solution)/shard_map/all_to_all | solution.py:887
  79.9 0.9 copy-done.10
  80.9 0.9 copy-done.12
  81.8 2.7 %third.1.absorbed_ref = f32[16,2,16,256]{3,2,1,0:T(8,128)S(1)} custom-call(s32[17]{0:T(128)S(1)} %pad_add_fusion.1.sc, f32[16,16,256]{2,1,0:T(8,128)S(1)} %copy-done.8, f32[16,16,256]{2,1,0:T(8,128)S(1)} %copy-done.10, f32[16,16,256]{2,1,0:T(8,128)S(1)} %copy-done.12, f32[16,16,256]{2,1,0:T(8,128)S(1)} %get-tuple-element.78.t2_ref.t_ref, ...), custom_call_target="tpu_custom_call" | custom-call | tf_op jit(solution)/shard_map/third/pallas_call | solution.py:599
  84.6 1.5 %collective-permute-start.10 = (f32[16,2,16,256]{3,2,1,0:T(8,128)S(1)}, f32[16,2,16,256]{3,2,1,0:T(8,128)S(1)}, u32[]{:S(2)}, u32[]{:S(2)}) collective-permute-start(f32[16,2,16,256]{3,2,1,0:T(8,128)S(1)} %third.1.absorbed_ref), channel_id=1, source_target_pairs={{0,16},{16,0},{1,17},{17,1},{2,18},{18,2},{3,19},{19,3},{4,20},{20... | collective-permute-start | bytes 1572872 | tf_op jit(solution)/shard_map/ppermute | solution.py:662
  86.0 18.6 %collective-permute-done.10.other_ref = f32[16,2,16,256]{3,2,1,0:T(8,128)S(1)} collective-permute-done((f32[16,2,16,256]{3,2,1,0:T(8,128)S(1)}, f32[16,2,16,256]{3,2,1,0:T(8,128)S(1)}, u32[]{:S(2)}, u32[]{:S(2)}) %collective-permute-start.10) | collective-permute-done | bytes 524320 | tf_op jit(solution)/shard_map/ppermute | solution.py:662
  104.6 1.8 %all-to-all-done.1 = f32[32,2,16,256]{3,2,1,0:T(8,128)S(1)} async-done(((f32[32,2,16,256]{3,2,1,0:T(8,128)}), f32[32,2,16,256]{3,2,1,0:T(8,128)S(1)}, u32[]{:S(2)}, u32[]{:S(2)}) %all-to-all-start.1) | async-done | bytes 1048608 | tf_op jit(solution)/shard_map/all_to_all | solution.py:887
  106.4 1.6 %join.1 = f32[2,16,32,256]{3,2,1,0:T(8,128)} custom-call(s32[17]{0:T(128)S(1)} %pad_add_fusion.1.sc, f32[16,2,16,256]{3,2,1,0:T(8,128)S(1)} %third.1.absorbed_ref, f32[2,16,2,16,256]{4,3,2,1,0:T(8,128)S(1)} %bitcast.52, f32[16,2,16,256]{3,2,1,0:T(8,128)S(1)} %collective-permute-done.10.other_ref), custom_call_target="tpu_custom_call" | custom-call | tf_op jit(solution)/shard_map/join/pallas_call | solution.py:599
  (79 shorter events, 6.6 us)
Async XLA Ops:
  0.0 11.8 %copy-start = (f32[16,16]{1,0:T(8,128)S(1)}, f32[16,16]{1,0:T(8,128)}, u32[]{:S(2)}) copy-start(f32[16,16]{1,0:T(8,128)} %param.17) | copy-start | bytes 3076
  0.0 11.8 %copy-start.20 = (f32[16]{0:T(128)S(1)}, f32[16]{0:T(128)}, u32[]{:S(2)}) copy-start(f32[16]{0:T(128)} %param.19) | copy-start | bytes 196
  2.7 14.8 %collective-permute-start.1 = (f32[4,2,32,256]{3,2,1,0:T(8,128)}, f32[4,2,32,256]{3,2,1,0:T(8,128)S(1)}, u32[]{:S(2)}, u32[]{:S(2)}) collective-permute-start(f32[4,2,32,256]{3,2,1,0:T(8,128)} %get-tuple-element.54), channel_id=1, source_target_pairs={{4,0},{8,4},{12,8},{0,12},{5,1},{9,5},{13,9},{1,13},{6,2},{10,6},{... | collective-permute-start | bytes 786440 | tf_op jit(solution)/shard_map/ppermute | solution.py:616
  2.8 14.7 %collective-permute-start.2 = (f32[4,2,32,256]{3,2,1,0:T(8,128)}, f32[4,2,32,256]{3,2,1,0:T(8,128)S(1)}, u32[]{:S(2)}, u32[]{:S(2)}) collective-permute-start(f32[4,2,32,256]{3,2,1,0:T(8,128)} %get-tuple-element.55), channel_id=1, source_target_pairs={{0,4},{4,8},{8,12},{12,0},{1,5},{5,9},{9,13},{13,1},{2,6},{6,10},{... | collective-permute-start | bytes 786440 | tf_op jit(solution)/shard_map/ppermute | solution.py:617
  5.4 14.2 %collective-permute-start = (f32[2,16,16,256]{3,2,1,0:T(8,128)}, f32[2,16,16,256]{3,2,1,0:T(8,128)S(1)}, u32[]{:S(2)}, u32[]{:S(2)}) collective-permute-start(f32[2,16,16,256]{3,2,1,0:T(8,128)} %get-tuple-element.51), channel_id=1, source_target_pairs={{0,16},{16,0},{1,17},{17,1},{2,18},{18,2},{3,19},{19,3},{4,20},{20... | collective-permute-start | bytes 1572872 | tf_op jit(solution)/shard_map/ppermute | solution.py:662
  6.6 17.4 %collective-permute-start.4 = (f32[16,256]{1,0:T(8,128)}, f32[16,256]{1,0:T(8,128)S(1)}, u32[]{:S(2)}, u32[]{:S(2)}) collective-permute-start(f32[16,256]{1,0:T(8,128)} %get-tuple-element.59), channel_id=1, source_target_pairs={{1,16},{2,17},{3,18},{0,19},{5,20},{6,21},{7,22},{4,23},{9,24},{10... | collective-permute-start | bytes 49160 | tf_op jit(solution)/shard_map/ppermute | solution.py:637
  12.3 5.0 %copy-start.19 = (s32[16,16]{1,0:T(8,128)S(1)}, s32[16,16]{1,0:T(8,128)}, u32[]{:S(2)}) copy-start(s32[16,16]{1,0:T(8,128)} %param.16) | copy-start | bytes 3076
  12.3 5.2 %copy-start.17 = (s32[64,128]{1,0:T(8,128)S(1)}, s32[64,128]{1,0:T(8,128)}, u32[]{:S(2)}) copy-start(s32[64,128]{1,0:T(8,128)} %param.14) | copy-start | bytes 98308
  12.3 5.1 %copy-start.18 = (s32[64,128]{1,0:T(8,128)S(1)}, s32[64,128]{1,0:T(8,128)}, u32[]{:S(2)}) copy-start(s32[64,128]{1,0:T(8,128)} %param.15) | copy-start | bytes 98308
  12.3 5.2 %copy-start.15 = (f32[4,2,16,256]{3,2,1,0:T(8,128)S(1)}, f32[4,2,16,256]{3,2,1,0:T(8,128)}, u32[]{:S(2)}) copy-start(f32[4,2,16,256]{3,2,1,0:T(8,128)} %get-tuple-element.52.left_ref) | copy-start | bytes 393220
  12.3 5.2 %copy-start.16 = (f32[4,2,16,256]{3,2,1,0:T(8,128)S(1)}, f32[4,2,16,256]{3,2,1,0:T(8,128)}, u32[]{:S(2)}) copy-start(f32[4,2,16,256]{3,2,1,0:T(8,128)} %get-tuple-element.53.right_ref) | copy-start | bytes 393220
  18.3 8.3 %collective-permute-start.3 = (f32[4,2,18,256]{3,2,1,0:T(8,128)}, f32[4,2,18,256]{3,2,1,0:T(8,128)}, u32[]{:S(2)}, u32[]{:S(2)}) collective-permute-start(f32[4,2,18,256]{3,2,1,0:T(8,128)} %corner.1), channel_id=1, source_target_pairs={{0,1},{1,2},{2,3},{3,0},{17,16},{18,17},{19,18},{16,19},{4,5},{5,6... | collective-permute-start | bytes 442376 | tf_op jit(solution)/shard_map/ppermute | solution.py:632
  19.6 4.3 %copy-start.1 = (f32[2,16,16,256]{3,2,1,0:T(8,128)}, f32[2,16,16,256]{3,2,1,0:T(8,128)S(1)}, u32[]{:S(2)}) copy-start(f32[2,16,16,256]{3,2,1,0:T(8,128)S(1)} %collective-permute-done.got_ref.refs_3_) | copy-start | bytes 1572868
  26.7 36.5 %all-to-all-start = ((f32[16,5,16,256]{3,2,1,0:T(8,128)}), f32[16,5,16,256]{3,2,1,0:T(8,128)S(1)}, u32[]{:S(2)}, u32[]{:S(2)}) async-start(f32[16,5,16,256]{3,2,1,0:T(8,128)} %first_tracer.1), calls=%async_computation | async-start | bytes 2621440 | tf_op jit(solution)/shard_map/all_to_all | solution.py:658
  33.1 3.5 %collective-permute-start.5 = (f32[2,32,256]{2,1,0:T(8,128)S(1)}, f32[2,32,256]{2,1,0:T(8,128)S(1)}, u32[]{:S(2)}, u32[]{:S(2)}) collective-permute-start(f32[2,32,256]{2,1,0:T(8,128)S(1)} %ring.1), channel_id=1, source_target_pairs={{0,16},{16,0},{1,17},{17,1},{2,18},{18,2},{3,19},{19,3},{4,20},{20... | collective-permute-start | bytes 196616 | tf_op jit(solution)/shard_map/ppermute | solution.py:662
  36.6 1.0 copy-start.2
  49.9 0.7 copy-start.3
  50.6 0.7 copy-start.13
  63.2 1.0 copy-start.14
  64.2 4.6 %copy-start.5 = (f32[16,16,256]{2,1,0:T(8,128)S(1)}, f32[16,16,256]{2,1,0:T(8,128)}, u32[]{:S(2)}) copy-start(f32[16,16,256]{2,1,0:T(8,128)} %copy-done.4) | copy-start | bytes 786436
  65.5 7.0 %collective-permute-start.6 = (f32[3,16,256]{2,1,0:T(8,128)S(1)}, f32[3,16,256]{2,1,0:T(8,128)S(1)}, u32[]{:S(2)}, u32[]{:S(2)}) collective-permute-start(f32[3,16,256]{2,1,0:T(8,128)S(1)} %get-tuple-element.80), channel_id=1, source_target_pairs={{4,0},{8,4},{12,8},{0,12},{5,1},{9,5},{13,9},{1,13},{6,2},{10,6},{... | collective-permute-start | bytes 147464 | tf_op jit(solution)/shard_map/ppermute | solution.py:616
  66.4 6.0 %collective-permute-start.7 = (f32[3,16,256]{2,1,0:T(8,128)S(1)}, f32[3,16,256]{2,1,0:T(8,128)S(1)}, u32[]{:S(2)}, u32[]{:S(2)}) collective-permute-start(f32[3,16,256]{2,1,0:T(8,128)S(1)} %get-tuple-element.81), channel_id=1, source_target_pairs={{0,4},{4,8},{8,12},{12,0},{1,5},{5,9},{9,13},{13,1},{2,6},{6,10},{... | collective-permute-start | bytes 147464 | tf_op jit(solution)/shard_map/ppermute | solution.py:617
  67.3 5.2 %collective-permute-start.8 = (f32[3,16,256]{2,1,0:T(8,128)S(1)}, f32[3,16,256]{2,1,0:T(8,128)S(1)}, u32[]{:S(2)}, u32[]{:S(2)}) collective-permute-start(f32[3,16,256]{2,1,0:T(8,128)S(1)} %get-tuple-element.82), channel_id=1, source_target_pairs={{16,0},{1,16},{17,1},{2,17},{18,2},{3,18},{19,3},{0,19},{20,4},{5,... | collective-permute-start | bytes 147464 | tf_op jit(solution)/shard_map/ppermute | solution.py:644
  68.0 5.6 %collective-permute-start.9 = (f32[3,16,256]{2,1,0:T(8,128)S(1)}, f32[3,16,256]{2,1,0:T(8,128)S(1)}, u32[]{:S(2)}, u32[]{:S(2)}) collective-permute-start(f32[3,16,256]{2,1,0:T(8,128)S(1)} %get-tuple-element.83), channel_id=1, source_target_pairs={{0,16},{16,1},{1,17},{17,2},{2,18},{18,3},{3,19},{19,0},{4,20},{20... | collective-permute-start | bytes 147464 | tf_op jit(solution)/shard_map/ppermute | solution.py:645
  71.8 0.7 copy-start.7
  72.5 3.6 %copy-start.9 = (f32[16,16,256]{2,1,0:T(8,128)}, f32[16,16,256]{2,1,0:T(8,128)S(1)}, u32[]{:S(2)}) copy-start(f32[16,16,256]{2,1,0:T(8,128)S(1)} %get-tuple-element.76.b_ref) | copy-start | bytes 786436
  72.5 3.6 %copy-start.11 = (f32[16,16,256]{2,1,0:T(8,128)}, f32[16,16,256]{2,1,0:T(8,128)S(1)}, u32[]{:S(2)}) copy-start(f32[16,16,256]{2,1,0:T(8,128)S(1)} %get-tuple-element.77.g_ref) | copy-start | bytes 786436
  76.1 3.8 %copy-start.8 = (f32[16,16,256]{2,1,0:T(8,128)S(1)}, f32[16,16,256]{2,1,0:T(8,128)}, u32[]{:S(2)}) copy-start(f32[16,16,256]{2,1,0:T(8,128)} %copy-done.7) | copy-start | bytes 786436
  76.1 30.3 %all-to-all-start.1 = ((f32[32,2,16,256]{3,2,1,0:T(8,128)}), f32[32,2,16,256]{3,2,1,0:T(8,128)S(1)}, u32[]{:S(2)}, u32[]{:S(2)}) async-start(f32[32,2,16,256]{3,2,1,0:T(8,128)} %bitcast.18), calls=%async_computation.1 | async-start | bytes 2097152 | tf_op jit(solution)/shard_map/all_to_all | solution.py:887
  79.9 1.0 copy-start.10
  80.9 0.9 copy-start.12
  84.6 20.0 %collective-permute-start.10 = (f32[16,2,16,256]{3,2,1,0:T(8,128)S(1)}, f32[16,2,16,256]{3,2,1,0:T(8,128)S(1)}, u32[]{:S(2)}, u32[]{:S(2)}) collective-permute-start(f32[16,2,16,256]{3,2,1,0:T(8,128)S(1)} %third.1.absorbed_ref), channel_id=1, source_target_pairs={{0,16},{16,0},{1,17},{17,1},{2,18},{18,2},{3,19},{19,3},{4,20},{20... | collective-permute-start | bytes 1572872 | tf_op jit(solution)/shard_map/ppermute | solution.py:662
  (2 other events, 1.4 us)

commit v7 on v6

--- a/solution.py
+++ b/solution.py
@@ -842,8 +842,8 @@
     projected, g = project(side_index, tracers, weights)
     low, high, left, right, first_column = edges
     north, south = exchange_rows(low, high)
+    left, right, first_column, projected, g = lax.optimization_barrier((left, right, first_column, projected, g))
     edge = east_column(first_column)
-    left, right, projected, g = lax.optimization_barrier((left, right, projected, g))
     projected, g = in_vmem(projected), in_vmem(g)
     outer = shape_of(4, 2, CY + 2, levels)
     [sides] = call(corner_kernel, side_index, (left, right, north, south), [None] * 4, (outer,), (), "corner")

time: 109 us -> 109 us (level)
  no operation moved by 1% of the time
where the time goes in v7:
time: 109 us; the launch traced here: 108 us
  waiting for transfers between devices  39.6 us (36%)
  Pallas kernels  34.6 us (32%)
  starting transfers between devices  22.4 us (21%)
  local copies, waits for them, and re-layouts  9.45 us (9%)
  matrix products  1.19 us (1%)
    ppermute x3, waiting for transfers between devices, swap(): return lax.ppermute(block, 'comp', [(0, 1), (1, 0)])  22 us
    all_to_all x1, waiting for transfers between devices, to_owners(): lax.all_to_all(blocks, ('py', 'px'), split_axis=0, concat_axis=0, tiled=T...  11.9 us
    pallas_call x7, Pallas kernels, call(): pl.pallas_call(kernel, grid_spec=pltpu.PrefetchScalarGridSpec(num_scalar_...  11.8 us
    pallas_call x2, Pallas kernels, ocean(): pl.pallas_call(functools.partial(ocean_kernel, advance), grid_spec=pltpu....  10.8 us
    unnamed x46, local copies, waits for them, and re-layouts  7.77 us
    ppermute x1, starting transfers between devices, east_column(): lax.ppermute(block, ('comp', 'px'), [((i + 1) % count, count + i) for i i...  5.22 us
    pallas_call x1, Pallas kernels, project(): pl.pallas_call(project_kernel, grid_spec=pltpu.PrefetchScalarGridSpec(num...  4.95 us
    all_to_all x1, starting transfers between devices, to_owners(): lax.all_to_all(blocks, ('py', 'px'), split_axis=0, concat_axis=0, tiled=T...  4.67 us
  transfers between devices with their start and end apart: 13, of which 6 were waited for; matrix products, arithmetic and copies ran while one was open for 3% of the time, Pallas kernels for 25%

profile of v7, /device:TPU:1, one launch (start us, length us, event | category | flops | bytes accessed | tf_op | source)
XLA Modules:
  0.0 108.0 jit_solution(1101620882660592503)
XLA Ops:
  0.0 2.7 %pack.1 = (f32[2,16,16,256]{3,2,1,0:T(8,128)}, f32[4,2,32,256]{3,2,1,0:T(8,128)}, f32[4,2,32,256]{3,2,1,0:T(8,128)}, f32[4,2,16,256]{3,2,1,0:T(8,128)}, f32[4,2,16,256]{3,2,1,0:T(8,128)}, /*index=5*/f32[16,256]{1,0:T(8,128)}) custom-call(s32[1]{0:T(128)} %bitcast.sc, f32[2,16,32,256]{3,2,1,0:T(8,128)} %bitcast.53, f32[2,16,32,256]{3,2,1,0:T(8,128)} %refs_0_.1, ...), custom_call_target="tpu_custom_call" | custom-call | tf_op jit(solution)/shard_map/pack/pallas_call | solution.py:276
  2.8 2.6 %collective-permute-start.2 = (f32[4,2,32,256]{3,2,1,0:T(8,128)}, f32[4,2,32,256]{3,2,1,0:T(8,128)S(1)}, u32[]{:S(2)}, u32[]{:S(2)}) collective-permute-start(f32[4,2,32,256]{3,2,1,0:T(8,128)} %get-tuple-element.57), channel_id=1, source_target_pairs={{0,4},{4,8},{8,12},{12,0},{1,5},{5,9},{9,13},{13,1},{2,6},{6,10},{... | collective-permute-start | bytes 786440 | tf_op jit(solution)/shard_map/ppermute | solution.py:617
  5.4 1.2 %collective-permute-start = (f32[2,16,16,256]{3,2,1,0:T(8,128)}, f32[2,16,16,256]{3,2,1,0:T(8,128)S(1)}, u32[]{:S(2)}, u32[]{:S(2)}) collective-permute-start(f32[2,16,16,256]{3,2,1,0:T(8,128)} %get-tuple-element.53), channel_id=1, source_target_pairs={{0,16},{16,0},{1,17},{17,1},{2,18},{18,2},{3,19},{19,3},{4,20},{20... | collective-permute-start | bytes 1572872 | tf_op jit(solution)/shard_map/ppermute | solution.py:662
  7.1 5.0 %project.1 = (f32[7,16,16,256]{3,2,1,0:T(8,128)S(1)}, f32[16,16,256]{2,1,0:T(8,128)S(1)}) custom-call(s32[1]{0:T(128)} %bitcast.sc, f32[16,16,32,256]{3,2,1,0:T(8,128)} %bitcast.56, f32[7,16]{1,0:T(8,128)S(1)} %stack.30.w_ref), custom_call_target="tpu_custom_call" | custom-call | tf_op jit(solution)/shard_map/project/pallas_call | solution.py:140
  12.0 5.2 %collective-permute-start.4 = (f32[16,256]{1,0:T(8,128)}, f32[16,256]{1,0:T(8,128)S(1)}, u32[]{:S(2)}, u32[]{:S(2)}) collective-permute-start(f32[16,256]{1,0:T(8,128)} %get-tuple-element.61), channel_id=1, source_target_pairs={{1,16},{2,17},{3,18},{0,19},{5,20},{6,21},{7,22},{4,23},{9,24},{10... | collective-permute-start | bytes 49160 | tf_op jit(solution)/shard_map/ppermute | solution.py:637
  17.5 0.7 corner.1
  18.6 0.8 convolution_bitcast_fusion.share_ref
  19.6 4.3 %first_tracer.1 = f32[16,5,16,256]{3,2,1,0:T(8,128)} custom-call(s32[1]{0:T(128)} %bitcast.sc, f32[7,16,16,256]{3,2,1,0:T(8,128)S(1)} %get-tuple-element.51.y_ref, f32[16,16,256]{2,1,0:T(8,128)S(1)} %get-tuple-element.52.g_ref, f32[2,16,16,256]{3,2,1,0:T(8,128)S(1)} %collective-permute-done.got_ref.refs_3_, f32[2,16,32,256]{3,2,1,0:T(8,128)} %bitcast.54, ...), custom_call_target="tpu_custom_call" | custom-call | tf_op jit(solution)/shard_map/first_tracer/pallas_call | solution.py:187
  23.9 2.7 %collective-permute-done.3.refs_6_ = f32[4,2,18,256]{3,2,1,0:T(8,128)} collective-permute-done((f32[4,2,18,256]{3,2,1,0:T(8,128)}, f32[4,2,18,256]{3,2,1,0:T(8,128)}, u32[]{:S(2)}, u32[]{:S(2)}) %collective-permute-start.3) | collective-permute-done | bytes 147488 | tf_op jit(solution)/shard_map/ppermute | solution.py:632
  26.7 4.7 %all-to-all-start = ((f32[16,5,16,256]{3,2,1,0:T(8,128)}), f32[16,5,16,256]{3,2,1,0:T(8,128)S(1)}, u32[]{:S(2)}, u32[]{:S(2)}) async-start(f32[16,5,16,256]{3,2,1,0:T(8,128)} %first_tracer.1), calls=%async_computation | async-start | bytes 2621440 | tf_op jit(solution)/shard_map/all_to_all | solution.py:658
  33.2 3.4 %collective-permute-done.5.refs_8_ = f32[2,32,256]{2,1,0:T(8,128)S(1)} collective-permute-done((f32[2,32,256]{2,1,0:T(8,128)S(1)}, f32[2,32,256]{2,1,0:T(8,128)S(1)}, u32[]{:S(2)}, u32[]{:S(2)}) %collective-permute-start.5) | collective-permute-done | bytes 65568 | tf_op jit(solution)/shard_map/ppermute | solution.py:662
  36.6 1.0 copy-done.2
  37.6 6.8 %ocean1.1 = (f32[2,18,24,256]{3,2,1,0:T(8,128)S(1)}, f32[18,24,256]{2,1,0:T(8,128)S(1)}, f32[16,16,256]{2,1,0:T(8,128)S(1)}, f32[16,16,256]{2,1,0:T(8,128)S(1)}) custom-call(s32[17]{0:T(128)S(1)} %pad_add_fusion.1.sc, f32[18]{0:T(128)S(1)} %multiply_add_fusion.coriolis_ref, f32[2,16,32,256]{3,2,1,0:T(8,128)} %refs_0_.1, f32[16,32,256]{2,1,0:T(8,128)} %refs_1_.1, ...), custom_call_target="tpu_custom_call" | custom-call | tf_op jit(solution)/shard_map/ocean1/pallas_call | solution.py:447
  45.9 4.0 %ocean2.1 = (f32[2,16,16,256]{3,2,1,0:T(8,128)S(1)}, f32[16,16,256]{2,1,0:T(8,128)S(1)}, f32[16,16,256]{2,1,0:T(8,128)S(1)}) custom-call(s32[17]{0:T(128)S(1)} %pad_add_fusion.1.sc, f32[18]{0:T(128)S(1)} %multiply_add_fusion.coriolis_ref, f32[2,18,24,256]{3,2,1,0:T(8,128)S(1)} %get-tuple-element.67.refs_0_, f32[18,24,256]{2,1,0:T(8,128)S(1)} %get-tuple-element.68.refs_1_, ...), custom_call_target="tpu_custom_call" | custom-call | tf_op jit(solution)/shard_map/ocean2/pallas_call | solution.py:447
  51.3 11.9 %all-to-all-done.y_hbm.y_ref = f32[16,5,16,256]{3,2,1,0:T(8,128)S(1)} async-done(((f32[16,5,16,256]{3,2,1,0:T(8,128)}), f32[16,5,16,256]{3,2,1,0:T(8,128)S(1)}, u32[]{:S(2)}, u32[]{:S(2)}) %all-to-all-start) | async-done | bytes 1310752 | tf_op jit(solution)/shard_map/all_to_all | solution.py:658
  63.2 0.9 copy-done.14
  64.1 1.3 %absorb.1 = (f32[16,16,256]{2,1,0:T(8,128)S(1)}, f32[16,16,256]{2,1,0:T(8,128)S(1)}, f32[3,16,256]{2,1,0:T(8,128)S(1)}, f32[3,16,256]{2,1,0:T(8,128)S(1)}, f32[3...) custom-call(s32[17]{0:T(128)S(1)} %pad_add_fusion.1.sc, f32[16,5,16,256]{3,2,1,0:T(8,128)S(1)} %all-to-all-done.y_hbm.y_ref, ...), custom_call_target="tpu_custom_call" | custom-call | tf_op jit(solution)/shard_map/absorb/pallas_call | solution.py:599
  65.5 0.9 collective-permute-start.6
  66.4 0.9 collective-permute-start.7
  67.3 0.7 collective-permute-start.8
  68.0 0.8 collective-permute-start.9
  68.8 3.0 %second.1 = (f32[16,16,256]{2,1,0:T(8,128)S(1)}, f32[16,16,256]{2,1,0:T(8,128)S(1)}, f32[16,16,256]{2,1,0:T(8,128)S(1)}, f32[16,16,256]{2,1,0:T(8,128)S(1)}) custom-call(s32[17]{0:T(128)S(1)} %pad_add_fusion.1.sc, f32[16,5,16,256]{3,2,1,0:T(8,128)S(1)} %all-to-all-done.y_hbm.y_ref, f32[16,16,256]{2,1,0:T(8,128)S(1)} %get-tuple-element.74.irr_ref, ...), custom_call_target="tpu_custom_call" | custom-call | tf_op jit(solution)/shard_map/second/pallas_call | solution.py:599
  72.5 1.2 %collective-permute-done.9.west_ref = f32[3,16,256]{2,1,0:T(8,128)S(1)} collective-permute-done((f32[3,16,256]{2,1,0:T(8,128)S(1)}, f32[3,16,256]{2,1,0:T(8,128)S(1)}, u32[]{:S(2)}, u32[]{:S(2)}) %collective-permute-start.9) | collective-permute-done | bytes 49184 | tf_op jit(solution)/shard_map/ppermute | solution.py:645
  73.6 2.4 %last_ocean.1 = f32[2,16,2,16,256]{4,3,2,1,0:T(8,128)} custom-call(s32[17]{0:T(128)S(1)} %pad_add_fusion.1.sc, f32[2,16,16,256]{3,2,1,0:T(8,128)S(1)} %get-tuple-element.73.speed_ref, f32[16,16,256]{2,1,0:T(8,128)S(1)} %get-tuple-element.80.t2_ref.t_ref, f32[3,16,256]{2,1,0:T(8,128)S(1)} %collective-permute-done.6.north_ref, ...), custom_call_target="tpu_custom_call" | custom-call | tf_op jit(solution)/shard_map/last_ocean/pallas_call | solution.py:599
  76.1 3.8 %all-to-all-start.1 = ((f32[32,2,16,256]{3,2,1,0:T(8,128)}), f32[32,2,16,256]{3,2,1,0:T(8,128)S(1)}, u32[]{:S(2)}, u32[]{:S(2)}) async-start(f32[32,2,16,256]{3,2,1,0:T(8,128)} %bitcast.18), calls=%async_computation.1 | async-start | bytes 2097152 | tf_op jit(solution)/shard_map/all_to_all | solution.py:887
  79.9 0.9 copy-done.10
  80.9 0.9 copy-done.12
  81.8 2.7 %third.1.absorbed_ref = f32[16,2,16,256]{3,2,1,0:T(8,128)S(1)} custom-call(s32[17]{0:T(128)S(1)} %pad_add_fusion.1.sc, f32[16,16,256]{2,1,0:T(8,128)S(1)} %copy-done.8, f32[16,16,256]{2,1,0:T(8,128)S(1)} %copy-done.10, f32[16,16,256]{2,1,0:T(8,128)S(1)} %copy-done.12, f32[16,16,256]{2,1,0:T(8,128)S(1)} %get-tuple-element.80.t2_ref.t_ref, ...), custom_call_target="tpu_custom_call" | custom-call | tf_op jit(solution)/shard_map/third/pallas_call | solution.py:599
  84.6 1.5 %collective-permute-start.10 = (f32[16,2,16,256]{3,2,1,0:T(8,128)S(1)}, f32[16,2,16,256]{3,2,1,0:T(8,128)S(1)}, u32[]{:S(2)}, u32[]{:S(2)}) collective-permute-start(f32[16,2,16,256]{3,2,1,0:T(8,128)S(1)} %third.1.absorbed_ref), channel_id=1, source_target_pairs={{0,16},{16,0},{1,17},{17,1},{2,18},{18,2},{3,19},{19,3},{4,20},{20... | collective-permute-start | bytes 1572872 | tf_op jit(solution)/shard_map/ppermute | solution.py:662
  86.0 18.6 %collective-permute-done.10.other_ref = f32[16,2,16,256]{3,2,1,0:T(8,128)S(1)} collective-permute-done((f32[16,2,16,256]{3,2,1,0:T(8,128)S(1)}, f32[16,2,16,256]{3,2,1,0:T(8,128)S(1)}, u32[]{:S(2)}, u32[]{:S(2)}) %collective-permute-start.10) | collective-permute-done | bytes 524320 | tf_op jit(solution)/shard_map/ppermute | solution.py:662
  104.6 1.8 %all-to-all-done.1 = f32[32,2,16,256]{3,2,1,0:T(8,128)S(1)} async-done(((f32[32,2,16,256]{3,2,1,0:T(8,128)}), f32[32,2,16,256]{3,2,1,0:T(8,128)S(1)}, u32[]{:S(2)}, u32[]{:S(2)}) %all-to-all-start.1) | async-done | bytes 1048608 | tf_op jit(solution)/shard_map/all_to_all | solution.py:887
  106.4 1.6 %join.1 = f32[2,16,32,256]{3,2,1,0:T(8,128)} custom-call(s32[17]{0:T(128)S(1)} %pad_add_fusion.1.sc, f32[16,2,16,256]{3,2,1,0:T(8,128)S(1)} %third.1.absorbed_ref, f32[2,16,2,16,256]{4,3,2,1,0:T(8,128)S(1)} %bitcast.52, f32[16,2,16,256]{3,2,1,0:T(8,128)S(1)} %collective-permute-done.10.other_ref), custom_call_target="tpu_custom_call" | custom-call | tf_op jit(solution)/shard_map/join/pallas_call | solution.py:599
  (79 shorter events, 6.6 us)
Async XLA Ops:
  0.0 6.6 %copy-start = (f32[16,16]{1,0:T(8,128)S(1)}, f32[16,16]{1,0:T(8,128)}, u32[]{:S(2)}) copy-start(f32[16,16]{1,0:T(8,128)} %param.17) | copy-start | bytes 3076
  0.0 6.6 %copy-start.20 = (f32[16]{0:T(128)S(1)}, f32[16]{0:T(128)}, u32[]{:S(2)}) copy-start(f32[16]{0:T(128)} %param.19) | copy-start | bytes 196
  2.7 14.8 %collective-permute-start.1 = (f32[4,2,32,256]{3,2,1,0:T(8,128)}, f32[4,2,32,256]{3,2,1,0:T(8,128)S(1)}, u32[]{:S(2)}, u32[]{:S(2)}) collective-permute-start(f32[4,2,32,256]{3,2,1,0:T(8,128)} %get-tuple-element.56), channel_id=1, source_target_pairs={{4,0},{8,4},{12,8},{0,12},{5,1},{9,5},{13,9},{1,13},{6,2},{10,6},{... | collective-permute-start | bytes 786440 | tf_op jit(solution)/shard_map/ppermute | solution.py:616
  2.8 14.7 %collective-permute-start.2 = (f32[4,2,32,256]{3,2,1,0:T(8,128)}, f32[4,2,32,256]{3,2,1,0:T(8,128)S(1)}, u32[]{:S(2)}, u32[]{:S(2)}) collective-permute-start(f32[4,2,32,256]{3,2,1,0:T(8,128)} %get-tuple-element.57), channel_id=1, source_target_pairs={{0,4},{4,8},{8,12},{12,0},{1,5},{5,9},{9,13},{13,1},{2,6},{6,10},{... | collective-permute-start | bytes 786440 | tf_op jit(solution)/shard_map/ppermute | solution.py:617
  5.4 14.2 %collective-permute-start = (f32[2,16,16,256]{3,2,1,0:T(8,128)}, f32[2,16,16,256]{3,2,1,0:T(8,128)S(1)}, u32[]{:S(2)}, u32[]{:S(2)}) collective-permute-start(f32[2,16,16,256]{3,2,1,0:T(8,128)} %get-tuple-element.53), channel_id=1, source_target_pairs={{0,16},{16,0},{1,17},{17,1},{2,18},{18,2},{3,19},{19,3},{4,20},{20... | collective-permute-start | bytes 1572872 | tf_op jit(solution)/shard_map/ppermute | solution.py:662
  7.0 10.3 %copy-start.19 = (s32[16,16]{1,0:T(8,128)S(1)}, s32[16,16]{1,0:T(8,128)}, u32[]{:S(2)}) copy-start(s32[16,16]{1,0:T(8,128)} %param.16) | copy-start | bytes 3076
  7.0 10.4 %copy-start.17 = (s32[64,128]{1,0:T(8,128)S(1)}, s32[64,128]{1,0:T(8,128)}, u32[]{:S(2)}) copy-start(s32[64,128]{1,0:T(8,128)} %param.14) | copy-start | bytes 98308
  7.1 10.4 %copy-start.18 = (s32[64,128]{1,0:T(8,128)S(1)}, s32[64,128]{1,0:T(8,128)}, u32[]{:S(2)}) copy-start(s32[64,128]{1,0:T(8,128)} %param.15) | copy-start | bytes 98308
  7.1 10.4 %copy-start.15 = (f32[4,2,16,256]{3,2,1,0:T(8,128)S(1)}, f32[4,2,16,256]{3,2,1,0:T(8,128)}, u32[]{:S(2)}) copy-start(f32[4,2,16,256]{3,2,1,0:T(8,128)} %get-tuple-element.54.left_ref) | copy-start | bytes 393220
  7.1 10.4 %copy-start.16 = (f32[4,2,16,256]{3,2,1,0:T(8,128)S(1)}, f32[4,2,16,256]{3,2,1,0:T(8,128)}, u32[]{:S(2)}) copy-start(f32[4,2,16,256]{3,2,1,0:T(8,128)} %get-tuple-element.55.right_ref) | copy-start | bytes 393220
  12.0 11.9 %collective-permute-start.4 = (f32[16,256]{1,0:T(8,128)}, f32[16,256]{1,0:T(8,128)S(1)}, u32[]{:S(2)}, u32[]{:S(2)}) collective-permute-start(f32[16,256]{1,0:T(8,128)} %get-tuple-element.61), channel_id=1, source_target_pairs={{1,16},{2,17},{3,18},{0,19},{5,20},{6,21},{7,22},{4,23},{9,24},{10... | collective-permute-start | bytes 49160 | tf_op jit(solution)/shard_map/ppermute | solution.py:637
  18.3 8.3 %collective-permute-start.3 = (f32[4,2,18,256]{3,2,1,0:T(8,128)}, f32[4,2,18,256]{3,2,1,0:T(8,128)}, u32[]{:S(2)}, u32[]{:S(2)}) collective-permute-start(f32[4,2,18,256]{3,2,1,0:T(8,128)} %corner.1), channel_id=1, source_target_pairs={{0,1},{1,2},{2,3},{3,0},{17,16},{18,17},{19,18},{16,19},{4,5},{5,6... | collective-permute-start | bytes 442376 | tf_op jit(solution)/shard_map/ppermute | solution.py:632
  19.6 4.3 %copy-start.1 = (f32[2,16,16,256]{3,2,1,0:T(8,128)}, f32[2,16,16,256]{3,2,1,0:T(8,128)S(1)}, u32[]{:S(2)}) copy-start(f32[2,16,16,256]{3,2,1,0:T(8,128)S(1)} %collective-permute-done.got_ref.refs_3_) | copy-start | bytes 1572868
  26.7 36.5 %all-to-all-start = ((f32[16,5,16,256]{3,2,1,0:T(8,128)}), f32[16,5,16,256]{3,2,1,0:T(8,128)S(1)}, u32[]{:S(2)}, u32[]{:S(2)}) async-start(f32[16,5,16,256]{3,2,1,0:T(8,128)} %first_tracer.1), calls=%async_computation | async-start | bytes 2621440 | tf_op jit(solution)/shard_map/all_to_all | solution.py:658
  33.1 3.5 %collective-permute-start.5 = (f32[2,32,256]{2,1,0:T(8,128)S(1)}, f32[2,32,256]{2,1,0:T(8,128)S(1)}, u32[]{:S(2)}, u32[]{:S(2)}) collective-permute-start(f32[2,32,256]{2,1,0:T(8,128)S(1)} %ring.1), channel_id=1, source_target_pairs={{0,16},{16,0},{1,17},{17,1},{2,18},{18,2},{3,19},{19,3},{4,20},{20... | collective-permute-start | bytes 196616 | tf_op jit(solution)/shard_map/ppermute | solution.py:662
  36.6 1.0 copy-start.2
  49.9 0.7 copy-start.3
  50.6 0.7 copy-start.13
  63.2 1.0 copy-start.14
  64.1 4.6 %copy-start.5 = (f32[16,16,256]{2,1,0:T(8,128)S(1)}, f32[16,16,256]{2,1,0:T(8,128)}, u32[]{:S(2)}) copy-start(f32[16,16,256]{2,1,0:T(8,128)} %copy-done.4) | copy-start | bytes 786436
  65.5 7.0 %collective-permute-start.6 = (f32[3,16,256]{2,1,0:T(8,128)S(1)}, f32[3,16,256]{2,1,0:T(8,128)S(1)}, u32[]{:S(2)}, u32[]{:S(2)}) collective-permute-start(f32[3,16,256]{2,1,0:T(8,128)S(1)} %get-tuple-element.82), channel_id=1, source_target_pairs={{4,0},{8,4},{12,8},{0,12},{5,1},{9,5},{13,9},{1,13},{6,2},{10,6},{... | collective-permute-start | bytes 147464 | tf_op jit(solution)/shard_map/ppermute | solution.py:616
  66.4 6.0 %collective-permute-start.7 = (f32[3,16,256]{2,1,0:T(8,128)S(1)}, f32[3,16,256]{2,1,0:T(8,128)S(1)}, u32[]{:S(2)}, u32[]{:S(2)}) collective-permute-start(f32[3,16,256]{2,1,0:T(8,128)S(1)} %get-tuple-element.83), channel_id=1, source_target_pairs={{0,4},{4,8},{8,12},{12,0},{1,5},{5,9},{9,13},{13,1},{2,6},{6,10},{... | collective-permute-start | bytes 147464 | tf_op jit(solution)/shard_map/ppermute | solution.py:617
  67.3 5.2 %collective-permute-start.8 = (f32[3,16,256]{2,1,0:T(8,128)S(1)}, f32[3,16,256]{2,1,0:T(8,128)S(1)}, u32[]{:S(2)}, u32[]{:S(2)}) collective-permute-start(f32[3,16,256]{2,1,0:T(8,128)S(1)} %get-tuple-element.84), channel_id=1, source_target_pairs={{16,0},{1,16},{17,1},{2,17},{18,2},{3,18},{19,3},{0,19},{20,4},{5,... | collective-permute-start | bytes 147464 | tf_op jit(solution)/shard_map/ppermute | solution.py:644
  68.0 5.6 %collective-permute-start.9 = (f32[3,16,256]{2,1,0:T(8,128)S(1)}, f32[3,16,256]{2,1,0:T(8,128)S(1)}, u32[]{:S(2)}, u32[]{:S(2)}) collective-permute-start(f32[3,16,256]{2,1,0:T(8,128)S(1)} %get-tuple-element.85), channel_id=1, source_target_pairs={{0,16},{16,1},{1,17},{17,2},{2,18},{18,3},{3,19},{19,0},{4,20},{20... | collective-permute-start | bytes 147464 | tf_op jit(solution)/shard_map/ppermute | solution.py:645
  71.7 0.7 copy-start.7
  72.5 3.6 %copy-start.9 = (f32[16,16,256]{2,1,0:T(8,128)}, f32[16,16,256]{2,1,0:T(8,128)S(1)}, u32[]{:S(2)}) copy-start(f32[16,16,256]{2,1,0:T(8,128)S(1)} %get-tuple-element.78.b_ref) | copy-start | bytes 786436
  72.5 3.6 %copy-start.11 = (f32[16,16,256]{2,1,0:T(8,128)}, f32[16,16,256]{2,1,0:T(8,128)S(1)}, u32[]{:S(2)}) copy-start(f32[16,16,256]{2,1,0:T(8,128)S(1)} %get-tuple-element.79.g_ref) | copy-start | bytes 786436
  76.1 3.8 %copy-start.8 = (f32[16,16,256]{2,1,0:T(8,128)S(1)}, f32[16,16,256]{2,1,0:T(8,128)}, u32[]{:S(2)}) copy-start(f32[16,16,256]{2,1,0:T(8,128)} %copy-done.7) | copy-start | bytes 786436
  76.1 30.3 %all-to-all-start.1 = ((f32[32,2,16,256]{3,2,1,0:T(8,128)}), f32[32,2,16,256]{3,2,1,0:T(8,128)S(1)}, u32[]{:S(2)}, u32[]{:S(2)}) async-start(f32[32,2,16,256]{3,2,1,0:T(8,128)} %bitcast.18), calls=%async_computation.1 | async-start | bytes 2097152 | tf_op jit(solution)/shard_map/all_to_all | solution.py:887
  79.9 1.0 copy-start.10
  80.9 0.9 copy-start.12
  84.6 20.0 %collective-permute-start.10 = (f32[16,2,16,256]{3,2,1,0:T(8,128)S(1)}, f32[16,2,16,256]{3,2,1,0:T(8,128)S(1)}, u32[]{:S(2)}, u32[]{:S(2)}) collective-permute-start(f32[16,2,16,256]{3,2,1,0:T(8,128)S(1)} %third.1.absorbed_ref), channel_id=1, source_target_pairs={{0,16},{16,0},{1,17},{17,1},{2,18},{18,2},{3,19},{19,3},{4,20},{20... | collective-permute-start | bytes 1572872 | tf_op jit(solution)/shard_map/ppermute | solution.py:662
  (2 other events, 1.4 us)
